TPU v7x, 32 devices: a whole 2x2x4 slice. The times are simulated.
32 devices in a mesh: group: 8 (over y, x, core), tensor: 4 (over z).
Axes of the slice: x: 2, y: 2, z: 4, core: 2. Of those that a mesh axis runs over, the one named last changes fastest.
Arguments:
- queries: bfloat16 [3072, 4096], P('group', 'tensor')
- text_kv: bfloat16 [3072, 2048], P('group', 'tensor')
- out_grad: bfloat16 [3072, 4096], P('group', 'tensor'), may hold values from -6 to 6
- text_segment: int32 [8, 384], P('group'), may hold values from 0 to 7, never falling along the last dimension, each value on 1 to 96 neighbouring positions
- visual_rows: bfloat16 [1024, 8192], P('group', 'tensor'), may hold values from -6 to 6
- kv_weight: bfloat16 [8192, 2048], P('tensor'), may hold values from -0.0625 to 0.0625
- visual_dest: int32 [1024, 1], P('group'), may hold values from 0 to 7, as said below
- visual_sample: int32 [1024], P('group'), may hold values from 0 to 7, as said below
Outputs:
- attended: bfloat16 [3072, 4096], P('group', 'tensor')
- query_grad: bfloat16 [3072, 4096], P('group', 'tensor')
- text_kv_grad: bfloat16 [3072, 2048], P('group', 'tensor')
- visual_grad: bfloat16 [1024, 8192], P('group', 'tensor')
Inputs may be any that keep to these rules, and one draw needn't show every extreme that they name: `visual_dest`: a group's rows come in aligned runs of 32 rows, each run to one pack, the runs of one group to distinct packs, so exactly 32 rows of a group reach each pack that it names and none reach the others. `visual_sample`: one sample for all rows of a run. `text_segment`: never falling along a pack, each sample at most 96 tokens.
All inputs are finite; a program needn't handle non-finite values.
Results may differ from a plain program's by a relative error of at most 0.015.
Values may be sent and summed in bfloat16 or wider, within the bound.
No kernel may reach another device: no remote copies, remote signals or barrier semaphores. Data moves between devices by JAX's collectives and lax.ppermute only.
A program may use at most 64 MiB of HBM per device.

v0:
```python
import math

import jax
import jax.numpy as jnp
from jax import lax
from jax.sharding import PartitionSpec as P

HD = 128
QPK = 4


def attend_local(queries, text_kv, out_grad, segment, vis_kv, vis_sample):
    length = queries.shape[0]
    local_heads = text_kv.shape[1] // (2 * HD)
    scale = 1.0 / math.sqrt(HD)
    query_heads = queries.reshape(length, local_heads, QPK, HD)
    grad_heads = out_grad.reshape(length, local_heads, QPK, HD)
    text_heads = text_kv.reshape(length, local_heads, 2, HD)
    vis_heads = vis_kv.reshape(vis_kv.shape[0], local_heads, 2, HD)
    keys = jnp.concatenate([text_heads[:, :, 0], vis_heads[:, :, 0]], axis=0)
    values = jnp.concatenate([text_heads[:, :, 1], vis_heads[:, :, 1]], axis=0)
    places = jnp.arange(length, dtype=jnp.int32)
    text_mask = (segment[:, None] == segment[None, :]) & (places[None, :] <= places[:, None])
    vis_mask = vis_sample[None, :] == segment[:, None]
    mask = jnp.concatenate([text_mask, vis_mask], axis=1)
    key_grad = jnp.zeros((keys.shape[0], local_heads, HD), jnp.float32)
    value_grad = jnp.zeros((keys.shape[0], local_heads, HD), jnp.float32)
    outputs = []
    query_grads = []
    for head in range(QPK):
        query_one = query_heads[:, :, head]
        grad_one = grad_heads[:, :, head]
        scores = (
            jnp.einsum("pgd,kgd->gpk", query_one, keys, preferred_element_type=jnp.float32) * scale
        )
        top = jnp.max(jnp.where(mask, scores, -jnp.inf), axis=-1, keepdims=True)
        expo = jnp.where(mask, jnp.exp(scores - top), 0.0)
        probs = expo / jnp.sum(expo, axis=-1, keepdims=True)
        weights = probs.astype(jnp.bfloat16)
        outputs.append(
            jnp.einsum("gpk,kgd->pgd", weights, values, preferred_element_type=jnp.float32).astype(
                jnp.bfloat16
            )
        )
        dprobs = jnp.einsum("pgd,kgd->gpk", grad_one, values, preferred_element_type=jnp.float32)
        inner = jnp.sum(probs * dprobs, axis=-1, keepdims=True)
        dscores = (probs * (dprobs - inner) * scale).astype(jnp.bfloat16)
        query_grads.append(
            jnp.einsum("gpk,kgd->pgd", dscores, keys, preferred_element_type=jnp.float32).astype(
                jnp.bfloat16
            )
        )
        key_grad = key_grad + jnp.einsum(
            "gpk,pgd->kgd", dscores, query_one, preferred_element_type=jnp.float32
        )
        value_grad = value_grad + jnp.einsum(
            "gpk,pgd->kgd", weights, grad_one, preferred_element_type=jnp.float32
        )
    attended = jnp.stack(outputs, axis=2).reshape(length, -1)
    query_grad = jnp.stack(query_grads, axis=2).reshape(length, -1)
    kv_grad = jnp.stack([key_grad.astype(jnp.bfloat16), value_grad.astype(jnp.bfloat16)], axis=2)
    text_grad = kv_grad[:length].reshape(length, -1)
    vis_grad = kv_grad[length:].reshape(vis_kv.shape[0], -1)
    return (attended, query_grad, text_grad, vis_grad)


def on_device(
    queries, text_kv, out_grad, text_segment, visual_rows, kv_weight, visual_dest, visual_sample
):
    group_count = lax.axis_size("group")
    row_count = visual_rows.shape[0]
    capacity = 2 * row_count // group_count
    slot_count = group_count * capacity
    partial_kv = jnp.dot(visual_rows, kv_weight, preferred_element_type=jnp.float32)
    visual_kv = lax.psum_scatter(partial_kv, "tensor", scatter_dimension=1, tiled=True).astype(
        jnp.bfloat16
    )
    destination = visual_dest[:, 0]
    targets = jnp.arange(group_count, dtype=jnp.int32)
    onehot = (destination[:, None] == targets[None, :]).astype(jnp.int32)
    row_order = jnp.arange(row_count, dtype=jnp.int32)
    earlier = (row_order[None, :] < row_order[:, None]).astype(jnp.int32)
    before = jnp.dot(earlier, onehot)
    rank = jnp.sum(before * onehot, axis=1)
    position = destination * capacity + rank
    select = position[None, :] == jnp.arange(slot_count, dtype=jnp.int32)[:, None]
    outgoing = jnp.dot(
        select.astype(jnp.bfloat16), visual_kv, preferred_element_type=jnp.float32
    ).astype(jnp.bfloat16)
    sample_tags = jnp.max(jnp.where(select, visual_sample[None, :], -1), axis=1)
    arrived, arrived_tags = (
        lax.all_to_all(outgoing, "group", split_axis=0, concat_axis=0, tiled=True),
        lax.all_to_all(sample_tags, "group", split_axis=0, concat_axis=0, tiled=True),
    )
    attended, query_grad, text_grad, vis_grad = attend_local(
        queries, text_kv, out_grad, text_segment[0], arrived, arrived_tags
    )
    returned = lax.all_to_all(vis_grad, "group", split_axis=0, concat_axis=0, tiled=True)
    kv_grad = jnp.take(returned, position, axis=0)
    visual_grad = jnp.dot(
        lax.all_gather(kv_grad, "tensor", axis=1, tiled=True),
        kv_weight.T,
        preferred_element_type=jnp.float32,
    ).astype(jnp.bfloat16)
    return (attended, query_grad, text_grad, visual_grad)


def solution(mesh):
    placed = (
        P("group", "tensor"),
        P("group", "tensor"),
        P("group", "tensor"),
        P("group", None),
        P("group", "tensor"),
        P("tensor", None),
        P("group", None),
        P("group"),
    )
    return jax.shard_map(
        on_device,
        mesh=mesh,
        in_specs=placed,
        out_specs=(
            P("group", "tensor"),
            P("group", "tensor"),
            P("group", "tensor"),
            P("group", "tensor"),
        ),
        check_vma=False,
    )
```

profile of v0, /device:TPU:0, one launch (start us, length us, event | category | flops | bytes accessed | tf_op | source)
XLA Modules:
  0.0 166.3 jit_solution(5540921267171185399)
XLA Ops:
  8.2 5.6 %fusion.126 = f32[128,2048]{1,0:T(8,128)} fusion(bf16[128,2048]{1,0:T(8,128)(2,1)S(1)} %copy-done, bf16[2048,2048]{1,0:T(8,128)(2,1)} %param.13), kind=kOutput, calls=%fused_computation.190 | convolution fusion | flops 1073741824 | bytes 9961472 | tf_op jit(solution)/shard_map/dot_general | solution.py:74
  14.9 5.2 %all-to-all-start.1 = ((s32[8,32,1]{1,2,0:T(1,128)}), s32[8,32,1]{1,2,0:T(1,128)S(1)}, u32[]{:S(2)}, u32[]{:S(2)}) async-start(s32[8,32,1]{1,2,0:T(1,128)} %bitcast.5), calls=%async_computation.2 | async-start | bytes 8192 | tf_op jit(solution)/shard_map/all_to_all | solution.py:93
  22.7 1.9 %all-to-all-done.1 = s32[8,32,1]{1,2,0:T(1,128)S(1)} async-done(((s32[8,32,1]{1,2,0:T(1,128)}), s32[8,32,1]{1,2,0:T(1,128)S(1)}, u32[]{:S(2)}, u32[]{:S(2)}) %all-to-all-start.1) | async-done | bytes 1056 | tf_op jit(solution)/shard_map/all_to_all | solution.py:93
  25.9 18.0 %reduce-scatter.2.cloned.1.call-done = f32[128,512]{1,0:T(8,128)} async-done(((f32[128,2048]{1,0:T(8,128)}), f32[128,512]{1,0:T(8,128)}) %reduce-scatter.2.cloned.1.call-update) | async-done | bytes 262160 | tf_op jit(solution)/shard_map/reduce_scatter | solution.py:75
  43.9 1.9 %convolution_convert_fusion.1 = bf16[256,512]{1,0:T(8,128)(2,1)} fusion(f32[128,512]{1,0:T(8,128)} %reduce-scatter.2.cloned.1.call-done, s32[128]{0:T(128)S(1)} %multiply_add_fusion), kind=kOutput, calls=%fused_computation.62 | convolution fusion | flops 33783808 | bytes 524800 | tf_op jit(solution)/shard_map/dot_general | solution.py:87
  45.7 3.7 %all-to-all-start = ((bf16[8,32,512]{2,1,0:T(8,128)(2,1)}), bf16[8,32,512]{2,1,0:T(8,128)(2,1)S(1)}, u32[]{:S(2)}, u32[]{:S(2)}) async-start(bf16[8,32,512]{2,1,0:T(8,128)(2,1)} %bitcast.3), calls=%async_computation.1 | async-start | bytes 524288 | tf_op jit(solution)/shard_map/all_to_all | solution.py:92
  49.6 6.7 %all-to-all-done = bf16[8,32,512]{2,1,0:T(8,128)(2,1)S(1)} async-done(((bf16[8,32,512]{2,1,0:T(8,128)(2,1)}), bf16[8,32,512]{2,1,0:T(8,128)(2,1)S(1)}, u32[]{:S(2)}, u32[]{:S(2)}) %all-to-all-start) | async-done | bytes 262176 | tf_op jit(solution)/shard_map/all_to_all | solution.py:92
  56.8 2.3 %fusion.125 = (f32[2,384]{1,0:T(2,128)S(1)}, f32[2,384,640]{1,2,0:T(8,128)}) fusion(pred[384,640]{0,1:T(8,128)(4,1)S(1)} %pad_add_fusion, bf16[384,2,4,128]{0,3,2,1:T(8,128)(2,1)S(1)} %bitcast.311, bf16[256,2,128]{2,0,1:T(8,128)(2,1)S(1)} %bitcast.327, bf16[384,2,128]{2,0,1:T(8,128)(2,1)S(1)} %bitcast.319), kind=kOutput, calls=%fused_computation.189 | convolution fusion | flops 255918720 | bytes 3509248 | tf_op jit(solution)/shard_map/sub | solution.py:37
  59.1 2.3 %fusion.124 = (f32[2,384]{1,0:T(2,128)S(1)}, f32[2,384,640]{1,2,0:T(8,128)}) fusion(pred[384,640]{0,1:T(8,128)(4,1)S(1)} %pad_add_fusion, bf16[384,2,4,128]{0,3,2,1:T(8,128)(2,1)S(1)} %bitcast.312, bf16[256,2,128]{2,0,1:T(8,128)(2,1)S(1)} %bitcast.328, bf16[384,2,128]{2,0,1:T(8,128)(2,1)S(1)} %bitcast.320), kind=kOutput, calls=%fused_computation.188 | convolution fusion | flops 255918720 | bytes 3509248 | tf_op jit(solution)/shard_map/sub | solution.py:37
  61.5 2.3 %fusion.123 = (f32[2,384]{1,0:T(2,128)S(1)}, f32[2,384,640]{1,2,0:T(8,128)}) fusion(pred[384,640]{0,1:T(8,128)(4,1)S(1)} %pad_add_fusion, bf16[384,2,4,128]{0,3,2,1:T(8,128)(2,1)S(1)} %bitcast.313, bf16[256,2,128]{2,0,1:T(8,128)(2,1)S(1)} %bitcast.329, bf16[384,2,128]{2,0,1:T(8,128)(2,1)S(1)} %bitcast.321), kind=kOutput, calls=%fused_computation.187 | convolution fusion | flops 255918720 | bytes 3509248 | tf_op jit(solution)/shard_map/sub | solution.py:37
  63.8 2.3 %fusion.122 = (f32[2,384]{1,0:T(2,128)S(1)}, f32[2,384,640]{1,2,0:T(8,128)}) fusion(pred[384,640]{0,1:T(8,128)(4,1)S(1)} %pad_add_fusion, bf16[384,2,4,128]{0,3,2,1:T(8,128)(2,1)S(1)} %bitcast.314, bf16[256,2,128]{2,0,1:T(8,128)(2,1)S(1)} %bitcast.330, bf16[384,2,128]{2,0,1:T(8,128)(2,1)S(1)} %bitcast.322), kind=kOutput, calls=%fused_computation.186 | convolution fusion | flops 255918720 | bytes 3509248 | tf_op jit(solution)/shard_map/sub | solution.py:37
  66.2 1.7 %fusion.85 = f32[2,640,384]{2,1,0:T(8,128)} fusion(bf16[384,2,4,128]{0,3,2,1:T(8,128)(2,1)S(1)} %bitcast.299, bf16[256,2,128]{0,2,1:T(8,128)(2,1)S(1)} %bitcast.291, bf16[384,2,128]{0,2,1:T(8,128)(2,1)S(1)} %get-tuple-element.19), kind=kOutput, calls=%fused_computation.138 | convolution fusion | flops 126484480 | bytes 2490368 | tf_op jit(solution)/shard_map/pgd,kgd->gpk/dot_general | solution.py:45
  67.9 1.8 %fusion.86 = f32[2,640,384]{2,1,0:T(8,128)} fusion(bf16[384,2,4,128]{0,3,2,1:T(8,128)(2,1)S(1)} %bitcast.300, bf16[256,2,128]{0,2,1:T(8,128)(2,1)S(1)} %bitcast.292, bf16[384,2,128]{0,2,1:T(8,128)(2,1)S(1)} %get-tuple-element.19), kind=kOutput, calls=%fused_computation.139 | convolution fusion | flops 126484480 | bytes 2490368 | tf_op jit(solution)/shard_map/pgd,kgd->gpk/dot_general | solution.py:45
  69.8 1.7 %fusion.87 = f32[2,640,384]{2,1,0:T(8,128)} fusion(bf16[384,2,4,128]{0,3,2,1:T(8,128)(2,1)S(1)} %bitcast.301, bf16[256,2,128]{0,2,1:T(8,128)(2,1)S(1)} %bitcast.293, bf16[384,2,128]{0,2,1:T(8,128)(2,1)S(1)} %get-tuple-element.19), kind=kOutput, calls=%fused_computation.140 | convolution fusion | flops 126484480 | bytes 2490368 | tf_op jit(solution)/shard_map/pgd,kgd->gpk/dot_general | solution.py:45
  71.5 1.8 %fusion.88 = f32[2,640,384]{2,1,0:T(8,128)} fusion(bf16[384,2,4,128]{0,3,2,1:T(8,128)(2,1)S(1)} %bitcast.302, bf16[256,2,128]{0,2,1:T(8,128)(2,1)S(1)} %bitcast.294, bf16[384,2,128]{0,2,1:T(8,128)(2,1)S(1)} %get-tuple-element.19), kind=kOutput, calls=%fused_computation.141 | convolution fusion | flops 126484480 | bytes 2490368 | tf_op jit(solution)/shard_map/pgd,kgd->gpk/dot_general | solution.py:45
  73.3 1.3 fusion.73
  74.6 4.9 %fusion.63 = f32[2,640,128]{1,2,0:T(8,128)} fusion(f32[2,640,384]{2,1,0:T(8,128)} %fusion.85, bf16[384,2,4,128]{0,3,2,1:T(8,128)(2,1)S(1)} %bitcast.315, f32[2,384,640]{1,2,0:T(8,128)} %get-tuple-element.29, f32[2,384]{1,0:T(2,128)S(1)} %get-tuple-element.28), kind=kOutput, calls=%fused_computation.102 | convolution fusion | flops 129271168 | bytes 8722432 | tf_op jit(solution)/shard_map/gpk,pgd->kgd/dot_general | solution.py:53
  79.6 2.1 %convolution_add_fusion.2 = f32[2,640,128]{1,2,0:T(8,128)S(1)} fusion(f32[2,640,128]{1,2,0:T(8,128)} %fusion.73, bf16[384,2,4,128]{0,3,2,1:T(8,128)(2,1)S(1)} %bitcast.304, f32[2,384,640]{1,2,0:T(8,128)} %get-tuple-element.27, f32[2,384]{1,0:T(2,128)S(1)} %get-tuple-element.26), kind=kOutput, calls=%fused_computation.56 | convolution fusion | flops 126976000 | bytes 3476480 | tf_op jit(solution)/shard_map/gpk,pgd->kgd/dot_general | solution.py:56
  81.7 5.2 %convolution_add_fusion.5 = f32[2,640,128]{1,2,0:T(8,128)} fusion(f32[2,640,128]{1,2,0:T(8,128)} %fusion.63, f32[2,640,384]{2,1,0:T(8,128)} %fusion.86, bf16[384,2,4,128]{0,3,2,1:T(8,128)(2,1)S(1)} %bitcast.316, f32[2,384,640]{1,2,0:T(8,128)} %get-tuple-element.27, f32[2,384]{1,0:T(2,128)S(1)} %get-tuple-element.26), kind=kOutput, calls=%fused_computation.59 | convolution fusion | flops 129435008 | bytes 9377792 | tf_op jit(solution)/shard_map/gpk,pgd->kgd/dot_general | solution.py:53
  86.9 2.9 %convolution_add_fusion.1 = f32[2,640,128]{1,2,0:T(8,128)} fusion(f32[2,640,128]{1,2,0:T(8,128)S(1)} %convolution_add_fusion.2, bf16[384,2,4,128]{0,3,2,1:T(8,128)(2,1)S(1)} %bitcast.305, f32[2,384,640]{1,2,0:T(8,128)} %get-tuple-element.25, f32[2,384]{1,0:T(2,128)S(1)} %get-tuple-element.24), kind=kOutput, calls=%fused_computation.55 | convolution fusion | flops 126976000 | bytes 3476480 | tf_op jit(solution)/shard_map/gpk,pgd->kgd/dot_general | solution.py:56
  89.8 5.1 %convolution_add_fusion.4 = f32[2,640,128]{1,2,0:T(8,128)} fusion(f32[2,640,128]{1,2,0:T(8,128)} %convolution_add_fusion.5, f32[2,640,384]{2,1,0:T(8,128)} %fusion.87, bf16[384,2,4,128]{0,3,2,1:T(8,128)(2,1)S(1)} %bitcast.317, f32[2,384,640]{1,2,0:T(8,128)} %get-tuple-element.25, f32[2,384]{1,0:T(2,128)S(1)} %get-tuple-element.24), kind=kOutput, calls=%fused_computation.58 | convolution fusion | flops 129435008 | bytes 9377792 | tf_op jit(solution)/shard_map/gpk,pgd->kgd/dot_general | solution.py:53
  94.8 2.1 %fusion.38 = bf16[640,2,1,128]{0,3,1,2:T(8,128)(2,1)S(1)} fusion(f32[2,640,128]{1,2,0:T(8,128)} %convolution_add_fusion.1, bf16[384,2,4,128]{0,3,2,1:T(8,128)(2,1)S(1)} %bitcast.306, f32[2,384,640]{1,2,0:T(8,128)} %get-tuple-element.23, f32[2,384]{1,0:T(2,128)S(1)} %get-tuple-element.22), kind=kOutput, calls=%fused_computation.63 | convolution fusion | flops 127139840 | bytes 3148800 | tf_op jit(solution)/shard_map/gpk,pgd->kgd/dot_general | solution.py:56
  97.0 4.4 %fusion.39 = bf16[640,2,1,128]{0,3,1,2:T(8,128)(2,1)S(1)} fusion(f32[2,640,128]{1,2,0:T(8,128)} %convolution_add_fusion.4, f32[2,640,384]{2,1,0:T(8,128)} %fusion.88, bf16[384,2,4,128]{0,3,2,1:T(8,128)(2,1)S(1)} %bitcast.318, f32[2,384,640]{1,2,0:T(8,128)} %get-tuple-element.23, f32[2,384]{1,0:T(2,128)S(1)} %get-tuple-element.22), kind=kOutput, calls=%fused_computation.64 | convolution fusion | flops 129598848 | bytes 9050112 | tf_op jit(solution)/shard_map/gpk,pgd->kgd/dot_general | solution.py:53
  101.5 4.0 %fusion.44 = bf16[384,2,1,128]{0,3,1,2:T(8,128)(2,1)S(1)} fusion(f32[2,640,384]{2,1,0:T(8,128)} %fusion.85, bf16[256,2,128]{2,0,1:T(8,128)(2,1)S(1)} %bitcast.331, bf16[384,2,128]{2,0,1:T(8,128)(2,1)S(1)} %bitcast.323, f32[2,384,640]{1,2,0:T(8,128)} %get-tuple-element.29, f32[2,384]{1,0:T(2,128)S(1)} %get-tuple-element.28), kind=kOutput, calls=%fused_computation.77 | convolution fusion | flops 130024832 | bytes 4459520 | tf_op jit(solution)/shard_map/gpk,kgd->pgd/dot_general | solution.py:49
  105.5 4.0 %fusion.45 = bf16[384,2,1,128]{0,3,1,2:T(8,128)(2,1)S(1)} fusion(f32[2,640,384]{2,1,0:T(8,128)} %fusion.86, bf16[256,2,128]{2,0,1:T(8,128)(2,1)S(1)} %bitcast.332, bf16[384,2,128]{2,0,1:T(8,128)(2,1)S(1)} %bitcast.324, f32[2,384,640]{1,2,0:T(8,128)} %get-tuple-element.27, f32[2,384]{1,0:T(2,128)S(1)} %get-tuple-element.26), kind=kOutput, calls=%fused_computation.78 | convolution fusion | flops 130024832 | bytes 4459520 | tf_op jit(solution)/shard_map/gpk,kgd->pgd/dot_general | solution.py:49
  109.6 4.3 %fusion.46 = bf16[384,2,1,128]{0,3,1,2:T(8,128)(2,1)S(1)} fusion(f32[2,640,384]{2,1,0:T(8,128)} %fusion.87, bf16[256,2,128]{2,0,1:T(8,128)(2,1)S(1)} %bitcast.333, bf16[384,2,128]{2,0,1:T(8,128)(2,1)S(1)} %bitcast.325, f32[2,384,640]{1,2,0:T(8,128)} %get-tuple-element.25, f32[2,384]{1,0:T(2,128)S(1)} %get-tuple-element.24), kind=kOutput, calls=%fused_computation.79 | convolution fusion | flops 130024832 | bytes 4459520 | tf_op jit(solution)/shard_map/gpk,kgd->pgd/dot_general | solution.py:49
  113.9 4.0 %fusion.47 = bf16[384,2,1,128]{0,3,1,2:T(8,128)(2,1)S(1)} fusion(f32[2,640,384]{2,1,0:T(8,128)} %fusion.88, bf16[256,2,128]{2,0,1:T(8,128)(2,1)S(1)} %bitcast.334, bf16[384,2,128]{2,0,1:T(8,128)(2,1)S(1)} %bitcast.326, f32[2,384,640]{1,2,0:T(8,128)} %get-tuple-element.23, f32[2,384]{1,0:T(2,128)S(1)} %get-tuple-element.22), kind=kOutput, calls=%fused_computation.80 | convolution fusion | flops 130024832 | bytes 4459520 | tf_op jit(solution)/shard_map/gpk,kgd->pgd/dot_general | solution.py:49
  117.9 2.1 %fusion.40 = bf16[384,2,1,128]{0,3,1,2:T(8,128)(2,1)S(1)} fusion(bf16[256,2,128]{0,2,1:T(8,128)(2,1)S(1)} %bitcast.295, bf16[384,2,128]{0,2,1:T(8,128)(2,1)S(1)} %get-tuple-element.19, f32[2,384,640]{1,2,0:T(8,128)} %get-tuple-element.29, f32[2,384]{1,0:T(2,128)S(1)} %get-tuple-element.28), kind=kOutput, calls=%fused_computation.73 | convolution fusion | flops 127565824 | bytes 2493440 | tf_op jit(solution)/shard_map/gpk,kgd->pgd/dot_general | solution.py:41
  125.2 3.4 %all-to-all-start.2 = ((bf16[8,32,512]{2,1,0:T(8,128)(2,1)}), bf16[8,32,512]{2,1,0:T(8,128)(2,1)S(1)}, u32[]{:S(2)}, u32[]{:S(2)}) async-start(bf16[8,32,512]{2,1,0:T(8,128)(2,1)} %all_to_all.24), calls=%async_computation.3 | async-start | bytes 524288 | tf_op jit(solution)/shard_map/all_to_all | solution.py:98
  132.4 3.1 %all-to-all-done.2 = bf16[8,32,512]{2,1,0:T(8,128)(2,1)S(1)} async-done(((bf16[8,32,512]{2,1,0:T(8,128)(2,1)}), bf16[8,32,512]{2,1,0:T(8,128)(2,1)S(1)}, u32[]{:S(2)}, u32[]{:S(2)}) %all-to-all-start.2) | async-done | bytes 262176 | tf_op jit(solution)/shard_map/all_to_all | solution.py:98
  136.4 16.0 %all_gather.3 = bf16[128,2048]{1,0:T(8,128)(2,1)S(1)} all-gather(bf16[128,512]{1,0:T(8,128)(2,1)S(1)} %broadcast_select_fusion), channel_id=1, replica_groups=mesh['group'=8,'tensor'=4] {'tensor'}, dimensions={1}, use_global_device_ids=true | all-gather | bytes 655360 | tf_op jit(solution)/shard_map/all_gather | solution.py:101
  152.4 7.1 %convolution_convert_fusion = bf16[128,2048]{1,0:T(8,128)(2,1)} fusion(bf16[128,2048]{1,0:T(8,128)(2,1)S(1)} %all_gather.3, bf16[2048,2048]{1,0:T(8,128)(2,1)} %param.13), kind=kOutput, calls=%fused_computation.9 | convolution fusion | flops 1074003968 | bytes 9437184 | tf_op jit(solution)/shard_map/dot_general | solution.py:100
  (73 shorter events, 16.5 us)
Async XLA Ops:
  7.2 1.0 copy-start
  7.2 6.7 %copy-start.11 = (s32[128,1]{0,1:T(1,128)S(1)}, s32[128,1]{0,1:T(1,128)}, u32[]{:S(2)}) copy-start(s32[128,1]{0,1:T(1,128)} %param.14) | copy-start | bytes 1540
  7.2 6.9 %copy-start.10 = (s32[128]{0:T(128)S(1)}, s32[128]{0:T(128)}, u32[]{:S(2)}) copy-start(s32[128]{0:T(128)} %param.15) | copy-start | bytes 1540
  7.2 12.8 %copy-start.4 = (bf16[384,512]{1,0:T(8,128)(2,1)S(1)}, bf16[384,512]{1,0:T(8,128)(2,1)}, u32[]{:S(2)}) copy-start(bf16[384,512]{1,0:T(8,128)(2,1)} %param.9) | copy-start | bytes 1179652
  7.2 13.0 %copy-start.9 = (s32[1,384]{1,0:T(1,128)S(1)}, s32[1,384]{1,0:T(1,128)}, u32[]{:S(2)}) copy-start(s32[1,384]{1,0:T(1,128)} %param.11) | copy-start | bytes 4612
  7.2 36.6 %reduce-scatter.2.cloned.1.call-start = ((), (), s32[]{:S(2)}) async-start(), calls=%async_computation.4 | async-start | bytes 1310720 | tf_op jit(solution)/shard_map/reduce_scatter | solution.py:75
  13.8 8.1 %copy-start.1 = (bf16[384,1024]{1,0:T(8,128)(2,1)S(1)}, bf16[384,1024]{1,0:T(8,128)(2,1)}, u32[]{:S(2)}) copy-start(bf16[384,1024]{1,0:T(8,128)(2,1)} %param.8) | copy-start | bytes 2359300
  13.9 8.5 %copy-start.2 = (bf16[384,1024]{1,0:T(8,128)(2,1)S(1)}, bf16[384,1024]{1,0:T(8,128)(2,1)}, u32[]{:S(2)}) copy-start(bf16[384,1024]{1,0:T(8,128)(2,1)} %param.10) | copy-start | bytes 2359300
  14.9 9.8 %all-to-all-start.1 = ((s32[8,32,1]{1,2,0:T(1,128)}), s32[8,32,1]{1,2,0:T(1,128)S(1)}, u32[]{:S(2)}, u32[]{:S(2)}) async-start(s32[8,32,1]{1,2,0:T(1,128)} %bitcast.5), calls=%async_computation.2 | async-start | bytes 8192 | tf_op jit(solution)/shard_map/all_to_all | solution.py:93
  22.3 27.2 %copy-start.3 = (pred[384,384]{0,1:T(8,128)(4,1)S(1)}, pred[384,384]{0,1:T(8,128)(4,1)}, u32[]{:S(2)}) copy-start(pred[384,384]{0,1:T(8,128)(4,1)} %fusion.66) | copy-start | bytes 442372
  22.7 34.1 %copy-start.6 = (bf16[384,2,1,128]{3,0,1,2:T(8,128)(2,1)S(1)}, bf16[384,2,1,128]{3,0,1,2:T(8,128)(2,1)}, u32[]{:S(2)}) copy-start(bf16[384,2,1,128]{3,0,1,2:T(8,128)(2,1)} %copy.242) | copy-start | bytes 589828
  45.7 10.6 %all-to-all-start = ((bf16[8,32,512]{2,1,0:T(8,128)(2,1)}), bf16[8,32,512]{2,1,0:T(8,128)(2,1)S(1)}, u32[]{:S(2)}, u32[]{:S(2)}) async-start(bf16[8,32,512]{2,1,0:T(8,128)(2,1)} %bitcast.3), calls=%async_computation.1 | async-start | bytes 524288 | tf_op jit(solution)/shard_map/all_to_all | solution.py:92
  56.8 7.0 %copy-start.7 = (bf16[256,2,1,128]{3,0,1,2:T(8,128)(2,1)}, bf16[256,2,1,128]{3,0,1,2:T(8,128)(2,1)S(1)}, u32[]{:S(2)}) copy-start(bf16[256,2,1,128]{3,0,1,2:T(8,128)(2,1)S(1)} %copy.253) | copy-start | bytes 393220
  69.8 3.6 %copy-start.13 = (f32[2,384,640]{1,2,0:T(8,128)S(1)}, f32[2,384,640]{1,2,0:T(8,128)}, u32[]{:S(2)}) copy-start(f32[2,384,640]{1,2,0:T(8,128)} %get-tuple-element.29) | copy-start | bytes 5898244
  97.0 4.5 %copy-start.8 = (bf16[256,2,1,128]{3,0,1,2:T(8,128)(2,1)S(1)}, bf16[256,2,1,128]{3,0,1,2:T(8,128)(2,1)}, u32[]{:S(2)}) copy-start(bf16[256,2,1,128]{3,0,1,2:T(8,128)(2,1)} %copy-done.7) | copy-start | bytes 393220
  117.9 2.1 %copy-start.14 = (f32[2,384,640]{1,2,0:T(8,128)S(1)}, f32[2,384,640]{1,2,0:T(8,128)}, u32[]{:S(2)}) copy-start(f32[2,384,640]{1,2,0:T(8,128)} %get-tuple-element.27) | copy-start | bytes 5898244
  120.0 1.5 copy-start.15
  121.6 1.5 copy-start.12
  125.2 10.3 %all-to-all-start.2 = ((bf16[8,32,512]{2,1,0:T(8,128)(2,1)}), bf16[8,32,512]{2,1,0:T(8,128)(2,1)S(1)}, u32[]{:S(2)}, u32[]{:S(2)}) async-start(bf16[8,32,512]{2,1,0:T(8,128)(2,1)} %all_to_all.24), calls=%async_computation.3 | async-start | bytes 524288 | tf_op jit(solution)/shard_map/all_to_all | solution.py:98
  129.7 1.3 copy-start.5
Sparse Core Ops, SparseCore 0:
  14.0 29.8 reduce-scatter.1
where the time goes:
time: 167 us; the launch traced here: 166 us
  matrix products  79.4 us (48%)
  waiting for transfers between devices  29.7 us (18%)
  blocking collectives  16 us (10%)
  between operations  14.4 us (9%)
  local copies, waits for them, and re-layouts  12.3 us (7%)
  starting transfers between devices  12.3 us (7%)
  other arithmetic  2.19 us (1%)
    dot_general x4, matrix products, attend_local(): jnp.einsum('gpk,pgd->kgd', dscores, query_one, preferred_element_type=jnp...  19.6 us
    reduce_scatter x1, waiting for transfers between devices, on_device(): lax.psum_scatter(partial_kv, 'tensor', scatter_dimension=1, tiled=True)  18 us
    dot_general x4, matrix products, attend_local(): jnp.einsum('gpk,kgd->pgd', dscores, keys, preferred_element_type=jnp.floa...  16.4 us
    all_gather x1, blocking collectives, on_device(): lax.all_gather(kv_grad, 'tensor', axis=1, tiled=True)  16 us
    sub x4, matrix products, attend_local(): expo = jnp.where(mask, jnp.exp(scores - top), 0.0)  9.25 us
    unnamed x41, local copies, waits for them, and re-layouts  8.53 us
    dot_general x4, matrix products, attend_local(): jnp.einsum('gpk,pgd->kgd', weights, grad_one, preferred_element_type=jnp....  8.45 us
    dot_general x4, matrix products, attend_local(): jnp.einsum('pgd,kgd->gpk', grad_one, values, preferred_element_type=jnp.f...  7.12 us
  transfers between devices with their start and end apart: 4, of which 4 were waited for; matrix products, arithmetic and copies ran while one was open for 5% of the time, Pallas kernels for 0%

commit v1 on v0

v1 whole, which is shorter than its diff:
```python
import functools
import math

import jax
import jax.numpy as jnp
from jax import lax
from jax.experimental import pallas as pl
from jax.experimental.pallas import tpu as pltpu
from jax.sharding import PartitionSpec as P

HD = 128
QPK = 4
TILE = 128
SCALE = 1.0 / math.sqrt(HD)
LOG2E = math.log2(math.e)
F32 = jnp.float32
BF16 = jnp.bfloat16
MIB = 1024 * 1024


def dot_nn(a, b):
    return lax.dot_general(a, b, (((1,), (0,)), ((), ())), preferred_element_type=F32)


def dot_nt(a, b):
    return lax.dot_general(a, b, (((1,), (1,)), ((), ())), preferred_element_type=F32)


def dot_tn(a, b):
    return lax.dot_general(a, b, (((0,), (0,)), ((), ())), preferred_element_type=F32)


def params(mib):
    return pltpu.CompilerParams(vmem_limit_bytes=mib * MIB)


def cost(flops, moved, exps=0):
    return pl.CostEstimate(flops=flops, bytes_accessed=moved, transcendentals=exps)


def project_kernel(order_ref, rows_ref, weight_ref, *refs, steps):
    outs, total = refs[:-1], refs[-1]
    block, step = pl.program_id(0), pl.program_id(1)
    depth = weight_ref.shape[0]
    part = dot_nn(rows_ref[:, pl.ds(pl.multiple_of(step * depth, depth), depth)], weight_ref[...])

    @pl.when(step == 0)
    def _():
        total[...] = part

    @pl.when(step > 0)
    def _():
        total[...] += part

    for at, out in enumerate(outs):

        @pl.when((step == steps - 1) & (block == at))
        def _(out=out):
            out[...] = total[...].astype(out.dtype)


def project(order, rows, weight, width, kinds):
    count, features = rows.shape
    steps = 4
    depth = features // steps
    whole = pl.BlockSpec((count, width), lambda i, k, order: (0, 0))
    return pl.pallas_call(
        functools.partial(project_kernel, steps=steps),
        out_shape=[jax.ShapeDtypeStruct((count, width), kind) for kind in kinds],
        grid_spec=pltpu.PrefetchScalarGridSpec(
            num_scalar_prefetch=1,
            grid=(len(kinds), steps),
            in_specs=[
                pl.BlockSpec((count, features), lambda i, k, order: (0, 0)),
                pl.BlockSpec((depth, width), lambda i, k, order: (k, order[i])),
            ],
            out_specs=[whole for _ in kinds],
            scratch_shapes=[pltpu.VMEM((count, width), F32)],
        ),
        compiler_params=params(12),
        cost_estimate=cost(
            2 * count * features * width * len(kinds), 2 * features * width * len(kinds)
        ),
        name="project",
    )(order, rows, weight)


def place_kernel(me_ref, dest_ref, sample_ref, own_ref, *refs, capacity, flips):
    parts, outs = refs[: -len(flips)], refs[-len(flips) :]
    total = own_ref[...]
    for part in parts:
        total = total + part[...].astype(F32)
    tags = jnp.broadcast_to(sample_ref[...] + 1, (total.shape[0], TILE)).astype(F32)
    wide = jnp.concatenate([total, tags], axis=1).astype(BF16)
    rows = total.shape[0]
    for out, targets in zip(outs, flips, strict=True):
        slots = len(targets) * capacity
        slot = lax.broadcasted_iota(jnp.int32, (slots, rows), 0)
        row = lax.broadcasted_iota(jnp.int32, (slots, rows), 1)
        target = jnp.zeros((slots, rows), jnp.int32)
        if len(targets) > 8:
            target = slot // capacity
        else:
            for at, flip in enumerate(targets):
                target = jnp.where(slot // capacity == at, me_ref[0] ^ flip, target)
        select = (dest_ref[...] == target) & (slot % capacity == row % capacity)
        out[...] = dot_nn(select.astype(F32).astype(BF16), wide).astype(BF16)


def place(me, dest_row, sample_col, own, parts, capacity, flips):
    rows, width = own.shape
    vmem = pl.BlockSpec(memory_space=pltpu.VMEM)
    return pl.pallas_call(
        functools.partial(place_kernel, capacity=capacity, flips=flips),
        out_shape=[
            jax.ShapeDtypeStruct((len(f) * capacity, width + TILE), BF16) for f in flips
        ],
        in_specs=[pl.BlockSpec(memory_space=pltpu.SMEM)] + [vmem] * (3 + len(parts)),
        out_specs=[vmem] * len(flips),
        compiler_params=params(8),
        cost_estimate=cost(2 * 256 * rows * width, 4 * rows * width),
        name="place",
    )(me, dest_row, sample_col, own, *parts)


def collect_kernel(me_ref, dest_ref, *refs, capacity, flips):
    parts, out = refs[:-1], refs[-1]
    rows = out.shape[0]
    total = jnp.zeros(out.shape, F32)
    for part, targets in zip(parts, flips, strict=True):
        slots = len(targets) * capacity
        slot = lax.broadcasted_iota(jnp.int32, (rows, slots), 1)
        row = lax.broadcasted_iota(jnp.int32, (rows, slots), 0)
        target = jnp.zeros((rows, slots), jnp.int32)
        if len(targets) > 8:
            target = slot // capacity
        else:
            for at, flip in enumerate(targets):
                target = jnp.where(slot // capacity == at, me_ref[0] ^ flip, target)
        select = (dest_ref[...] == target) & (slot % capacity == row % capacity)
        total = total + dot_nn(select.astype(F32).astype(BF16), part[...])
    out[...] = total.astype(BF16)


def collect(me, dest_col, parts, capacity, flips):
    rows, width = dest_col.shape[0], parts[0].shape[1]
    vmem = pl.BlockSpec(memory_space=pltpu.VMEM)
    return pl.pallas_call(
        functools.partial(collect_kernel, capacity=capacity, flips=flips),
        out_shape=jax.ShapeDtypeStruct((rows, width), BF16),
        in_specs=[pl.BlockSpec(memory_space=pltpu.SMEM)] + [vmem] * (1 + len(parts)),
        out_specs=vmem,
        compiler_params=params(8),
        cost_estimate=cost(2 * 256 * rows * width, 4 * rows * width),
        name="collect",
    )(me, dest_col, *parts)


def stacked(ref, tile, head):
    first = head * QPK * HD
    return jnp.concatenate(
        [
            ref[tile * TILE : (tile + 1) * TILE, first + j * HD : first + (j + 1) * HD]
            for j in range(QPK)
        ],
        axis=0,
    )


def text_span(tile):
    return max(0, tile - 1) * TILE, (tile + 1) * TILE


def text_mask(segment_ref, tile):
    low, high = text_span(tile)
    span = high - low
    own = segment_ref[:, tile * TILE : (tile + 1) * TILE].astype(F32)
    keys = jnp.concatenate(
        [
            jnp.broadcast_to(segment_ref[:, at : at + TILE].astype(F32), (TILE, TILE)).T
            for at in range(low, high, TILE)
        ],
        axis=0,
    )
    key_place = lax.broadcasted_iota(jnp.int32, (span, TILE), 0) + low
    token_place = lax.broadcasted_iota(jnp.int32, (span, TILE), 1) + tile * TILE
    mask = (keys == own) & (key_place <= token_place)
    return jnp.where(mask, 0.0, -jnp.inf)


def slot_mask(tags, segment_ref, tile):
    own = segment_ref[:, tile * TILE : (tile + 1) * TILE].astype(F32) + 1.0
    return jnp.where(tags.astype(F32) == own, 0.0, -jnp.inf)


def repeated(mask):
    return jnp.concatenate([mask] * QPK, axis=1)


def text_stats_kernel(query_ref, grad_ref, kv_ref, segment_ref, top_ref, sum_ref, inner_ref):
    tiles, heads = query_ref.shape[0] // TILE, kv_ref.shape[1] // (2 * HD)
    for tile in range(tiles):
        low, high = text_span(tile)
        mask = repeated(text_mask(segment_ref, tile))
        for head in range(heads):
            at = head * tiles + tile
            keys = kv_ref[low:high, head * 2 * HD : head * 2 * HD + HD]
            values = kv_ref[low:high, head * 2 * HD + HD : (head + 1) * 2 * HD]
            scores = dot_nt(keys, stacked(query_ref, tile, head)) + mask
            top = jnp.max(scores, axis=0, keepdims=True)
            expo = jnp.exp2((scores - top) * (SCALE * LOG2E))
            dprobs = dot_nt(values, stacked(grad_ref, tile, head))
            top_ref[at : at + 1, :] = top
            sum_ref[at : at + 1, :] = jnp.sum(expo, axis=0, keepdims=True)
            inner_ref[at : at + 1, :] = jnp.sum(expo * dprobs, axis=0, keepdims=True)


def text_stats(queries, out_grad, text_kv, segment):
    tiles, heads = queries.shape[0] // TILE, text_kv.shape[1] // (2 * HD)
    vmem = pl.BlockSpec(memory_space=pltpu.VMEM)
    shape = jax.ShapeDtypeStruct((tiles * heads, QPK * TILE), F32)
    pairs = heads * QPK * (2 * tiles - 1) * TILE * TILE
    return pl.pallas_call(
        text_stats_kernel,
        out_shape=[shape] * 3,
        in_specs=[vmem] * 4,
        out_specs=[vmem] * 3,
        compiler_params=params(24),
        cost_estimate=cost(4 * pairs * HD, 4 * queries.size, pairs),
        name="text_stats",
    )(queries, out_grad, text_kv, segment)


def slot_grad_kernel(
    query_ref, grad_ref, segment_ref, top_ref, sum_ref, inner_ref, *refs, arrivals
):
    visual, refs = refs[:arrivals], refs[arrivals:]
    outs, (all_top_ref, scale_ref, all_inner_ref) = refs[:arrivals], refs[arrivals:]
    tiles = query_ref.shape[0] // TILE
    width = visual[0].shape[1] - TILE
    heads = width // (2 * HD)
    tags = jnp.concatenate([one[:, width:] for one in visual], axis=0)
    masks = [slot_mask(tags, segment_ref, tile) for tile in range(tiles)]
    for head in range(heads):
        first = head * 2 * HD
        keys = jnp.concatenate([one[:, first : first + HD] for one in visual], axis=0)
        values = jnp.concatenate([one[:, first + HD : first + 2 * HD] for one in visual], axis=0)
        key_grad = jnp.zeros((keys.shape[0], HD), F32)
        value_grad = jnp.zeros((keys.shape[0], HD), F32)
        for tile in range(tiles):
            at = head * tiles + tile
            query, grad = stacked(query_ref, tile, head), stacked(grad_ref, tile, head)
            scores = dot_nt(keys, query) + repeated(masks[tile])
            dprobs = dot_nt(values, grad)
            text_top = top_ref[at : at + 1, :]
            top = jnp.maximum(text_top, jnp.max(scores, axis=0, keepdims=True))
            expo = jnp.exp2((scores - top) * (SCALE * LOG2E))
            shift = jnp.exp2((text_top - top) * (SCALE * LOG2E))
            total = sum_ref[at : at + 1, :] * shift + jnp.sum(expo, axis=0, keepdims=True)
            inverse = 1.0 / total
            inner = (
                inner_ref[at : at + 1, :] * shift + jnp.sum(expo * dprobs, axis=0, keepdims=True)
            ) * inverse
            probs = expo * inverse
            dscores = (probs * (dprobs - inner)).astype(BF16)
            value_grad = value_grad + dot_nn(probs.astype(BF16), grad)
            key_grad = key_grad + dot_nn(dscores, query)
            all_top_ref[at : at + 1, :] = top
            scale_ref[at : at + 1, :] = inverse
            all_inner_ref[at : at + 1, :] = inner
        start = 0
        for out in outs:
            count = out.shape[0]
            out[:, first : first + HD] = (key_grad[start : start + count] * SCALE).astype(BF16)
            out[:, first + HD : first + 2 * HD] = value_grad[start : start + count].astype(BF16)
            start += count


def slot_grad(queries, out_grad, segment, stats, visual):
    vmem = pl.BlockSpec(memory_space=pltpu.VMEM)
    shape = jax.ShapeDtypeStruct(stats[0].shape, F32)
    slots = sum(one.shape[0] for one in visual)
    pairs = slots * queries.shape[0] * queries.shape[1] // HD
    found = pl.pallas_call(
        functools.partial(slot_grad_kernel, arrivals=len(visual)),
        out_shape=[
            jax.ShapeDtypeStruct((one.shape[0], one.shape[1] - TILE), BF16) for one in visual
        ]
        + [shape] * 3,
        in_specs=[vmem] * (6 + len(visual)),
        out_specs=[vmem] * (3 + len(visual)),
        compiler_params=params(24),
        cost_estimate=cost(8 * pairs * HD, 4 * queries.size, pairs),
        name="slot_grad",
    )(queries, out_grad, segment, *stats, *visual)
    return found[: len(visual)], found[len(visual) :]


def text_grad_kernel(
    query_ref, grad_ref, kv_ref, segment_ref, top_ref, scale_ref, inner_ref, *refs, arrivals
):
    visual = refs[:arrivals]
    attended_ref, query_grad_ref, kv_grad_ref = refs[arrivals:]
    tiles, heads = query_ref.shape[0] // TILE, kv_ref.shape[1] // (2 * HD)
    width = kv_ref.shape[1]
    tags = jnp.concatenate([one[:, width:] for one in visual], axis=0)
    masks = [
        jnp.concatenate(
            [text_mask(segment_ref, tile), slot_mask(tags, segment_ref, tile)], axis=0
        )
        for tile in range(tiles)
    ]
    for head in range(heads):
        first = head * 2 * HD
        slot_keys = jnp.concatenate([one[:, first : first + HD] for one in visual], axis=0)
        slot_values = jnp.concatenate(
            [one[:, first + HD : first + 2 * HD] for one in visual], axis=0
        )
        key_held = value_held = None
        for tile in range(tiles):
            at = head * tiles + tile
            low, high = text_span(tile)
            keys = jnp.concatenate([kv_ref[low:high, first : first + HD], slot_keys], axis=0)
            values = jnp.concatenate(
                [kv_ref[low:high, first + HD : first + 2 * HD], slot_values], axis=0
            )
            query, grad = stacked(query_ref, tile, head), stacked(grad_ref, tile, head)
            scores = dot_nt(keys, query) + repeated(masks[tile])
            expo = jnp.exp2((scores - top_ref[at : at + 1, :]) * (SCALE * LOG2E))
            probs = expo * scale_ref[at : at + 1, :]
            dprobs = dot_nt(values, grad)
            dscores = (probs * (dprobs - inner_ref[at : at + 1, :])).astype(BF16)
            weights = probs.astype(BF16)
            attended = dot_tn(values, weights)
            query_grad = dot_tn(keys, dscores) * SCALE
            place_at = slice(tile * TILE, (tile + 1) * TILE)
            for j in range(QPK):
                columns = slice((head * QPK + j) * HD, (head * QPK + j + 1) * HD)
                lanes = slice(j * TILE, (j + 1) * TILE)
                attended_ref[place_at, columns] = attended[:, lanes].T.astype(BF16)
                query_grad_ref[place_at, columns] = query_grad[:, lanes].T.astype(BF16)
            key_part = dot_nn(dscores[: high - low], query)
            value_part = dot_nn(weights[: high - low], grad)
            if tile > 0:
                before = slice((tile - 1) * TILE, tile * TILE)
                kv_grad_ref[before, first : first + HD] = (
                    (key_held + key_part[:TILE]) * SCALE
                ).astype(BF16)
                kv_grad_ref[before, first + HD : first + 2 * HD] = (
                    value_held + value_part[:TILE]
                ).astype(BF16)
            key_held, value_held = key_part[high - low - TILE :], value_part[high - low - TILE :]
        last = slice((tiles - 1) * TILE, tiles * TILE)
        kv_grad_ref[last, first : first + HD] = (key_held * SCALE).astype(BF16)
        kv_grad_ref[last, first + HD : first + 2 * HD] = value_held.astype(BF16)


def text_grad(queries, out_grad, text_kv, segment, stats, visual):
    vmem = pl.BlockSpec(memory_space=pltpu.VMEM)
    slots = sum(one.shape[0] for one in visual)
    pairs = (slots + 2 * TILE) * queries.shape[0] * queries.shape[1] // HD
    return pl.pallas_call(
        functools.partial(text_grad_kernel, arrivals=len(visual)),
        out_shape=[
            jax.ShapeDtypeStruct(queries.shape, BF16),
            jax.ShapeDtypeStruct(queries.shape, BF16),
            jax.ShapeDtypeStruct(text_kv.shape, BF16),
        ],
        in_specs=[vmem] * (7 + len(visual)),
        out_specs=[vmem] * 3,
        compiler_params=params(32),
        cost_estimate=cost(12 * pairs * HD, 8 * queries.size, pairs),
        name="text_grad",
    )(queries, out_grad, text_kv, segment, *stats, *visual)


def feature_kernel(order_ref, *refs, count, held, last):
    parts, (weight_ref, *rest) = refs[:count], refs[count:]
    before_ref = rest[0] if held else None
    out_ref, total = rest[-2], rest[-1]
    step = pl.program_id(0)
    for at, part in enumerate(parts):

        @pl.when(step == at)
        def _(at=at, part=part):
            term = dot_nt(part[...], weight_ref[...])
            if at == 0:
                total[...] = term + before_ref[...] if held else term
            else:
                total[...] += term

    @pl.when(step == count - 1)
    def _():
        out_ref[...] = total[...].astype(out_ref.dtype)


def feature_grad(order, parts, weight, before, last):
    rows, width = parts[0].shape
    features = weight.shape[0]
    count = len(parts)
    whole = lambda shape: pl.BlockSpec(shape, lambda i, order: (0, 0))
    return pl.pallas_call(
        functools.partial(feature_kernel, count=count, held=before is not None, last=last),
        out_shape=jax.ShapeDtypeStruct((rows, features), BF16 if last else F32),
        grid_spec=pltpu.PrefetchScalarGridSpec(
            num_scalar_prefetch=1,
            grid=(count,),
            in_specs=[whole((rows, width))] * count
            + [pl.BlockSpec((features, width), lambda i, order: (0, order[i]))]
            + ([whole((rows, features))] if before is not None else []),
            out_specs=whole((rows, features)),
            scratch_shapes=[pltpu.VMEM((rows, features), F32)],
        ),
        compiler_params=params(16),
        cost_estimate=cost(2 * rows * width * features * count, 2 * width * features * count),
        name="feature_grad",
    )(order, *parts, weight, *([before] if before is not None else []))


def flipped(count, flip):
    return [(i, i ^ flip) for i in range(count)]


def on_device(
    queries, text_kv, out_grad, text_segment, visual_rows, kv_weight, visual_dest, visual_sample
):
    groups, shares = lax.axis_size("group"), lax.axis_size("tensor")
    rows = visual_rows.shape[0]
    capacity = 2 * rows // groups
    width = kv_weight.shape[1] // shares
    here = lax.axis_index("tensor").astype(jnp.int32)
    me = lax.axis_index("group").astype(jnp.int32).reshape(1)
    dest_row = visual_dest.reshape(1, rows)
    sample_col = visual_sample.reshape(rows, 1)

    flips = list(range(shares - 1, 0, -1)) + [0]
    order = here ^ jnp.array(flips, jnp.int32)
    half = shares // 2
    blocks = project(order[:half], visual_rows, kv_weight, width, [BF16] * half)
    landed = [
        lax.ppermute(block, "tensor", flipped(shares, flip))
        for block, flip in zip(blocks, flips[:half], strict=True)
    ]
    near = project(
        order[half:], visual_rows, kv_weight, width, [BF16] * (shares - half - 1) + [F32]
    )
    landed += [
        lax.ppermute(block, "tensor", flipped(shares, flip))
        for block, flip in zip(near[:-1], flips[half:-1], strict=True)
    ]
    stats = text_stats(queries, out_grad, text_kv, text_segment)

    pairwise = groups == 8
    if pairwise:
        same = [2 * j for j in range(groups // 2)]
        other = [2 * j + 1 for j in range(groups // 2)]
        slots = [[flip] for flip in same] + [other]
        *mine, across = place(me, dest_row, sample_col, near[-1], landed, capacity, slots)
        theirs = lax.ppermute(across, "group", flipped(groups, 1))
        pairs = [
            jnp.concatenate([one, theirs[j * capacity : (j + 1) * capacity]], axis=0)
            for j, one in enumerate(mine)
        ]
        visual = [
            pair if flip == 0 else lax.ppermute(pair, "group", flipped(groups, flip))
            for pair, flip in zip(pairs, same, strict=True)
        ]
    else:
        slots = [list(range(groups))]
        (sent,) = place(me, dest_row, sample_col, near[-1], landed, capacity, slots)
        visual = [
            lax.all_to_all(
                sent.reshape(groups, capacity, -1), "group", split_axis=0, concat_axis=0, tiled=True
            ).reshape(groups * capacity, -1)
        ]

    grads, final = slot_grad(queries, out_grad, text_segment, stats, visual)
    attended, query_grad, text_kv_grad = text_grad(
        queries, out_grad, text_kv, text_segment, final, visual
    )

    if pairwise:
        back = [
            grad if flip == 0 else lax.ppermute(grad, "group", flipped(groups, flip))
            for grad, flip in zip(grads, same, strict=True)
        ]
        kept = jnp.concatenate([one[:capacity] for one in back], axis=0)
        passed = jnp.concatenate([one[capacity:] for one in back], axis=0)
        passed = lax.ppermute(passed, "group", flipped(groups, 1))
        returned, slots = [kept, passed], [same, other]
    else:
        returned = [
            lax.all_to_all(
                grads[0].reshape(groups, capacity, -1),
                "group",
                split_axis=0,
                concat_axis=0,
                tiled=True,
            ).reshape(groups * capacity, -1)
        ]
    kv_grad = collect(me, visual_dest, returned, capacity, slots)

    gathered = [
        lax.ppermute(kv_grad, "tensor", flipped(shares, flip)) for flip in flips[:-1]
    ] + [kv_grad]
    begun = feature_grad(order[half:][::-1], gathered[half:][::-1], kv_weight, None, False)
    visual_grad = feature_grad(order[:half], gathered[:half], kv_weight, begun, True)
    return (attended, query_grad, text_kv_grad, visual_grad)


def solution(mesh):
    placed = (
        P("group", "tensor"),
        P("group", "tensor"),
        P("group", "tensor"),
        P("group", None),
        P("group", "tensor"),
        P("tensor", None),
        P("group", None),
        P("group"),
    )
    return jax.shard_map(
        on_device,
        mesh=mesh,
        in_specs=placed,
        out_specs=(
            P("group", "tensor"),
            P("group", "tensor"),
            P("group", "tensor"),
            P("group", "tensor"),
        ),
        check_vma=False,
    )
```

time: 167 us -> 66.4 us (0.40)
  matrix products: 79.4 us -> 0 us
  Pallas kernels: 0 us -> 22.5 us
  blocking collectives: 16 us -> 0 us
  between operations: 14.4 us -> 0.84 us
  waiting for transfers between devices: 29.7 us -> 16.2 us
  starting transfers between devices: 12.3 us -> 17.6 us
  local copies, waits for them, and re-layouts: 12.3 us -> 8.27 us
    dot_general x24 -> x0, matrix products: 70.2 us -> none  [the longest x4 19.6 us: attend_local(): jnp.einsum('gpk,pgd->kgd', dscores, query_one, preferred_element_type=jnp...]
    pallas_call x0 -> x9, Pallas kernels: none -> 22.5 us  [the longest x2 6.32 us: project(): pl.pallas_call(functools.partial(project_kernel, steps=steps), out_shape=...]
    reduce_scatter x1 -> x0, waiting for transfers between devices: 18 us -> none  [on_device(): lax.psum_scatter(partial_kv, 'tensor', scatter_dimension=1, tiled=True)]
    ppermute x0 -> x14, starting transfers between devices: none -> 17.6 us  [the longest x3 5.82 us: on_device(): lax.ppermute(block, 'tensor', flipped(shares, flip))]
    ppermute x0 -> x14, waiting for transfers between devices: none -> 16.2 us  [the longest x3 7.06 us: on_device(): lax.ppermute(block, 'tensor', flipped(shares, flip))]
    all_gather x1 -> x0, blocking collectives: 16 us -> none  [on_device(): lax.all_gather(kv_grad, 'tensor', axis=1, tiled=True)]
    all_to_all x3 -> x0, starting transfers between devices: 12.2 us -> none  [the longest x1 5.17 us: on_device(): lax.all_to_all(sample_tags, 'group', split_axis=0, concat_axis=0, tiled=T...]
    all_to_all x3 -> x0, waiting for transfers between devices: 11.7 us -> none  [the longest x1 6.73 us: on_device(): lax.all_to_all(outgoing, 'group', split_axis=0, concat_axis=0, tiled=True)]
  transfers between devices with their start and end apart: 4 -> 14, of which waited for: 4 -> 10; matrix products, arithmetic and copies ran while one was open for 5% -> 1% of each run, Pallas kernels for 0% -> 18%
where the time goes in v1:
time: 66.4 us; the launch traced here: 66.2 us
  Pallas kernels  22.5 us (34%)
  starting transfers between devices  17.6 us (27%)
  waiting for transfers between devices  16.2 us (24%)
  local copies, waits for them, and re-layouts  8.27 us (12%)
  between operations  0.84 us (1%)
  other arithmetic  0.72 us (1%)
    unnamed x23, local copies, waits for them, and re-layouts  7.96 us
    ppermute x3, waiting for transfers between devices, on_device(): lax.ppermute(block, 'tensor', flipped(shares, flip))  7.06 us
    pallas_call x2, Pallas kernels, project(): pl.pallas_call(functools.partial(project_kernel, steps=steps), out_shape=...  6.32 us
    pallas_call x2, Pallas kernels, feature_grad(): pl.pallas_call(functools.partial(feature_kernel, count=count, held=before...  5.91 us
    ppermute x3, starting transfers between devices, on_device(): lax.ppermute(block, 'tensor', flipped(shares, flip))  5.82 us
    pallas_call x1, Pallas kernels, text_grad(): pl.pallas_call(functools.partial(text_grad_kernel, arrivals=len(visual)),...  5.13 us
    ppermute x3, waiting for transfers between devices, on_device(): lax.ppermute(pair, 'group', flipped(groups, flip))  4.85 us
    ppermute x3, starting transfers between devices, on_device(): lax.ppermute(kv_grad, 'tensor', flipped(shares, flip))  4.44 us
  transfers between devices with their start and end apart: 14, of which 10 were waited for; matrix products, arithmetic and copies ran while one was open for 1% of the time, Pallas kernels for 18%

profile of v1, /device:TPU:0, one launch (start us, length us, event | category | flops | bytes accessed | tf_op | source)
XLA Modules:
  0.0 66.2 jit_solution(2314041255286885732)
XLA Ops:
  0.6 0.7 %broadcast_xor_fusion = s32[4]{0:T(128)S(1)} fusion(s32[4]{0:T(128)} %constant.11.clone, s32[]{:T(128)S(6)} %axis_index.25), kind=kLoop, calls=%fused_computation.6 | loop fusion | flops 4 | bytes 36 | tf_op jit(solution)/shard_map/xor | solution.py:437
  1.4 3.4 %copy-done = bf16[2048,2048]{1,0:T(8,128)(2,1)S(1)} copy-done((bf16[2048,2048]{1,0:T(8,128)(2,1)S(1)}, bf16[2048,2048]{1,0:T(8,128)(2,1)}, u32[]{:S(2)}) %copy-start) | copy-done | bytes 8388632
  4.8 1.0 %copy-done.3 = bf16[128,2048]{1,0:T(8,128)(2,1)S(1)} copy-done((bf16[128,2048]{1,0:T(8,128)(2,1)S(1)}, bf16[128,2048]{1,0:T(8,128)(2,1)}, u32[]{:S(2)}) %copy-start.3) | copy-done | bytes 524312
  5.9 3.1 %project.3 = (bf16[128,512]{1,0:T(8,128)(2,1)S(1)}, bf16[128,512]{1,0:T(8,128)(2,1)S(1)}) custom-call(s32[2]{0:T(128)S(1)} %get-tuple-element.60.order_ref, bf16[128,2048]{1,0:T(8,128)(2,1)S(1)} %copy-done.3, bf16[2048,2048]{1,0:T(8,128)(2,1)S(1)} %copy-done), custom_call_target="tpu_custom_call" | custom-call | flops 536870912 | bytes 4194304 | tf_op jit(solution)/shard_map/project/pallas_call | solution.py:67
  9.0 5.1 %collective-permute-start = (bf16[128,512]{1,0:T(8,128)(2,1)S(1)}, bf16[128,512]{1,0:T(8,128)(2,1)S(1)}, u32[]{:S(2)}, u32[]{:S(2)}) collective-permute-start(bf16[128,512]{1,0:T(8,128)(2,1)S(1)} %get-tuple-element.30), channel_id=1, source_target_pairs={{0,3},{1,2},{2,1},{3,0},{4,7},{5,6},{6,5},{7,4},{8,11},{9,10},{10,... | collective-permute-start | bytes 393224 | tf_op jit(solution)/shard_map/ppermute | solution.py:441
  14.1 3.2 %project.2 = (bf16[128,512]{1,0:T(8,128)(2,1)S(1)}, f32[128,512]{1,0:T(8,128)S(1)}) custom-call(s32[2]{0:T(128)S(1)} %get-tuple-element.61.order_ref, bf16[128,2048]{1,0:T(8,128)(2,1)S(1)} %copy-done.4, bf16[2048,2048]{1,0:T(8,128)(2,1)S(1)} %copy-done.1), custom_call_target="tpu_custom_call" | custom-call | flops 536870912 | bytes 4194304 | tf_op jit(solution)/shard_map/project/pallas_call | solution.py:67
  17.3 0.7 %collective-permute-start.2 = (bf16[128,512]{1,0:T(8,128)(2,1)S(1)}, bf16[128,512]{1,0:T(8,128)(2,1)S(1)}, u32[]{:S(2)}, u32[]{:S(2)}) collective-permute-start(bf16[128,512]{1,0:T(8,128)(2,1)S(1)} %get-tuple-element.32), channel_id=1, source_target_pairs={{0,1},{1,0},{2,3},{3,2},{4,5},{5,4},{6,7},{7,6},{8,9},{9,8},{10,11... | collective-permute-start | bytes 393224 | tf_op jit(solution)/shard_map/ppermute | solution.py:448
  18.1 0.4 collective-permute-done.refs_0_
  18.5 6.6 %collective-permute-done.1.refs_1_ = bf16[128,512]{1,0:T(8,128)(2,1)S(1)} collective-permute-done((bf16[128,512]{1,0:T(8,128)(2,1)S(1)}, bf16[128,512]{1,0:T(8,128)(2,1)S(1)}, u32[]{:S(2)}, u32[]{:S(2)}) %collective-permute-start.1) | collective-permute-done | bytes 131104 | tf_op jit(solution)/shard_map/ppermute | solution.py:441
  25.2 0.3 place.1
  25.7 1.1 %text_stats.1 = (f32[6,512]{1,0:T(8,128)S(1)}, f32[6,512]{1,0:T(8,128)S(1)}, f32[6,512]{1,0:T(8,128)S(1)}) custom-call(bf16[384,1024]{1,0:T(8,128)(2,1)S(1)} %copy-done.5, bf16[384,1024]{1,0:T(8,128)(2,1)S(1)} %copy-done.6, bf16[384,512]{1,0:T(8,128)(2,1)S(1)} %copy-done.7, s32[1,384]{1,0:T(1,128)S(1)} %copy-done.9), custom_call_target="tpu_custom_call" | custom-call | flops 335544320 | bytes 1572864 | tf_op jit(solution)/shard_map/text_stats/pallas_call | solution.py:223
  27.1 1.6 %collective-permute-start.4 = (bf16[64,640]{1,0:T(8,128)(2,1)S(1)}, bf16[64,640]{1,0:T(8,128)(2,1)S(1)}, u32[]{:S(2)}, u32[]{:S(2)}) collective-permute-start(bf16[64,640]{1,0:T(8,128)(2,1)S(1)} %pad_maximum_fusion.3), channel_id=1, source_target_pairs={{0,8},{4,12},{8,0},{12,4},{16,24},{20,28},{24,16},{28,20},{1,9},{5... | collective-permute-start | bytes 245768 | tf_op jit(solution)/shard_map/ppermute | solution.py:465
  28.6 1.6 %collective-permute-start.5 = (bf16[64,640]{1,0:T(8,128)(2,1)S(1)}, bf16[64,640]{1,0:T(8,128)(2,1)S(1)}, u32[]{:S(2)}, u32[]{:S(2)}) collective-permute-start(bf16[64,640]{1,0:T(8,128)(2,1)S(1)} %pad_maximum_fusion.4), channel_id=1, source_target_pairs={{0,16},{4,20},{8,24},{12,28},{16,0},{20,4},{24,8},{28,12},{1,17},{... | collective-permute-start | bytes 245768 | tf_op jit(solution)/shard_map/ppermute | solution.py:465
  30.2 0.5 collective-permute-start.6
  30.8 1.0 %collective-permute-done.4.refs_1_ = bf16[64,640]{1,0:T(8,128)(2,1)S(1)} collective-permute-done((bf16[64,640]{1,0:T(8,128)(2,1)S(1)}, bf16[64,640]{1,0:T(8,128)(2,1)S(1)}, u32[]{:S(2)}, u32[]{:S(2)}) %collective-permute-start.4) | collective-permute-done | bytes 81952 | tf_op jit(solution)/shard_map/ppermute | solution.py:465
  31.8 2.2 %collective-permute-done.5.refs_2_ = bf16[64,640]{1,0:T(8,128)(2,1)S(1)} collective-permute-done((bf16[64,640]{1,0:T(8,128)(2,1)S(1)}, bf16[64,640]{1,0:T(8,128)(2,1)S(1)}, u32[]{:S(2)}, u32[]{:S(2)}) %collective-permute-start.5) | collective-permute-done | bytes 81952 | tf_op jit(solution)/shard_map/ppermute | solution.py:465
  33.9 1.7 %collective-permute-done.6.refs_3_ = bf16[64,640]{1,0:T(8,128)(2,1)S(1)} collective-permute-done((bf16[64,640]{1,0:T(8,128)(2,1)S(1)}, bf16[64,640]{1,0:T(8,128)(2,1)S(1)}, u32[]{:S(2)}, u32[]{:S(2)}) %collective-permute-start.6) | collective-permute-done | bytes 81952 | tf_op jit(solution)/shard_map/ppermute | solution.py:465
  35.6 3.4 %slot_grad.1 = (bf16[64,512]{1,0:T(8,128)(2,1)S(1)}, bf16[64,512]{1,0:T(8,128)(2,1)S(1)}, bf16[64,512]{1,0:T(8,128)(2,1)S(1)}, bf16[64,512]{1,0:T(8,128)(2,1)S(1...) custom-call(bf16[384,1024]{1,0:T(8,128)(2,1)S(1)} %copy-done.5, ...), custom_call_target="tpu_custom_call" | custom-call | flops 805306368 | bytes 1572864 | tf_op jit(solution)/shard_map/slot_grad/pallas_call | solution.py:284
  39.0 0.6 collective-permute-start.7
  39.6 0.8 %collective-permute-start.8 = (bf16[64,512]{1,0:T(8,128)(2,1)S(1)}, bf16[64,512]{1,0:T(8,128)(2,1)S(1)}, u32[]{:S(2)}, u32[]{:S(2)}) collective-permute-start(bf16[64,512]{1,0:T(8,128)(2,1)S(1)} %get-tuple-element.46), channel_id=1, source_target_pairs={{0,16},{4,20},{8,24},{12,28},{16,0},{20,4},{24,8},{28,12},{1,17},{... | collective-permute-start | bytes 196616 | tf_op jit(solution)/shard_map/ppermute | solution.py:484
  40.4 2.2 %collective-permute-start.9 = (bf16[64,512]{1,0:T(8,128)(2,1)S(1)}, bf16[64,512]{1,0:T(8,128)(2,1)S(1)}, u32[]{:S(2)}, u32[]{:S(2)}) collective-permute-start(bf16[64,512]{1,0:T(8,128)(2,1)S(1)} %get-tuple-element.47), channel_id=1, source_target_pairs={{0,24},{4,28},{8,16},{12,20},{16,8},{20,12},{24,0},{28,4},{1,25},{... | collective-permute-start | bytes 196616 | tf_op jit(solution)/shard_map/ppermute | solution.py:484
  42.6 0.8 %collective-permute-done.7 = bf16[64,512]{1,0:T(8,128)(2,1)S(1)} collective-permute-done((bf16[64,512]{1,0:T(8,128)(2,1)S(1)}, bf16[64,512]{1,0:T(8,128)(2,1)S(1)}, u32[]{:S(2)}, u32[]{:S(2)}) %collective-permute-start.7) | collective-permute-done | bytes 65568 | tf_op jit(solution)/shard_map/ppermute | solution.py:484
  43.3 0.5 collective-permute-done.8
  43.9 1.7 %collective-permute-done.9 = bf16[64,512]{1,0:T(8,128)(2,1)S(1)} collective-permute-done((bf16[64,512]{1,0:T(8,128)(2,1)S(1)}, bf16[64,512]{1,0:T(8,128)(2,1)S(1)}, u32[]{:S(2)}, u32[]{:S(2)}) %collective-permute-start.9) | collective-permute-done | bytes 65568 | tf_op jit(solution)/shard_map/ppermute | solution.py:484
  45.9 1.1 %collective-permute-done.10.refs_1_ = bf16[128,512]{1,0:T(8,128)(2,1)S(1)} collective-permute-done((bf16[128,512]{1,0:T(8,128)(2,1)S(1)}, bf16[128,512]{1,0:T(8,128)(2,1)S(1)}, u32[]{:S(2)}, u32[]{:S(2)}) %collective-permute-start.10) | collective-permute-done | bytes 131104 | tf_op jit(solution)/shard_map/ppermute | solution.py:489
  47.0 0.3 collect.1.refs_0_
  47.3 3.0 %collective-permute-start.12 = (bf16[128,512]{1,0:T(8,128)(2,1)S(1)}, bf16[128,512]{1,0:T(8,128)(2,1)S(1)}, u32[]{:S(2)}, u32[]{:S(2)}) collective-permute-start(bf16[128,512]{1,0:T(8,128)(2,1)S(1)} %collect.1.refs_0_), channel_id=1, source_target_pairs={{0,2},{1,3},{2,0},{3,1},{4,6},{5,7},{6,4},{7,5},{8,10},{9,11},{10,... | collective-permute-start | bytes 393224 | tf_op jit(solution)/shard_map/ppermute | solution.py:504
  50.4 1.3 %collective-permute-start.11 = (bf16[128,512]{1,0:T(8,128)(2,1)S(1)}, bf16[128,512]{1,0:T(8,128)(2,1)S(1)}, u32[]{:S(2)}, u32[]{:S(2)}) collective-permute-start(bf16[128,512]{1,0:T(8,128)(2,1)S(1)} %collect.1.refs_0_), channel_id=1, source_target_pairs={{0,3},{1,2},{2,1},{3,0},{4,7},{5,6},{6,5},{7,4},{8,11},{9,10},{10,... | collective-permute-start | bytes 393224 | tf_op jit(solution)/shard_map/ppermute | solution.py:504
  51.7 5.1 %text_grad.1 = (bf16[384,1024]{1,0:T(8,128)(2,1)}, bf16[384,1024]{1,0:T(8,128)(2,1)}, bf16[384,512]{1,0:T(8,128)(2,1)}) custom-call(bf16[384,1024]{1,0:T(8,128)(2,1)S(1)} %copy-done.5, bf16[384,1024]{1,0:T(8,128)(2,1)S(1)} %copy-done.6, bf16[384,512]{1,0:T(8,128)(2,1)S(1)} %copy-done.7, s32[1,384]{1,0:T(1,128)S(1)} %copy-done.9, ...), custom_call_target="tpu_custom_call" | custom-call | flops 2415919104 | bytes 3145728 | tf_op jit(solution)/shard_map/text_grad/pallas_call | solution.py:362
  56.8 3.4 %copy-done.2 = bf16[2048,2048]{1,0:T(8,128)(2,1)S(1)} copy-done((bf16[2048,2048]{1,0:T(8,128)(2,1)S(1)}, bf16[2048,2048]{1,0:T(8,128)(2,1)}, u32[]{:S(2)}) %copy-start.2) | copy-done | bytes 8388632
  60.2 2.5 %feature_grad.2.refs_3_ = f32[128,2048]{1,0:T(8,128)S(1)} custom-call(s32[2]{0:T(128)S(1)} %rev.3.order_ref, bf16[128,512]{1,0:T(8,128)(2,1)S(1)} %collect.1.refs_0_, bf16[128,512]{1,0:T(8,128)(2,1)S(1)} %collective-permute-done.13.refs_1_, bf16[2048,2048]{1,0:T(8,128)(2,1)S(1)} %copy-done.2), custom_call_target="tpu_custom_call" | custom-call | flops 536870912 | bytes 4194304 | tf_op jit(solution)/shard_map/feature_grad/pallas_call | solution.py:402
  62.8 3.4 %feature_grad.3 = bf16[128,2048]{1,0:T(8,128)(2,1)} custom-call(s32[2]{0:T(128)S(1)} %get-tuple-element.60.order_ref, bf16[128,512]{1,0:T(8,128)(2,1)S(1)} %collective-permute-done.11.refs_0_, bf16[128,512]{1,0:T(8,128)(2,1)S(1)} %collective-permute-done.12.refs_1_, bf16[2048,2048]{1,0:T(8,128)(2,1)S(1)} %copy-done.2, f32[128,2048]{1,0:T(8,128)S(1)} %feature_grad.2.refs_3_), custom_call_target="tpu_custom_call" | custom-call | flops 536870912 | bytes 4194304 | tf_op jit(solution)/shard_map/feature_grad/pallas_call | solution.py:402
  (43 shorter events, 1.0 us)
Async XLA Ops:
  1.4 3.4 %copy-start = (bf16[2048,2048]{1,0:T(8,128)(2,1)S(1)}, bf16[2048,2048]{1,0:T(8,128)(2,1)}, u32[]{:S(2)}) copy-start(bf16[2048,2048]{1,0:T(8,128)(2,1)} %refs_2_.3) | copy-start | bytes 25165828
  4.8 1.0 %copy-start.3 = (bf16[128,2048]{1,0:T(8,128)(2,1)S(1)}, bf16[128,2048]{1,0:T(8,128)(2,1)}, u32[]{:S(2)}) copy-start(bf16[128,2048]{1,0:T(8,128)(2,1)} %rows_ref.3) | copy-start | bytes 1572868
  5.8 8.3 %copy-start.1 = (bf16[2048,2048]{1,0:T(8,128)(2,1)S(1)}, bf16[2048,2048]{1,0:T(8,128)(2,1)}, u32[]{:S(2)}) copy-start(bf16[2048,2048]{1,0:T(8,128)(2,1)} %refs_2_.3) | copy-start | bytes 25165828
  5.8 8.3 %copy-start.4 = (bf16[128,2048]{1,0:T(8,128)(2,1)S(1)}, bf16[128,2048]{1,0:T(8,128)(2,1)}, u32[]{:S(2)}) copy-start(bf16[128,2048]{1,0:T(8,128)(2,1)} %rows_ref.3) | copy-start | bytes 1572868
  5.8 12.2 %copy-start.10 = (s32[128]{0:T(128)S(1)}, s32[128]{0:T(128)}, u32[]{:S(2)}) copy-start(s32[128]{0:T(128)} %param.16) | copy-start | bytes 1540
  5.8 19.4 %copy-start.8 = (s32[128,1]{0,1:T(1,128)S(1)}, s32[128,1]{0,1:T(1,128)}, u32[]{:S(2)}) copy-start(s32[128,1]{0,1:T(1,128)} %param.15) | copy-start | bytes 1540
  5.8 19.8 %copy-start.5 = (bf16[384,1024]{1,0:T(8,128)(2,1)S(1)}, bf16[384,1024]{1,0:T(8,128)(2,1)}, u32[]{:S(2)}) copy-start(bf16[384,1024]{1,0:T(8,128)(2,1)} %query_ref.5) | copy-start | bytes 2359300
  5.8 19.8 %copy-start.6 = (bf16[384,1024]{1,0:T(8,128)(2,1)S(1)}, bf16[384,1024]{1,0:T(8,128)(2,1)}, u32[]{:S(2)}) copy-start(bf16[384,1024]{1,0:T(8,128)(2,1)} %grad_ref.5) | copy-start | bytes 2359300
  5.8 19.8 %copy-start.7 = (bf16[384,512]{1,0:T(8,128)(2,1)S(1)}, bf16[384,512]{1,0:T(8,128)(2,1)}, u32[]{:S(2)}) copy-start(bf16[384,512]{1,0:T(8,128)(2,1)} %kv_ref.3) | copy-start | bytes 1179652
  5.8 19.8 %copy-start.9 = (s32[1,384]{1,0:T(1,128)S(1)}, s32[1,384]{1,0:T(1,128)}, u32[]{:S(2)}) copy-start(s32[1,384]{1,0:T(1,128)} %segment_ref.5) | copy-start | bytes 4612
  9.0 9.5 %collective-permute-start = (bf16[128,512]{1,0:T(8,128)(2,1)S(1)}, bf16[128,512]{1,0:T(8,128)(2,1)S(1)}, u32[]{:S(2)}, u32[]{:S(2)}) collective-permute-start(bf16[128,512]{1,0:T(8,128)(2,1)S(1)} %get-tuple-element.30), channel_id=1, source_target_pairs={{0,3},{1,2},{2,1},{3,0},{4,7},{5,6},{6,5},{7,4},{8,11},{9,10},{10,... | collective-permute-start | bytes 393224 | tf_op jit(solution)/shard_map/ppermute | solution.py:441
  14.1 11.1 %collective-permute-start.1 = (bf16[128,512]{1,0:T(8,128)(2,1)S(1)}, bf16[128,512]{1,0:T(8,128)(2,1)S(1)}, u32[]{:S(2)}, u32[]{:S(2)}) collective-permute-start(bf16[128,512]{1,0:T(8,128)(2,1)S(1)} %get-tuple-element.31), channel_id=1, source_target_pairs={{0,2},{1,3},{2,0},{3,1},{4,6},{5,7},{6,4},{7,5},{8,10},{9,11},{10,... | collective-permute-start | bytes 393224 | tf_op jit(solution)/shard_map/ppermute | solution.py:441
  17.3 7.9 %collective-permute-start.2 = (bf16[128,512]{1,0:T(8,128)(2,1)S(1)}, bf16[128,512]{1,0:T(8,128)(2,1)S(1)}, u32[]{:S(2)}, u32[]{:S(2)}) collective-permute-start(bf16[128,512]{1,0:T(8,128)(2,1)S(1)} %get-tuple-element.32), channel_id=1, source_target_pairs={{0,1},{1,0},{2,3},{3,2},{4,5},{5,4},{6,7},{7,6},{8,9},{9,8},{10,11... | collective-permute-start | bytes 393224 | tf_op jit(solution)/shard_map/ppermute | solution.py:448
  25.6 1.5 %collective-permute-start.3 = (bf16[128,640]{1,0:T(8,128)(2,1)S(1)}, bf16[128,640]{1,0:T(8,128)(2,1)S(1)}, u32[]{:S(2)}, u32[]{:S(2)}) collective-permute-start(bf16[128,640]{1,0:T(8,128)(2,1)S(1)} %get-tuple-element.34), channel_id=1, source_target_pairs={{0,4},{4,0},{8,12},{12,8},{16,20},{20,16},{24,28},{28,24},{1,5},{5... | collective-permute-start | bytes 491528 | tf_op jit(solution)/shard_map/ppermute | solution.py:459
  27.1 4.7 %collective-permute-start.4 = (bf16[64,640]{1,0:T(8,128)(2,1)S(1)}, bf16[64,640]{1,0:T(8,128)(2,1)S(1)}, u32[]{:S(2)}, u32[]{:S(2)}) collective-permute-start(bf16[64,640]{1,0:T(8,128)(2,1)S(1)} %pad_maximum_fusion.3), channel_id=1, source_target_pairs={{0,8},{4,12},{8,0},{12,4},{16,24},{20,28},{24,16},{28,20},{1,9},{5... | collective-permute-start | bytes 245768 | tf_op jit(solution)/shard_map/ppermute | solution.py:465
  28.6 5.3 %collective-permute-start.5 = (bf16[64,640]{1,0:T(8,128)(2,1)S(1)}, bf16[64,640]{1,0:T(8,128)(2,1)S(1)}, u32[]{:S(2)}, u32[]{:S(2)}) collective-permute-start(bf16[64,640]{1,0:T(8,128)(2,1)S(1)} %pad_maximum_fusion.4), channel_id=1, source_target_pairs={{0,16},{4,20},{8,24},{12,28},{16,0},{20,4},{24,8},{28,12},{1,17},{... | collective-permute-start | bytes 245768 | tf_op jit(solution)/shard_map/ppermute | solution.py:465
  30.2 5.4 %collective-permute-start.6 = (bf16[64,640]{1,0:T(8,128)(2,1)S(1)}, bf16[64,640]{1,0:T(8,128)(2,1)S(1)}, u32[]{:S(2)}, u32[]{:S(2)}) collective-permute-start(bf16[64,640]{1,0:T(8,128)(2,1)S(1)} %pad_maximum_fusion.5), channel_id=1, source_target_pairs={{0,24},{4,28},{8,16},{12,20},{16,8},{20,12},{24,0},{28,4},{1,25},{... | collective-permute-start | bytes 245768 | tf_op jit(solution)/shard_map/ppermute | solution.py:465
  39.0 4.3 %collective-permute-start.7 = (bf16[64,512]{1,0:T(8,128)(2,1)S(1)}, bf16[64,512]{1,0:T(8,128)(2,1)S(1)}, u32[]{:S(2)}, u32[]{:S(2)}) collective-permute-start(bf16[64,512]{1,0:T(8,128)(2,1)S(1)} %get-tuple-element.45), channel_id=1, source_target_pairs={{0,8},{4,12},{8,0},{12,4},{16,24},{20,28},{24,16},{28,20},{1,9},{5... | collective-permute-start | bytes 196616 | tf_op jit(solution)/shard_map/ppermute | solution.py:484
  39.6 4.3 %collective-permute-start.8 = (bf16[64,512]{1,0:T(8,128)(2,1)S(1)}, bf16[64,512]{1,0:T(8,128)(2,1)S(1)}, u32[]{:S(2)}, u32[]{:S(2)}) collective-permute-start(bf16[64,512]{1,0:T(8,128)(2,1)S(1)} %get-tuple-element.46), channel_id=1, source_target_pairs={{0,16},{4,20},{8,24},{12,28},{16,0},{20,4},{24,8},{28,12},{1,17},{... | collective-permute-start | bytes 196616 | tf_op jit(solution)/shard_map/ppermute | solution.py:484
  40.4 5.2 %collective-permute-start.9 = (bf16[64,512]{1,0:T(8,128)(2,1)S(1)}, bf16[64,512]{1,0:T(8,128)(2,1)S(1)}, u32[]{:S(2)}, u32[]{:S(2)}) collective-permute-start(bf16[64,512]{1,0:T(8,128)(2,1)S(1)} %get-tuple-element.47), channel_id=1, source_target_pairs={{0,24},{4,28},{8,16},{12,20},{16,8},{20,12},{24,0},{28,4},{1,25},{... | collective-permute-start | bytes 196616 | tf_op jit(solution)/shard_map/ppermute | solution.py:484
  45.6 1.4 %collective-permute-start.10 = (bf16[128,512]{1,0:T(8,128)(2,1)S(1)}, bf16[128,512]{1,0:T(8,128)(2,1)S(1)}, u32[]{:S(2)}, u32[]{:S(2)}) collective-permute-start(bf16[128,512]{1,0:T(8,128)(2,1)S(1)} %pad_maximum_fusion.1), channel_id=1, source_target_pairs={{0,4},{4,0},{8,12},{12,8},{16,20},{20,16},{24,28},{28,24},{1,5},{5... | collective-permute-start | bytes 393224 | tf_op jit(solution)/shard_map/ppermute | solution.py:489
  47.3 9.6 %collective-permute-start.13 = (bf16[128,512]{1,0:T(8,128)(2,1)S(1)}, bf16[128,512]{1,0:T(8,128)(2,1)S(1)}, u32[]{:S(2)}, u32[]{:S(2)}) collective-permute-start(bf16[128,512]{1,0:T(8,128)(2,1)S(1)} %collect.1.refs_0_), channel_id=1, source_target_pairs={{0,1},{1,0},{2,3},{3,2},{4,5},{5,4},{6,7},{7,6},{8,9},{9,8},{10,11... | collective-permute-start | bytes 393224 | tf_op jit(solution)/shard_map/ppermute | solution.py:504
  47.3 15.4 %collective-permute-start.12 = (bf16[128,512]{1,0:T(8,128)(2,1)S(1)}, bf16[128,512]{1,0:T(8,128)(2,1)S(1)}, u32[]{:S(2)}, u32[]{:S(2)}) collective-permute-start(bf16[128,512]{1,0:T(8,128)(2,1)S(1)} %collect.1.refs_0_), channel_id=1, source_target_pairs={{0,2},{1,3},{2,0},{3,1},{4,6},{5,7},{6,4},{7,5},{8,10},{9,11},{10,... | collective-permute-start | bytes 393224 | tf_op jit(solution)/shard_map/ppermute | solution.py:504
  50.4 12.4 %collective-permute-start.11 = (bf16[128,512]{1,0:T(8,128)(2,1)S(1)}, bf16[128,512]{1,0:T(8,128)(2,1)S(1)}, u32[]{:S(2)}, u32[]{:S(2)}) collective-permute-start(bf16[128,512]{1,0:T(8,128)(2,1)S(1)} %collect.1.refs_0_), channel_id=1, source_target_pairs={{0,3},{1,2},{2,1},{3,0},{4,7},{5,6},{6,5},{7,4},{8,11},{9,10},{10,... | collective-permute-start | bytes 393224 | tf_op jit(solution)/shard_map/ppermute | solution.py:504
  56.8 3.4 %copy-start.2 = (bf16[2048,2048]{1,0:T(8,128)(2,1)S(1)}, bf16[2048,2048]{1,0:T(8,128)(2,1)}, u32[]{:S(2)}) copy-start(bf16[2048,2048]{1,0:T(8,128)(2,1)} %refs_2_.3) | copy-start | bytes 25165828

commit v2 on v1

v2 whole, which is shorter than its diff:
```python
import functools
import math

import jax
import jax.numpy as jnp
from jax import lax
from jax.experimental import pallas as pl
from jax.experimental.pallas import tpu as pltpu
from jax.sharding import PartitionSpec as P

HD = 128
QPK = 4
TILE = 128
SCALE = 1.0 / math.sqrt(HD)
LOG2E = math.log2(math.e)
F32 = jnp.float32
BF16 = jnp.bfloat16
MIB = 1024 * 1024


def dot_nn(a, b):
    return lax.dot_general(a, b, (((1,), (0,)), ((), ())), preferred_element_type=F32)


def dot_nt(a, b):
    return lax.dot_general(a, b, (((1,), (1,)), ((), ())), preferred_element_type=F32)


def dot_tn(a, b):
    return lax.dot_general(a, b, (((0,), (0,)), ((), ())), preferred_element_type=F32)


def in_hbm(x):
    return pltpu.with_memory_space_constraint(x, pltpu.HBM)


def params(mib):
    return pltpu.CompilerParams(vmem_limit_bytes=mib * MIB)


def cost(flops, moved, exps=0):
    return pl.CostEstimate(flops=flops, bytes_accessed=moved, transcendentals=exps)


def project_kernel(rows_ref, weight_ref, *refs, turns, steps, held):
    count, refs = len(turns), refs[held:]
    outs, weights = refs[:count], refs[count : 2 * count]
    rows, rows_sem, weight_sems = refs[2 * count :]
    here, shares = lax.axis_index("tensor"), lax.axis_size("tensor")
    odd = lax.axis_index("group") & 1
    features, width = weights[0].shape
    depth = features // steps
    rows_copy = pltpu.make_async_copy(rows_ref, rows, rows_sem)
    rows_copy.start()
    copies = []
    for at, (even_turn, odd_turn) in enumerate(turns):
        turn = jnp.where(odd == 1, odd_turn, even_turn)
        first = pl.multiple_of(lax.rem(here + turn, shares) * width, width)
        for step in range(steps):
            part = pl.ds(step * depth, depth)
            copy = pltpu.make_async_copy(
                weight_ref.at[part, pl.ds(first, width)],
                weights[at].at[part],
                weight_sems.at[at, step],
            )
            copy.start()
            copies.append(copy)
    rows_copy.wait()
    for at, out in enumerate(outs):
        total = None
        for step in range(steps):
            copies[at * steps + step].wait()
            part = slice(step * depth, (step + 1) * depth)
            term = dot_nn(rows[:, part], weights[at][part, :])
            total = term if total is None else total + term
        out[...] = total.astype(out.dtype)


def project(rows, weight, after, width, turns, kinds):
    count, features = rows.shape
    steps = 4
    vmem, hbm = pl.BlockSpec(memory_space=pltpu.VMEM), pl.BlockSpec(memory_space=pltpu.HBM)
    found = pl.pallas_call(
        functools.partial(project_kernel, turns=turns, steps=steps, held=len(after)),
        out_shape=[jax.ShapeDtypeStruct((count, width), kind) for kind in kinds]
        + [jax.ShapeDtypeStruct((features, width), BF16) for _ in kinds],
        in_specs=[hbm, hbm] + [pl.BlockSpec(memory_space=pl.ANY)] * len(after),
        out_specs=[vmem] * (2 * len(kinds)),
        scratch_shapes=[
            pltpu.VMEM((count, features), BF16),
            pltpu.SemaphoreType.DMA,
            pltpu.SemaphoreType.DMA((len(kinds), steps)),
        ],
        compiler_params=params(16),
        cost_estimate=cost(
            2 * count * features * width * len(kinds), 2 * features * width * len(kinds)
        ),
        name="project",
    )(in_hbm(rows), in_hbm(weight), *after)
    return found[: len(kinds)], found[len(kinds) :]


FLIPS = ((2, 4), (4, 2), (6, 6), (0, 0))


def target_of(slot, capacity, across, flips):
    if across is None:
        return slot // capacity
    me = lax.axis_index("group") ^ across
    odd = me & 1
    target = jnp.zeros(slot.shape, jnp.int32)
    for at, (even_flip, odd_flip) in enumerate(flips):
        pack = me ^ jnp.where(odd == 1, odd_flip, even_flip)
        target = jnp.where(slot // capacity == at, pack, target)
    return target


def place_kernel(dest_ref, sample_ref, own_ref, *refs, capacity, plan):
    parts, outs = refs[: -len(plan)], refs[-len(plan) :]
    total = own_ref[...]
    for part in parts:
        total = total + part[...].astype(F32)
    tags = jnp.broadcast_to(sample_ref[...] + 1, (TILE, total.shape[0])).astype(F32).T
    wide = jnp.concatenate([total, tags], axis=1).astype(BF16)
    rows = total.shape[0]
    for out, across in zip(outs, plan, strict=True):
        slots = out.shape[0]
        slot = lax.broadcasted_iota(jnp.int32, (slots, rows), 0)
        row = lax.broadcasted_iota(jnp.int32, (slots, rows), 1)
        target = target_of(slot, capacity, across, FLIPS)
        select = (dest_ref[...] == target) & (slot % capacity == row % capacity)
        out[...] = dot_nn(select.astype(F32).astype(BF16), wide).astype(BF16)


def place(dest_row, sample_row, own, parts, capacity, slots, plan):
    rows, width = own.shape
    vmem = pl.BlockSpec(memory_space=pltpu.VMEM)
    return pl.pallas_call(
        functools.partial(place_kernel, capacity=capacity, plan=plan),
        out_shape=[jax.ShapeDtypeStruct((slots, width + TILE), BF16) for _ in plan],
        in_specs=[vmem] * (3 + len(parts)),
        out_specs=[vmem] * len(plan),
        compiler_params=params(8),
        cost_estimate=cost(2 * 256 * rows * width, 4 * rows * width),
        name="place",
    )(dest_row, sample_row, own, *parts)


def collect_kernel(dest_ref, *refs, capacity, plan):
    parts, out = refs[:-1], refs[-1]
    rows = out.shape[0]
    total = jnp.zeros(out.shape, F32)
    for part, across in zip(parts, plan, strict=True):
        slots = part.shape[0]
        slot = lax.broadcasted_iota(jnp.int32, (rows, slots), 1)
        row = lax.broadcasted_iota(jnp.int32, (rows, slots), 0)
        target = target_of(slot, capacity, across, FLIPS[::-1])
        dest = jnp.broadcast_to(dest_ref[...], (slots, rows)).astype(F32).T
        select = (dest == target.astype(F32)) & (slot % capacity == row % capacity)
        total = total + dot_nn(select.astype(F32).astype(BF16), part[...])
    out[...] = total.astype(BF16)


def collect(dest_row, parts, capacity, plan):
    rows, width = dest_row.shape[1], parts[0].shape[1]
    vmem = pl.BlockSpec(memory_space=pltpu.VMEM)
    return pl.pallas_call(
        functools.partial(collect_kernel, capacity=capacity, plan=plan),
        out_shape=jax.ShapeDtypeStruct((rows, width), BF16),
        in_specs=[vmem] * (1 + len(parts)),
        out_specs=vmem,
        compiler_params=params(8),
        cost_estimate=cost(2 * 256 * rows * width, 4 * rows * width),
        name="collect",
    )(dest_row, *parts)


def stacked(ref, tile, head):
    first = head * QPK * HD
    return jnp.concatenate(
        [
            ref[tile * TILE : (tile + 1) * TILE, first + j * HD : first + (j + 1) * HD]
            for j in range(QPK)
        ],
        axis=0,
    )


def text_span(tile):
    return max(0, tile - 1) * TILE, (tile + 1) * TILE


def text_mask(segment_ref, tile):
    low, high = text_span(tile)
    span = high - low
    own = segment_ref[:, tile * TILE : (tile + 1) * TILE].astype(F32)
    keys = jnp.concatenate(
        [
            jnp.broadcast_to(segment_ref[:, at : at + TILE].astype(F32), (TILE, TILE)).T
            for at in range(low, high, TILE)
        ],
        axis=0,
    )
    key_place = lax.broadcasted_iota(jnp.int32, (span, TILE), 0) + low
    token_place = lax.broadcasted_iota(jnp.int32, (span, TILE), 1) + tile * TILE
    mask = (keys == own) & (key_place <= token_place)
    return jnp.where(mask, 0.0, -jnp.inf)


def slot_mask(tags, segment_ref, tile):
    own = segment_ref[:, tile * TILE : (tile + 1) * TILE].astype(F32) + 1.0
    return jnp.where(tags.astype(F32) == own, 0.0, -jnp.inf)


def repeated(mask):
    return jnp.concatenate([mask] * QPK, axis=1)


def text_stats_kernel(query_ref, grad_ref, kv_ref, segment_ref, top_ref, sum_ref, inner_ref):
    tiles, heads = query_ref.shape[0] // TILE, kv_ref.shape[1] // (2 * HD)
    for tile in range(tiles):
        low, high = text_span(tile)
        mask = repeated(text_mask(segment_ref, tile))
        for head in range(heads):
            at = head * tiles + tile
            keys = kv_ref[low:high, head * 2 * HD : head * 2 * HD + HD]
            values = kv_ref[low:high, head * 2 * HD + HD : (head + 1) * 2 * HD]
            scores = dot_nt(keys, stacked(query_ref, tile, head)) + mask
            top = jnp.max(scores, axis=0, keepdims=True)
            expo = jnp.exp2((scores - top) * (SCALE * LOG2E))
            dprobs = dot_nt(values, stacked(grad_ref, tile, head))
            top_ref[at : at + 1, :] = top
            sum_ref[at : at + 1, :] = jnp.sum(expo, axis=0, keepdims=True)
            inner_ref[at : at + 1, :] = jnp.sum(expo * dprobs, axis=0, keepdims=True)


def text_stats(queries, out_grad, text_kv, segment):
    tiles, heads = queries.shape[0] // TILE, text_kv.shape[1] // (2 * HD)
    vmem = pl.BlockSpec(memory_space=pltpu.VMEM)
    shape = jax.ShapeDtypeStruct((tiles * heads, QPK * TILE), F32)
    pairs = heads * QPK * (2 * tiles - 1) * TILE * TILE
    return pl.pallas_call(
        text_stats_kernel,
        out_shape=[shape] * 3,
        in_specs=[vmem] * 4,
        out_specs=[vmem] * 3,
        compiler_params=params(24),
        cost_estimate=cost(4 * pairs * HD, 4 * queries.size, pairs),
        name="text_stats",
    )(queries, out_grad, text_kv, segment)


def slot_grad_kernel(
    query_ref, grad_ref, segment_ref, top_ref, sum_ref, inner_ref, *refs, arrivals
):
    visual, refs = refs[:arrivals], refs[arrivals:]
    outs, (all_top_ref, scale_ref, all_inner_ref) = refs[:arrivals], refs[arrivals:]
    tiles = query_ref.shape[0] // TILE
    width = visual[0].shape[1] - TILE
    heads = width // (2 * HD)
    tags = jnp.concatenate([one[:, width:] for one in visual], axis=0)
    masks = [slot_mask(tags, segment_ref, tile) for tile in range(tiles)]
    for head in range(heads):
        first = head * 2 * HD
        keys = jnp.concatenate([one[:, first : first + HD] for one in visual], axis=0)
        values = jnp.concatenate([one[:, first + HD : first + 2 * HD] for one in visual], axis=0)
        key_grad = jnp.zeros((keys.shape[0], HD), F32)
        value_grad = jnp.zeros((keys.shape[0], HD), F32)
        for tile in range(tiles):
            at = head * tiles + tile
            query, grad = stacked(query_ref, tile, head), stacked(grad_ref, tile, head)
            scores = dot_nt(keys, query) + repeated(masks[tile])
            dprobs = dot_nt(values, grad)
            text_top = top_ref[at : at + 1, :]
            top = jnp.maximum(text_top, jnp.max(scores, axis=0, keepdims=True))
            expo = jnp.exp2((scores - top) * (SCALE * LOG2E))
            shift = jnp.exp2((text_top - top) * (SCALE * LOG2E))
            total = sum_ref[at : at + 1, :] * shift + jnp.sum(expo, axis=0, keepdims=True)
            inverse = 1.0 / total
            inner = (
                inner_ref[at : at + 1, :] * shift + jnp.sum(expo * dprobs, axis=0, keepdims=True)
            ) * inverse
            probs = expo * inverse
            dscores = (probs * (dprobs - inner)).astype(BF16)
            value_grad = value_grad + dot_nn(probs.astype(BF16), grad)
            key_grad = key_grad + dot_nn(dscores, query)
            all_top_ref[at : at + 1, :] = top
            scale_ref[at : at + 1, :] = inverse
            all_inner_ref[at : at + 1, :] = inner
        for at, out in enumerate(outs[::-1]):
            rows = slice(at * out.shape[0], (at + 1) * out.shape[0])
            out[:, first : first + HD] = (key_grad[rows] * SCALE).astype(BF16)
            out[:, first + HD : first + 2 * HD] = value_grad[rows].astype(BF16)


def slot_grad(queries, out_grad, segment, stats, visual):
    vmem = pl.BlockSpec(memory_space=pltpu.VMEM)
    shape = jax.ShapeDtypeStruct(stats[0].shape, F32)
    slots = sum(one.shape[0] for one in visual)
    pairs = slots * queries.shape[0] * queries.shape[1] // HD
    found = pl.pallas_call(
        functools.partial(slot_grad_kernel, arrivals=len(visual)),
        out_shape=[
            jax.ShapeDtypeStruct((one.shape[0], one.shape[1] - TILE), BF16) for one in visual
        ]
        + [shape] * 3,
        in_specs=[vmem] * (6 + len(visual)),
        out_specs=[vmem] * (3 + len(visual)),
        compiler_params=params(24),
        cost_estimate=cost(8 * pairs * HD, 4 * queries.size, pairs),
        name="slot_grad",
    )(queries, out_grad, segment, *stats, *visual)
    return found[: len(visual)][::-1], found[len(visual) :]


def text_grad_kernel(
    query_ref,
    grad_ref,
    kv_ref,
    segment_ref,
    top_ref,
    scale_ref,
    inner_ref,
    *refs,
    arrivals,
    head,
    held,
):
    visual, refs = refs[:arrivals], refs[arrivals + held :]
    outs, (attended_all, query_grad_all, kv_grad_all, sems) = refs[:3], refs[3:]
    tiles, width = query_ref.shape[0] // TILE, kv_ref.shape[1]
    first = head * 2 * HD
    tags = jnp.concatenate([one[:, width:] for one in visual], axis=0)
    slot_keys = jnp.concatenate([one[:, first : first + HD] for one in visual], axis=0)
    slot_values = jnp.concatenate([one[:, first + HD : first + 2 * HD] for one in visual], axis=0)
    key_held = value_held = None
    copies = []

    def send(which, held, rows, start):
        copy = pltpu.make_async_copy(
            held.at[rows],
            outs[which].at[rows, start : start + held.shape[1]],
            sems.at[len(copies)],
        )
        copy.start()
        copies.append(copy)

    for tile in range(tiles):
        at = head * tiles + tile
        low, high = text_span(tile)
        mask = repeated(
            jnp.concatenate(
                [text_mask(segment_ref, tile), slot_mask(tags, segment_ref, tile)], axis=0
            )
        )
        keys = jnp.concatenate([kv_ref[low:high, first : first + HD], slot_keys], axis=0)
        values = jnp.concatenate(
            [kv_ref[low:high, first + HD : first + 2 * HD], slot_values], axis=0
        )
        query, grad = stacked(query_ref, tile, head), stacked(grad_ref, tile, head)
        scores = dot_nt(keys, query) + mask
        expo = jnp.exp2((scores - top_ref[at : at + 1, :]) * (SCALE * LOG2E))
        probs = expo * scale_ref[at : at + 1, :]
        dprobs = dot_nt(values, grad)
        dscores = (probs * (dprobs - inner_ref[at : at + 1, :])).astype(BF16)
        weights = probs.astype(BF16)
        attended = dot_tn(values, weights)
        query_grad = dot_tn(keys, dscores) * SCALE
        rows = slice(tile * TILE, (tile + 1) * TILE)
        for j in range(QPK):
            lanes = slice(j * TILE, (j + 1) * TILE)
            columns = slice(j * HD, (j + 1) * HD)
            attended_all[rows, columns] = attended[:, lanes].T.astype(BF16)
            query_grad_all[rows, columns] = query_grad[:, lanes].T.astype(BF16)
        send(0, attended_all, rows, head * QPK * HD)
        send(1, query_grad_all, rows, head * QPK * HD)
        key_part = dot_nn(dscores[: high - low], query)
        value_part = dot_nn(weights[: high - low], grad)
        if tile > 0:
            before = slice((tile - 1) * TILE, tile * TILE)
            kv_grad_all[before, :HD] = ((key_held + key_part[:TILE]) * SCALE).astype(BF16)
            kv_grad_all[before, HD:] = (value_held + value_part[:TILE]).astype(BF16)
            send(2, kv_grad_all, before, first)
        key_held, value_held = key_part[high - low - TILE :], value_part[high - low - TILE :]
    last = slice((tiles - 1) * TILE, tiles * TILE)
    kv_grad_all[last, :HD] = (key_held * SCALE).astype(BF16)
    kv_grad_all[last, HD:] = value_held.astype(BF16)
    send(2, kv_grad_all, last, first)
    for copy in copies:
        copy.wait()


def text_grad(queries, out_grad, text_kv, segment, stats, visual, head, before):
    vmem, hbm = pl.BlockSpec(memory_space=pltpu.VMEM), pl.BlockSpec(memory_space=pltpu.HBM)
    length = queries.shape[0]
    slots = sum(one.shape[0] for one in visual)
    pairs = (slots + 2 * TILE) * length * QPK
    first = 7 + len(visual)
    return pl.pallas_call(
        functools.partial(
            text_grad_kernel, arrivals=len(visual), head=head, held=len(before)
        ),
        out_shape=[
            jax.ShapeDtypeStruct(queries.shape, BF16),
            jax.ShapeDtypeStruct(queries.shape, BF16),
            jax.ShapeDtypeStruct(text_kv.shape, BF16),
        ],
        in_specs=[vmem] * first + [hbm] * len(before),
        out_specs=[hbm] * 3,
        scratch_shapes=[
            pltpu.VMEM((length, QPK * HD), BF16),
            pltpu.VMEM((length, QPK * HD), BF16),
            pltpu.VMEM((length, 2 * HD), BF16),
            pltpu.SemaphoreType.DMA((3 * length // TILE,)),
        ],
        input_output_aliases={first + i: i for i in range(len(before))},
        compiler_params=params(24),
        cost_estimate=cost(12 * pairs * HD, 8 * queries.size, pairs),
        name="text_grad",
    )(queries, out_grad, text_kv, segment, *stats, *visual, *before)


def near_kernel(*refs, count):
    total = None
    for part, weight in zip(refs[:count], refs[count : 2 * count], strict=True):
        term = dot_nt(part[...], weight[...])
        total = term if total is None else total + term
    refs[-1][...] = total


def near_grad(parts, weights):
    rows, (features, width) = parts[0].shape[0], weights[0].shape
    vmem = pl.BlockSpec(memory_space=pltpu.VMEM)
    return pl.pallas_call(
        functools.partial(near_kernel, count=len(parts)),
        out_shape=jax.ShapeDtypeStruct((rows, features), F32),
        in_specs=[vmem] * (2 * len(parts)),
        out_specs=vmem,
        compiler_params=params(16),
        cost_estimate=cost(
            2 * rows * width * features * len(parts), 2 * width * features * len(parts)
        ),
        name="near_grad",
    )(*parts, *weights)


def far_kernel(part_ref, weight_ref, before_ref, out_ref):
    out_ref[...] = before_ref[...] + dot_nt(part_ref[...], weight_ref[...])


def far_grad(part, weight, before):
    rows, width = part.shape
    features = weight.shape[0]
    vmem = pl.BlockSpec(memory_space=pltpu.VMEM)
    return pl.pallas_call(
        far_kernel,
        out_shape=jax.ShapeDtypeStruct((rows, features), F32),
        in_specs=[vmem] * 3,
        out_specs=vmem,
        compiler_params=params(16),
        cost_estimate=cost(2 * rows * width * features, 2 * width * features),
        name="far_grad",
    )(part, weight, before)


def last_kernel(part_ref, weight_ref, before_ref, out_ref, rounded, sems):
    steps = sems.shape[0]
    count = out_ref.shape[1] // steps
    copies = []
    for step in range(steps):
        columns = slice(step * count, (step + 1) * count)
        term = dot_nt(part_ref[...], weight_ref[columns, :])
        rounded[:, columns] = (before_ref[:, columns] + term).astype(BF16)
        copies.append(
            pltpu.make_async_copy(
                rounded.at[:, columns], out_ref.at[:, columns], sems.at[step]
            )
        )
        copies[-1].start()
    for copy in copies:
        copy.wait()


def last_grad(part, weight, before):
    rows, width = part.shape
    features = weight.shape[0]
    vmem, hbm = pl.BlockSpec(memory_space=pltpu.VMEM), pl.BlockSpec(memory_space=pltpu.HBM)
    return pl.pallas_call(
        last_kernel,
        out_shape=jax.ShapeDtypeStruct((rows, features), BF16),
        in_specs=[vmem] * 3,
        out_specs=hbm,
        scratch_shapes=[pltpu.VMEM((rows, features), BF16), pltpu.SemaphoreType.DMA((4,))],
        compiler_params=params(16),
        cost_estimate=cost(2 * rows * width * features, 2 * width * features),
        name="last_grad",
    )(part, weight, before)


def turned(groups, shares, turns, sign):
    return [
        (g * shares + t, g * shares + (t + sign * turns[g % 2]) % shares)
        for g in range(groups)
        for t in range(shares)
    ]


def on_device(
    queries, text_kv, out_grad, text_segment, visual_rows, kv_weight, visual_dest, visual_sample
):
    groups, shares = lax.axis_size("group"), lax.axis_size("tensor")
    rows = visual_rows.shape[0]
    capacity = 2 * rows // groups
    width = kv_weight.shape[1] // shares
    dest_row = visual_dest.reshape(1, rows)
    sample_row = visual_sample.reshape(1, rows)

    around = list(range(1, shares))
    turns = list(zip(around, around[1:] + around[:1], strict=True))
    axes = ("group", "tensor")
    landed, columns = [], []
    for batch in (turns[: shares // 2], turns[shares // 2 :]):
        blocks, weights = project(visual_rows, kv_weight, (), width, batch, [BF16] * len(batch))
        landed += [
            lax.ppermute(block, axes, turned(groups, shares, turn, 1))
            for block, turn in zip(blocks, batch, strict=True)
        ]
        columns += weights
    (own,), (own_columns,) = project(
        visual_rows, kv_weight, blocks[-1:], width, [(0, 0)], [F32]
    )
    stats = text_stats(queries, out_grad, text_kv, text_segment)

    pairwise = groups == 8
    if pairwise:
        ways = [
            [(g, g ^ (odd_flip if g % 2 else even_flip)) for g in range(groups)]
            for even_flip, odd_flip in FLIPS
        ]
        neighbour = [(g, g ^ 1) for g in range(groups)]
        plan = [0, 1]
        mine, across = place(
            dest_row, sample_row, own, landed, capacity, len(FLIPS) * capacity, plan
        )
        theirs = lax.ppermute(across, "group", neighbour)
        pairs = [
            jnp.concatenate(
                [mine[j * capacity : (j + 1) * capacity], theirs[j * capacity : (j + 1) * capacity]],
                axis=0,
            )
            for j in range(len(FLIPS))
        ]
        visual = [lax.ppermute(pair, "group", way) for pair, way in zip(pairs[:-1], ways[:-1])]
        visual.append(pairs[-1])
    else:
        plan = [None]
        (sent,) = place(
            dest_row, sample_row, own, landed, capacity, groups * capacity, plan
        )
        visual = [
            lax.all_to_all(
                sent.reshape(groups, capacity, -1), "group", split_axis=0, concat_axis=0, tiled=True
            ).reshape(groups * capacity, -1)
        ]

    grads, final = slot_grad(queries, out_grad, text_segment, stats, visual)
    inputs = (queries, out_grad, text_kv, text_segment, final, visual)
    text_outs = text_grad(*inputs, 0, ())

    if pairwise:
        back = [lax.ppermute(grad, "group", way) for grad, way in zip(grads[:-1], ways[:-1])]
        back = [grads[-1]] + back[::-1]
        *back, kept = lax.optimization_barrier((*back, text_outs[2]))
        text_outs = (*text_outs[:2], kept)
        kept = jnp.concatenate([one[:capacity] for one in back], axis=0)
        passed = jnp.concatenate([one[capacity:] for one in back], axis=0)
        returned = [kept, lax.ppermute(passed, "group", neighbour)]
    else:
        returned = [
            lax.all_to_all(
                grads[0].reshape(groups, capacity, -1),
                "group",
                split_axis=0,
                concat_axis=0,
                tiled=True,
            ).reshape(groups * capacity, -1)
        ]
    kv_grad = collect(dest_row, returned, capacity, plan)

    for head in range(1, text_kv.shape[1] // (2 * HD)):
        text_outs = text_grad(*inputs, head, text_outs)
    attended, query_grad, text_kv_grad = text_outs

    gathered = [
        lax.ppermute(kv_grad, axes, turned(groups, shares, turn, -1)) for turn in turns
    ]
    total = near_grad([kv_grad, gathered[0]], [own_columns, columns[0]])
    for part, weight in zip(gathered[2:], columns[2:], strict=True):
        total = far_grad(part, weight, total)
    total = last_grad(gathered[1], columns[1], total)
    return (attended, query_grad, text_kv_grad, total)


def solution(mesh):
    placed = (
        P("group", "tensor"),
        P("group", "tensor"),
        P("group", "tensor"),
        P("group", None),
        P("group", "tensor"),
        P("tensor", None),
        P("group", None),
        P("group"),
    )
    return jax.shard_map(
        on_device,
        mesh=mesh,
        in_specs=placed,
        out_specs=(
            P("group", "tensor"),
            P("group", "tensor"),
            P("group", "tensor"),
            P("group", "tensor"),
        ),
        check_vma=False,
    )
```

time: 66.4 us -> 57.2 us (0.86)
  local copies, waits for them, and re-layouts: 8.27 us -> 0.09 us
  starting transfers between devices: 17.6 us -> 19.8 us
  Pallas kernels: 22.5 us -> 21.1 us
  waiting for transfers between devices: 16.2 us -> 14.9 us
    unnamed x23 -> x12, local copies, waits for them, and re-layouts: 7.96 us -> 0.04 us
    ppermute x14, starting transfers between devices: 17.6 us -> 19.8 us  [the longest x3 7.07 us: on_device(): lax.ppermute(block, axes, turned(groups, shares, turn, 1))]
    pallas_call x7 -> x10, Pallas kernels: 18 us -> 16.6 us  [the longest x3 6.6 us: project(): pl.pallas_call(functools.partial(project_kernel, turns=turns, steps=steps...]
    ppermute x14, waiting for transfers between devices: 16.2 us -> 14.9 us  [the longest x3 5.02 us: on_device(): lax.ppermute(kv_grad, axes, turned(groups, shares, turn, -1))]
  transfers between devices with their start and end apart: 14 -> 14, of which waited for: 10 -> 12; matrix products, arithmetic and copies ran while one was open for 1% -> 0% of each run, Pallas kernels for 18% -> 23%
where the time goes in v2:
time: 57.2 us; the launch traced here: 57 us
  Pallas kernels  21.1 us (37%)
  starting transfers between devices  19.8 us (35%)
  waiting for transfers between devices  14.9 us (26%)
  between operations  1.05 us (2%)
    ppermute x3, starting transfers between devices, on_device(): lax.ppermute(block, axes, turned(groups, shares, turn, 1))  7.07 us
    pallas_call x3, Pallas kernels, project(): pl.pallas_call(functools.partial(project_kernel, turns=turns, steps=steps...  6.6 us
    pallas_call x2, Pallas kernels, text_grad(): pl.pallas_call(functools.partial(text_grad_kernel, arrivals=len(visual),...  5.63 us
    ppermute x3, starting transfers between devices, on_device(): lax.ppermute(kv_grad, axes, turned(groups, shares, turn, -1))  5.37 us
    ppermute x3, waiting for transfers between devices, on_device(): lax.ppermute(kv_grad, axes, turned(groups, shares, turn, -1))  5.02 us
    ppermute x3, waiting for transfers between devices, on_device(): lax.ppermute(pair, 'group', way)  3.91 us
    ppermute x3, starting transfers between devices, on_device(): lax.ppermute(pair, 'group', way)  3.68 us
    ppermute x3, starting transfers between devices, on_device(): lax.ppermute(grad, 'group', way)  3.55 us
  transfers between devices with their start and end apart: 14, of which 12 were waited for; matrix products, arithmetic and copies ran while one was open for 0% of the time, Pallas kernels for 23%

profile of v2, /device:TPU:0, one launch (start us, length us, event | category | flops | bytes accessed | tf_op | source)
XLA Modules:
  0.0 57.0 jit_solution(5775756938185522386)
XLA Ops:
  0.6 2.7 %project.5 = (bf16[128,512]{1,0:T(8,128)(2,1)S(1)}, bf16[128,512]{1,0:T(8,128)(2,1)S(1)}, bf16[2048,512]{1,0:T(8,128)(2,1)S(1)}, bf16[2048,512]{1,0:T(8,128)(2,1)S(1)}) custom-call(bf16[128,2048]{1,0:T(8,128)(2,1)} %rows_ref.5, bf16[2048,2048]{1,0:T(8,128)(2,1)} %weight_ref.5), custom_call_target="tpu_custom_call" | custom-call | flops 536870912 | bytes 4194304 | tf_op jit(solution)/shard_map/project/pallas_call | solution.py:83
  3.3 3.1 %collective-permute-start = (bf16[128,512]{1,0:T(8,128)(2,1)S(1)}, bf16[128,512]{1,0:T(8,128)(2,1)S(1)}, u32[]{:S(2)}, u32[]{:S(2)}) collective-permute-start(bf16[128,512]{1,0:T(8,128)(2,1)S(1)} %get-tuple-element.40), channel_id=1, source_target_pairs={{0,1},{1,2},{2,3},{3,0},{4,6},{5,7},{6,4},{7,5},{8,9},{9,10},{10,1... | collective-permute-start | bytes 393224 | tf_op jit(solution)/shard_map/ppermute | solution.py:525
  6.4 2.6 %collective-permute-start.1 = (bf16[128,512]{1,0:T(8,128)(2,1)S(1)}, bf16[128,512]{1,0:T(8,128)(2,1)S(1)}, u32[]{:S(2)}, u32[]{:S(2)}) collective-permute-start(bf16[128,512]{1,0:T(8,128)(2,1)S(1)} %get-tuple-element.41), channel_id=1, source_target_pairs={{0,2},{1,3},{2,0},{3,1},{4,7},{5,4},{6,5},{7,6},{8,10},{9,11},{10,... | collective-permute-start | bytes 393224 | tf_op jit(solution)/shard_map/ppermute | solution.py:525
  9.0 2.0 %project.3 = (bf16[128,512]{1,0:T(8,128)(2,1)S(1)}, bf16[2048,512]{1,0:T(8,128)(2,1)S(1)}) custom-call(bf16[128,2048]{1,0:T(8,128)(2,1)} %rows_ref.5, bf16[2048,2048]{1,0:T(8,128)(2,1)} %weight_ref.5), custom_call_target="tpu_custom_call" | custom-call | flops 268435456 | bytes 2097152 | tf_op jit(solution)/shard_map/project/pallas_call | solution.py:83
  11.0 1.4 %collective-permute-start.2 = (bf16[128,512]{1,0:T(8,128)(2,1)S(1)}, bf16[128,512]{1,0:T(8,128)(2,1)S(1)}, u32[]{:S(2)}, u32[]{:S(2)}) collective-permute-start(bf16[128,512]{1,0:T(8,128)(2,1)S(1)} %get-tuple-element.38.refs_0_), channel_id=1, source_target_pairs={{0,3},{1,0},{2,1},{3,2},{4,5},{5,6},{6,7},{7,4},{8,11},{9,8},{10,9... | collective-permute-start | bytes 393224 | tf_op jit(solution)/shard_map/ppermute | solution.py:525
  12.4 2.0 %project.4 = (f32[128,512]{1,0:T(8,128)S(1)}, bf16[2048,512]{1,0:T(8,128)(2,1)S(1)}) custom-call(bf16[128,2048]{1,0:T(8,128)(2,1)} %rows_ref.5, bf16[2048,2048]{1,0:T(8,128)(2,1)} %weight_ref.5, bf16[128,512]{1,0:T(8,128)(2,1)S(1)} %get-tuple-element.38.refs_0_), custom_call_target="tpu_custom_call" | custom-call | flops 268435456 | bytes 2097152 | tf_op jit(solution)/shard_map/project/pallas_call | solution.py:83
  14.4 1.2 %text_stats.1 = (f32[6,512]{1,0:T(8,128)S(1)}, f32[6,512]{1,0:T(8,128)S(1)}, f32[6,512]{1,0:T(8,128)S(1)}) custom-call(bf16[384,1024]{1,0:T(8,128)(2,1)S(1)} %copy-done, bf16[384,1024]{1,0:T(8,128)(2,1)S(1)} %copy-done.1, bf16[384,512]{1,0:T(8,128)(2,1)S(1)} %copy-done.2, s32[1,384]{1,0:T(1,128)S(1)} %copy-done.4), custom_call_target="tpu_custom_call" | custom-call | flops 335544320 | bytes 1572864 | tf_op jit(solution)/shard_map/text_stats/pallas_call | solution.py:242
  15.6 2.1 %collective-permute-done.1.refs_1_ = bf16[128,512]{1,0:T(8,128)(2,1)S(1)} collective-permute-done((bf16[128,512]{1,0:T(8,128)(2,1)S(1)}, bf16[128,512]{1,0:T(8,128)(2,1)S(1)}, u32[]{:S(2)}, u32[]{:S(2)}) %collective-permute-start.1) | collective-permute-done | bytes 131104 | tf_op jit(solution)/shard_map/ppermute | solution.py:525
  17.7 0.4 collective-permute-done.2.refs_2_
  18.2 0.3 place.1
  18.6 1.4 %collective-permute-done.3 = bf16[128,640]{1,0:T(8,128)(2,1)S(1)} collective-permute-done((bf16[128,640]{1,0:T(8,128)(2,1)S(1)}, bf16[128,640]{1,0:T(8,128)(2,1)S(1)}, u32[]{:S(2)}, u32[]{:S(2)}) %collective-permute-start.3) | collective-permute-done | bytes 163872 | tf_op jit(solution)/shard_map/ppermute | solution.py:545
  20.0 2.5 %collective-permute-start.6 = (bf16[64,640]{1,0:T(8,128)(2,1)S(1)}, bf16[64,640]{1,0:T(8,128)(2,1)S(1)}, u32[]{:S(2)}, u32[]{:S(2)}) collective-permute-start(bf16[64,640]{1,0:T(8,128)(2,1)S(1)} %pad_maximum_fusion.4), channel_id=1, source_target_pairs={{0,24},{4,28},{8,16},{12,20},{16,8},{20,12},{24,0},{28,4},{1,25},{... | collective-permute-start | bytes 245768 | tf_op jit(solution)/shard_map/ppermute | solution.py:553
  22.5 0.6 %collective-permute-start.5 = (bf16[64,640]{1,0:T(8,128)(2,1)S(1)}, bf16[64,640]{1,0:T(8,128)(2,1)S(1)}, u32[]{:S(2)}, u32[]{:S(2)}) collective-permute-start(bf16[64,640]{1,0:T(8,128)(2,1)S(1)} %pad_maximum_fusion.3), channel_id=1, source_target_pairs={{0,16},{4,12},{8,24},{12,4},{16,0},{20,28},{24,8},{28,20},{1,17},{... | collective-permute-start | bytes 245768 | tf_op jit(solution)/shard_map/ppermute | solution.py:553
  23.1 0.6 %collective-permute-start.4 = (bf16[64,640]{1,0:T(8,128)(2,1)S(1)}, bf16[64,640]{1,0:T(8,128)(2,1)S(1)}, u32[]{:S(2)}, u32[]{:S(2)}) collective-permute-start(bf16[64,640]{1,0:T(8,128)(2,1)S(1)} %pad_maximum_fusion.2), channel_id=1, source_target_pairs={{0,8},{4,20},{8,0},{12,28},{16,24},{20,4},{24,16},{28,12},{1,9},{5... | collective-permute-start | bytes 245768 | tf_op jit(solution)/shard_map/ppermute | solution.py:553
  23.7 2.3 %collective-permute-done.6.refs_2_ = bf16[64,640]{1,0:T(8,128)(2,1)S(1)} collective-permute-done((bf16[64,640]{1,0:T(8,128)(2,1)S(1)}, bf16[64,640]{1,0:T(8,128)(2,1)S(1)}, u32[]{:S(2)}, u32[]{:S(2)}) %collective-permute-start.6) | collective-permute-done | bytes 81952 | tf_op jit(solution)/shard_map/ppermute | solution.py:553
  25.9 1.5 %collective-permute-done.5.refs_1_ = bf16[64,640]{1,0:T(8,128)(2,1)S(1)} collective-permute-done((bf16[64,640]{1,0:T(8,128)(2,1)S(1)}, bf16[64,640]{1,0:T(8,128)(2,1)S(1)}, u32[]{:S(2)}, u32[]{:S(2)}) %collective-permute-start.5) | collective-permute-done | bytes 81952 | tf_op jit(solution)/shard_map/ppermute | solution.py:553
  27.6 3.4 %slot_grad.1 = (bf16[64,512]{1,0:T(8,128)(2,1)S(1)}, bf16[64,512]{1,0:T(8,128)(2,1)S(1)}, bf16[64,512]{1,0:T(8,128)(2,1)S(1)}, bf16[64,512]{1,0:T(8,128)(2,1)S(1...) custom-call(bf16[384,1024]{1,0:T(8,128)(2,1)S(1)} %copy-done, ...), custom_call_target="tpu_custom_call" | custom-call | flops 805306368 | bytes 1572864 | tf_op jit(solution)/shard_map/slot_grad/pallas_call | solution.py:301
  31.0 2.1 %collective-permute-start.7 = (bf16[64,512]{1,0:T(8,128)(2,1)S(1)}, bf16[64,512]{1,0:T(8,128)(2,1)S(1)}, u32[]{:S(2)}, u32[]{:S(2)}) collective-permute-start(bf16[64,512]{1,0:T(8,128)(2,1)S(1)} %get-tuple-element.50), channel_id=1, source_target_pairs={{0,24},{4,28},{8,16},{12,20},{16,8},{20,12},{24,0},{28,4},{1,25},{... | collective-permute-start | bytes 196616 | tf_op jit(solution)/shard_map/ppermute | solution.py:571
  33.1 0.7 %collective-permute-start.8 = (bf16[64,512]{1,0:T(8,128)(2,1)S(1)}, bf16[64,512]{1,0:T(8,128)(2,1)S(1)}, u32[]{:S(2)}, u32[]{:S(2)}) collective-permute-start(bf16[64,512]{1,0:T(8,128)(2,1)S(1)} %get-tuple-element.51), channel_id=1, source_target_pairs={{0,16},{4,12},{8,24},{12,4},{16,0},{20,28},{24,8},{28,20},{1,17},{... | collective-permute-start | bytes 196616 | tf_op jit(solution)/shard_map/ppermute | solution.py:571
  33.8 0.8 %collective-permute-start.9 = (bf16[64,512]{1,0:T(8,128)(2,1)S(1)}, bf16[64,512]{1,0:T(8,128)(2,1)S(1)}, u32[]{:S(2)}, u32[]{:S(2)}) collective-permute-start(bf16[64,512]{1,0:T(8,128)(2,1)S(1)} %get-tuple-element.52), channel_id=1, source_target_pairs={{0,8},{4,20},{8,0},{12,28},{16,24},{20,4},{24,16},{28,12},{1,9},{5... | collective-permute-start | bytes 196616 | tf_op jit(solution)/shard_map/ppermute | solution.py:571
  34.6 2.8 %text_grad.2 = (bf16[384,1024]{1,0:T(8,128)(2,1)}, bf16[384,1024]{1,0:T(8,128)(2,1)}, bf16[384,512]{1,0:T(8,128)(2,1)}) custom-call(bf16[384,1024]{1,0:T(8,128)(2,1)S(1)} %copy-done, bf16[384,1024]{1,0:T(8,128)(2,1)S(1)} %copy-done.1, bf16[384,512]{1,0:T(8,128)(2,1)S(1)} %copy-done.2, s32[1,384]{1,0:T(1,128)S(1)} %copy-done.4, ...), custom_call_target="tpu_custom_call" | custom-call | flops 1207959552 | bytes 3145728 | tf_op jit(solution)/shard_map/text_grad/pallas_call | solution.py:399
  37.6 0.4 collective-permute-done.9
  38.2 1.3 %collective-permute-done.10.refs_1_ = bf16[128,512]{1,0:T(8,128)(2,1)S(1)} collective-permute-done((bf16[128,512]{1,0:T(8,128)(2,1)S(1)}, bf16[128,512]{1,0:T(8,128)(2,1)S(1)}, u32[]{:S(2)}, u32[]{:S(2)}) %collective-permute-start.10) | collective-permute-done | bytes 131104 | tf_op jit(solution)/shard_map/ppermute | solution.py:577
  39.8 4.7 %collective-permute-start.13 = (bf16[128,512]{1,0:T(8,128)(2,1)S(1)}, bf16[128,512]{1,0:T(8,128)(2,1)S(1)}, u32[]{:S(2)}, u32[]{:S(2)}) collective-permute-start(bf16[128,512]{1,0:T(8,128)(2,1)S(1)} %collect.1.refs_0_), channel_id=1, source_target_pairs={{0,3},{1,0},{2,1},{3,2},{4,6},{5,7},{6,4},{7,5},{8,11},{9,8},{10,9... | collective-permute-start | bytes 393224 | tf_op jit(solution)/shard_map/ppermute | solution.py:595
  44.5 0.7 %collective-permute-start.11 = (bf16[128,512]{1,0:T(8,128)(2,1)S(1)}, bf16[128,512]{1,0:T(8,128)(2,1)S(1)}, u32[]{:S(2)}, u32[]{:S(2)}) collective-permute-start(bf16[128,512]{1,0:T(8,128)(2,1)S(1)} %collect.1.refs_0_), channel_id=1, source_target_pairs={{0,2},{1,3},{2,0},{3,1},{4,5},{5,6},{6,7},{7,4},{8,10},{9,11},{10,... | collective-permute-start | bytes 393224 | tf_op jit(solution)/shard_map/ppermute | solution.py:595
  45.2 2.8 %text_grad.3 = (bf16[384,1024]{1,0:T(8,128)(2,1)}, bf16[384,1024]{1,0:T(8,128)(2,1)}, bf16[384,512]{1,0:T(8,128)(2,1)}) custom-call(bf16[384,1024]{1,0:T(8,128)(2,1)S(1)} %copy-done, bf16[384,1024]{1,0:T(8,128)(2,1)S(1)} %copy-done.1, bf16[384,512]{1,0:T(8,128)(2,1)S(1)} %copy-done.2, ...), custom_call_target="tpu_custom_call", output_to_operand_aliasing={{0}: (11, {}), {1}: (12, {}), {2}: (13, {})} | custom-call | flops 1207959552 | bytes 3145728 | tf_op jit(solution)/shard_map/text_grad/pallas_call | solution.py:399
  48.0 0.4 collective-permute-done.13.refs_1_
  48.4 1.5 %near_grad.1.before_ref = f32[128,2048]{1,0:T(8,128)S(1)} custom-call(bf16[128,512]{1,0:T(8,128)(2,1)S(1)} %collect.1.refs_0_, bf16[128,512]{1,0:T(8,128)(2,1)S(1)} %collective-permute-done.13.refs_1_, bf16[2048,512]{1,0:T(8,128)(2,1)S(1)} %get-tuple-element.64.refs_2_, bf16[2048,512]{1,0:T(8,128)(2,1)S(1)} %get-tuple-element.65.refs_3_), custom_call_target="tpu_custom_call" | custom-call | flops 536870912 | bytes 4194304 | tf_op jit(solution)/shard_map/near_grad/pallas_call | solution.py:434
  49.8 2.8 %collective-permute-done.12.part_ref = bf16[128,512]{1,0:T(8,128)(2,1)S(1)} collective-permute-done((bf16[128,512]{1,0:T(8,128)(2,1)S(1)}, bf16[128,512]{1,0:T(8,128)(2,1)S(1)}, u32[]{:S(2)}, u32[]{:S(2)}) %collective-permute-start.12) | collective-permute-done | bytes 131104 | tf_op jit(solution)/shard_map/ppermute | solution.py:595
  52.6 0.8 %far_grad.1.before_ref = f32[128,2048]{1,0:T(8,128)S(1)} custom-call(bf16[128,512]{1,0:T(8,128)(2,1)S(1)} %collective-permute-done.12.part_ref, bf16[2048,512]{1,0:T(8,128)(2,1)S(1)} %get-tuple-element.63.weight_ref, f32[128,2048]{1,0:T(8,128)S(1)} %near_grad.1.before_ref), custom_call_target="tpu_custom_call" | custom-call | flops 268435456 | bytes 2097152 | tf_op jit(solution)/shard_map/far_grad/pallas_call | solution.py:455
  53.5 1.9 %collective-permute-done.11.part_ref = bf16[128,512]{1,0:T(8,128)(2,1)S(1)} collective-permute-done((bf16[128,512]{1,0:T(8,128)(2,1)S(1)}, bf16[128,512]{1,0:T(8,128)(2,1)S(1)}, u32[]{:S(2)}, u32[]{:S(2)}) %collective-permute-start.11) | collective-permute-done | bytes 131104 | tf_op jit(solution)/shard_map/ppermute | solution.py:595
  55.3 1.5 %last_grad.1 = bf16[128,2048]{1,0:T(8,128)(2,1)} custom-call(bf16[128,512]{1,0:T(8,128)(2,1)S(1)} %collective-permute-done.11.part_ref, bf16[2048,512]{1,0:T(8,128)(2,1)S(1)} %get-tuple-element.62.weight_ref, f32[128,2048]{1,0:T(8,128)S(1)} %far_grad.1.before_ref), custom_call_target="tpu_custom_call" | custom-call | flops 268435456 | bytes 2097152 | tf_op jit(solution)/shard_map/last_grad/pallas_call | solution.py:488
  (30 shorter events, 1.0 us)
Async XLA Ops:
  3.3 12.3 %collective-permute-start = (bf16[128,512]{1,0:T(8,128)(2,1)S(1)}, bf16[128,512]{1,0:T(8,128)(2,1)S(1)}, u32[]{:S(2)}, u32[]{:S(2)}) collective-permute-start(bf16[128,512]{1,0:T(8,128)(2,1)S(1)} %get-tuple-element.40), channel_id=1, source_target_pairs={{0,1},{1,2},{2,3},{3,0},{4,6},{5,7},{6,4},{7,5},{8,9},{9,10},{10,1... | collective-permute-start | bytes 393224 | tf_op jit(solution)/shard_map/ppermute | solution.py:525
  6.4 11.4 %collective-permute-start.1 = (bf16[128,512]{1,0:T(8,128)(2,1)S(1)}, bf16[128,512]{1,0:T(8,128)(2,1)S(1)}, u32[]{:S(2)}, u32[]{:S(2)}) collective-permute-start(bf16[128,512]{1,0:T(8,128)(2,1)S(1)} %get-tuple-element.41), channel_id=1, source_target_pairs={{0,2},{1,3},{2,0},{3,1},{4,7},{5,4},{6,5},{7,6},{8,10},{9,11},{10,... | collective-permute-start | bytes 393224 | tf_op jit(solution)/shard_map/ppermute | solution.py:525
  10.9 3.4 %copy-start = (bf16[384,1024]{1,0:T(8,128)(2,1)S(1)}, bf16[384,1024]{1,0:T(8,128)(2,1)}, u32[]{:S(2)}) copy-start(bf16[384,1024]{1,0:T(8,128)(2,1)} %query_ref.7) | copy-start | bytes 2359300
  11.0 3.4 %copy-start.1 = (bf16[384,1024]{1,0:T(8,128)(2,1)S(1)}, bf16[384,1024]{1,0:T(8,128)(2,1)}, u32[]{:S(2)}) copy-start(bf16[384,1024]{1,0:T(8,128)(2,1)} %grad_ref.7) | copy-start | bytes 2359300
  11.0 3.4 %copy-start.2 = (bf16[384,512]{1,0:T(8,128)(2,1)S(1)}, bf16[384,512]{1,0:T(8,128)(2,1)}, u32[]{:S(2)}) copy-start(bf16[384,512]{1,0:T(8,128)(2,1)} %kv_ref.5) | copy-start | bytes 1179652
  11.0 3.4 %copy-start.4 = (s32[1,384]{1,0:T(1,128)S(1)}, s32[1,384]{1,0:T(1,128)}, u32[]{:S(2)}) copy-start(s32[1,384]{1,0:T(1,128)} %segment_ref.7) | copy-start | bytes 4612
  11.0 7.2 %copy-start.3 = (s32[128,1]{0,1:T(1,128)S(1)}, s32[128,1]{0,1:T(1,128)}, u32[]{:S(2)}) copy-start(s32[128,1]{0,1:T(1,128)} %param.14) | copy-start | bytes 1540
  11.0 7.2 %copy-start.5 = (s32[128]{0:T(128)S(1)}, s32[128]{0:T(128)}, u32[]{:S(2)}) copy-start(s32[128]{0:T(128)} %param.15) | copy-start | bytes 1540
  11.0 7.2 %collective-permute-start.2 = (bf16[128,512]{1,0:T(8,128)(2,1)S(1)}, bf16[128,512]{1,0:T(8,128)(2,1)S(1)}, u32[]{:S(2)}, u32[]{:S(2)}) collective-permute-start(bf16[128,512]{1,0:T(8,128)(2,1)S(1)} %get-tuple-element.38.refs_0_), channel_id=1, source_target_pairs={{0,3},{1,0},{2,1},{3,2},{4,5},{5,6},{6,7},{7,4},{8,11},{9,8},{10,9... | collective-permute-start | bytes 393224 | tf_op jit(solution)/shard_map/ppermute | solution.py:525
  18.5 1.5 %collective-permute-start.3 = (bf16[128,640]{1,0:T(8,128)(2,1)S(1)}, bf16[128,640]{1,0:T(8,128)(2,1)S(1)}, u32[]{:S(2)}, u32[]{:S(2)}) collective-permute-start(bf16[128,640]{1,0:T(8,128)(2,1)S(1)} %get-tuple-element.43), channel_id=1, source_target_pairs={{0,4},{4,0},{8,12},{12,8},{16,20},{20,16},{24,28},{28,24},{1,5},{5... | collective-permute-start | bytes 491528 | tf_op jit(solution)/shard_map/ppermute | solution.py:545
  20.0 6.0 %collective-permute-start.6 = (bf16[64,640]{1,0:T(8,128)(2,1)S(1)}, bf16[64,640]{1,0:T(8,128)(2,1)S(1)}, u32[]{:S(2)}, u32[]{:S(2)}) collective-permute-start(bf16[64,640]{1,0:T(8,128)(2,1)S(1)} %pad_maximum_fusion.4), channel_id=1, source_target_pairs={{0,24},{4,28},{8,16},{12,20},{16,8},{20,12},{24,0},{28,4},{1,25},{... | collective-permute-start | bytes 245768 | tf_op jit(solution)/shard_map/ppermute | solution.py:553
  22.5 4.9 %collective-permute-start.5 = (bf16[64,640]{1,0:T(8,128)(2,1)S(1)}, bf16[64,640]{1,0:T(8,128)(2,1)S(1)}, u32[]{:S(2)}, u32[]{:S(2)}) collective-permute-start(bf16[64,640]{1,0:T(8,128)(2,1)S(1)} %pad_maximum_fusion.3), channel_id=1, source_target_pairs={{0,16},{4,12},{8,24},{12,4},{16,0},{20,28},{24,8},{28,20},{1,17},{... | collective-permute-start | bytes 245768 | tf_op jit(solution)/shard_map/ppermute | solution.py:553
  23.1 4.5 %collective-permute-start.4 = (bf16[64,640]{1,0:T(8,128)(2,1)S(1)}, bf16[64,640]{1,0:T(8,128)(2,1)S(1)}, u32[]{:S(2)}, u32[]{:S(2)}) collective-permute-start(bf16[64,640]{1,0:T(8,128)(2,1)S(1)} %pad_maximum_fusion.2), channel_id=1, source_target_pairs={{0,8},{4,20},{8,0},{12,28},{16,24},{20,4},{24,16},{28,12},{1,9},{5... | collective-permute-start | bytes 245768 | tf_op jit(solution)/shard_map/ppermute | solution.py:553
  31.0 6.4 %collective-permute-start.7 = (bf16[64,512]{1,0:T(8,128)(2,1)S(1)}, bf16[64,512]{1,0:T(8,128)(2,1)S(1)}, u32[]{:S(2)}, u32[]{:S(2)}) collective-permute-start(bf16[64,512]{1,0:T(8,128)(2,1)S(1)} %get-tuple-element.50), channel_id=1, source_target_pairs={{0,24},{4,28},{8,16},{12,20},{16,8},{20,12},{24,0},{28,4},{1,25},{... | collective-permute-start | bytes 196616 | tf_op jit(solution)/shard_map/ppermute | solution.py:571
  33.1 4.5 %collective-permute-start.8 = (bf16[64,512]{1,0:T(8,128)(2,1)S(1)}, bf16[64,512]{1,0:T(8,128)(2,1)S(1)}, u32[]{:S(2)}, u32[]{:S(2)}) collective-permute-start(bf16[64,512]{1,0:T(8,128)(2,1)S(1)} %get-tuple-element.51), channel_id=1, source_target_pairs={{0,16},{4,12},{8,24},{12,4},{16,0},{20,28},{24,8},{28,20},{1,17},{... | collective-permute-start | bytes 196616 | tf_op jit(solution)/shard_map/ppermute | solution.py:571
  33.8 4.3 %collective-permute-start.9 = (bf16[64,512]{1,0:T(8,128)(2,1)S(1)}, bf16[64,512]{1,0:T(8,128)(2,1)S(1)}, u32[]{:S(2)}, u32[]{:S(2)}) collective-permute-start(bf16[64,512]{1,0:T(8,128)(2,1)S(1)} %get-tuple-element.52), channel_id=1, source_target_pairs={{0,8},{4,20},{8,0},{12,28},{16,24},{20,4},{24,16},{28,12},{1,9},{5... | collective-permute-start | bytes 196616 | tf_op jit(solution)/shard_map/ppermute | solution.py:571
  38.1 1.4 %collective-permute-start.10 = (bf16[128,512]{1,0:T(8,128)(2,1)S(1)}, bf16[128,512]{1,0:T(8,128)(2,1)S(1)}, u32[]{:S(2)}, u32[]{:S(2)}) collective-permute-start(bf16[128,512]{1,0:T(8,128)(2,1)S(1)} %pad_maximum_fusion.1), channel_id=1, source_target_pairs={{0,4},{4,0},{8,12},{12,8},{16,20},{20,16},{24,28},{28,24},{1,5},{5... | collective-permute-start | bytes 393224 | tf_op jit(solution)/shard_map/ppermute | solution.py:577
  39.8 8.6 %collective-permute-start.13 = (bf16[128,512]{1,0:T(8,128)(2,1)S(1)}, bf16[128,512]{1,0:T(8,128)(2,1)S(1)}, u32[]{:S(2)}, u32[]{:S(2)}) collective-permute-start(bf16[128,512]{1,0:T(8,128)(2,1)S(1)} %collect.1.refs_0_), channel_id=1, source_target_pairs={{0,3},{1,0},{2,1},{3,2},{4,6},{5,7},{6,4},{7,5},{8,11},{9,8},{10,9... | collective-permute-start | bytes 393224 | tf_op jit(solution)/shard_map/ppermute | solution.py:595
  44.5 8.1 %collective-permute-start.12 = (bf16[128,512]{1,0:T(8,128)(2,1)S(1)}, bf16[128,512]{1,0:T(8,128)(2,1)S(1)}, u32[]{:S(2)}, u32[]{:S(2)}) collective-permute-start(bf16[128,512]{1,0:T(8,128)(2,1)S(1)} %collect.1.refs_0_), channel_id=1, source_target_pairs={{0,1},{1,2},{2,3},{3,0},{4,7},{5,4},{6,5},{7,6},{8,9},{9,10},{10,1... | collective-permute-start | bytes 393224 | tf_op jit(solution)/shard_map/ppermute | solution.py:595
  44.5 10.8 %collective-permute-start.11 = (bf16[128,512]{1,0:T(8,128)(2,1)S(1)}, bf16[128,512]{1,0:T(8,128)(2,1)S(1)}, u32[]{:S(2)}, u32[]{:S(2)}) collective-permute-start(bf16[128,512]{1,0:T(8,128)(2,1)S(1)} %collect.1.refs_0_), channel_id=1, source_target_pairs={{0,2},{1,3},{2,0},{3,1},{4,5},{5,6},{6,7},{7,4},{8,10},{9,11},{10,... | collective-permute-start | bytes 393224 | tf_op jit(solution)/shard_map/ppermute | solution.py:595

commit v3 on v2

v3 whole, which is shorter than its diff:
```python
import functools
import math

import jax
import jax.numpy as jnp
from jax import lax
from jax.experimental import pallas as pl
from jax.experimental.pallas import tpu as pltpu
from jax.sharding import PartitionSpec as P

HD = 128
QPK = 4
TILE = 128
SCALE = 1.0 / math.sqrt(HD)
LOG2E = math.log2(math.e)
F32 = jnp.float32
BF16 = jnp.bfloat16
MIB = 1024 * 1024


def dot_nn(a, b):
    return lax.dot_general(a, b, (((1,), (0,)), ((), ())), preferred_element_type=F32)


def dot_nt(a, b):
    return lax.dot_general(a, b, (((1,), (1,)), ((), ())), preferred_element_type=F32)


def dot_tn(a, b):
    return lax.dot_general(a, b, (((0,), (0,)), ((), ())), preferred_element_type=F32)


def in_hbm(x):
    return pltpu.with_memory_space_constraint(x, pltpu.HBM)


def params(mib):
    return pltpu.CompilerParams(vmem_limit_bytes=mib * MIB)


def cost(flops, moved, exps=0):
    return pl.CostEstimate(flops=flops, bytes_accessed=moved, transcendentals=exps)


def project_kernel(rows_ref, weight_ref, *refs, flips, steps, held):
    count, refs = len(flips), refs[held:]
    outs, weights = refs[:count], refs[count : 2 * count]
    rows, rows_sem, weight_sems = refs[2 * count :]
    here = lax.axis_index("tensor")
    features, width = weights[0].shape
    depth = features // steps
    rows_copy = pltpu.make_async_copy(rows_ref, rows, rows_sem)
    rows_copy.start()
    copies = []
    for at, flip in enumerate(flips):
        first = pl.multiple_of((here ^ flip) * width, width)
        for step in range(steps):
            part = pl.ds(step * depth, depth)
            copy = pltpu.make_async_copy(
                weight_ref.at[part, pl.ds(first, width)],
                weights[at].at[part],
                weight_sems.at[at, step],
            )
            copy.start()
            copies.append(copy)
    rows_copy.wait()
    for at, out in enumerate(outs):
        total = None
        for step in range(steps):
            copies[at * steps + step].wait()
            part = slice(step * depth, (step + 1) * depth)
            term = dot_nn(rows[:, part], weights[at][part, :])
            total = term if total is None else total + term
        out[...] = total.astype(out.dtype)


def project(rows, weight, after, width, flips, kinds):
    count, features = rows.shape
    steps = 4
    vmem, hbm = pl.BlockSpec(memory_space=pltpu.VMEM), pl.BlockSpec(memory_space=pltpu.HBM)
    found = pl.pallas_call(
        functools.partial(project_kernel, flips=flips, steps=steps, held=len(after)),
        out_shape=[jax.ShapeDtypeStruct((count, width), kind) for kind in kinds]
        + [jax.ShapeDtypeStruct((features, width), BF16) for _ in kinds],
        in_specs=[hbm, hbm] + [pl.BlockSpec(memory_space=pl.ANY)] * len(after),
        out_specs=[vmem] * (2 * len(kinds)),
        scratch_shapes=[
            pltpu.VMEM((count, features), BF16),
            pltpu.SemaphoreType.DMA,
            pltpu.SemaphoreType.DMA((len(kinds), steps)),
        ],
        compiler_params=params(16),
        cost_estimate=cost(
            2 * count * features * width * len(kinds), 2 * features * width * len(kinds)
        ),
        name="project",
    )(in_hbm(rows), in_hbm(weight), *after)
    return found[: len(kinds)], found[len(kinds) :]


FLIPS = ((6, 6), (4, 2), (2, 4), (0, 0))
BACK = (0, 2, 1)


def target_of(slot, capacity, flips):
    if flips is None:
        return slot // capacity
    me = lax.axis_index("group")
    odd = me & 1
    chip = jnp.zeros(slot.shape, jnp.int32)
    for at, (even_flip, odd_flip) in enumerate(flips):
        pack = me ^ jnp.where(odd == 1, odd_flip, even_flip)
        chip = jnp.where(slot // (2 * capacity) == at, pack, chip)
    return chip ^ ((slot // capacity) & 1)


def place_kernel(dest_ref, sample_ref, own_ref, *refs, capacity, flips, count):
    parts, outs = refs[:-count], refs[-count:]
    total = own_ref[...]
    for part in parts:
        total = total + part[...].astype(F32)
    rows = total.shape[0]
    tags = jnp.broadcast_to(sample_ref[...] + 1, (TILE, rows)).astype(F32).T
    wide = jnp.concatenate([total, tags], axis=1).astype(BF16)
    each = outs[0].shape[0]
    slot = lax.broadcasted_iota(jnp.int32, (each * count, rows), 0)
    row = lax.broadcasted_iota(jnp.int32, (each * count, rows), 1)
    target = target_of(slot, capacity, flips)
    select = (dest_ref[...] == target) & (slot % capacity == row % capacity)
    placed = dot_nn(select.astype(F32).astype(BF16), wide).astype(BF16)
    for at, out in enumerate(outs):
        out[...] = placed[at * each : (at + 1) * each]


def place(dest_row, sample_row, own, parts, capacity, slots, flips):
    rows, width = own.shape
    count = len(flips) if flips else 1
    vmem = pl.BlockSpec(memory_space=pltpu.VMEM)
    return pl.pallas_call(
        functools.partial(place_kernel, capacity=capacity, flips=flips, count=count),
        out_shape=[jax.ShapeDtypeStruct((slots // count, width + TILE), BF16)] * count,
        in_specs=[vmem] * (3 + len(parts)),
        out_specs=[vmem] * count,
        compiler_params=params(8),
        cost_estimate=cost(2 * slots * rows * width, 4 * rows * width),
        name="place",
    )(dest_row, sample_row, own, *parts)


def collect_kernel(dest_ref, *refs, capacity, flips):
    parts, out = refs[:-1], refs[-1]
    rows = out.shape[0]
    grads = jnp.concatenate([part[...] for part in parts], axis=0)
    slots = grads.shape[0]
    slot = lax.broadcasted_iota(jnp.int32, (rows, slots), 1)
    row = lax.broadcasted_iota(jnp.int32, (rows, slots), 0)
    target = target_of(slot, capacity, flips)
    dest = jnp.broadcast_to(dest_ref[...], (slots, rows)).astype(F32).T
    select = (dest == target.astype(F32)) & (slot % capacity == row % capacity)
    out[...] = dot_nn(select.astype(F32).astype(BF16), grads).astype(BF16)


def collect(dest_row, parts, capacity, flips):
    rows, width = dest_row.shape[1], parts[0].shape[1]
    vmem = pl.BlockSpec(memory_space=pltpu.VMEM)
    return pl.pallas_call(
        functools.partial(collect_kernel, capacity=capacity, flips=flips),
        out_shape=jax.ShapeDtypeStruct((rows, width), BF16),
        in_specs=[vmem] * (1 + len(parts)),
        out_specs=vmem,
        compiler_params=params(8),
        cost_estimate=cost(2 * 256 * rows * width, 4 * rows * width),
        name="collect",
    )(dest_row, *parts)


def stacked(ref, tile, head):
    first = head * QPK * HD
    return jnp.concatenate(
        [
            ref[tile * TILE : (tile + 1) * TILE, first + j * HD : first + (j + 1) * HD]
            for j in range(QPK)
        ],
        axis=0,
    )


def text_span(tile):
    return max(0, tile - 1) * TILE, (tile + 1) * TILE


def text_mask(segment_ref, tile):
    low, high = text_span(tile)
    span = high - low
    own = segment_ref[:, tile * TILE : (tile + 1) * TILE].astype(F32)
    keys = jnp.concatenate(
        [
            jnp.broadcast_to(segment_ref[:, at : at + TILE].astype(F32), (TILE, TILE)).T
            for at in range(low, high, TILE)
        ],
        axis=0,
    )
    key_place = lax.broadcasted_iota(jnp.int32, (span, TILE), 0) + low
    token_place = lax.broadcasted_iota(jnp.int32, (span, TILE), 1) + tile * TILE
    mask = (keys == own) & (key_place <= token_place)
    return jnp.where(mask, 0.0, -jnp.inf)


def slot_mask(tags, segment_ref, tile):
    own = segment_ref[:, tile * TILE : (tile + 1) * TILE].astype(F32) + 1.0
    return jnp.where(tags.astype(F32) == own, 0.0, -jnp.inf)


def repeated(mask):
    return jnp.concatenate([mask] * QPK, axis=1)


def text_stats_kernel(query_ref, grad_ref, kv_ref, segment_ref, top_ref, sum_ref, inner_ref):
    tiles, heads = query_ref.shape[0] // TILE, kv_ref.shape[1] // (2 * HD)
    for tile in range(tiles):
        low, high = text_span(tile)
        mask = repeated(text_mask(segment_ref, tile))
        for head in range(heads):
            at = head * tiles + tile
            keys = kv_ref[low:high, head * 2 * HD : head * 2 * HD + HD]
            values = kv_ref[low:high, head * 2 * HD + HD : (head + 1) * 2 * HD]
            scores = dot_nt(keys, stacked(query_ref, tile, head)) + mask
            top = jnp.max(scores, axis=0, keepdims=True)
            expo = jnp.exp2((scores - top) * (SCALE * LOG2E))
            dprobs = dot_nt(values, stacked(grad_ref, tile, head))
            top_ref[at : at + 1, :] = top
            sum_ref[at : at + 1, :] = jnp.sum(expo, axis=0, keepdims=True)
            inner_ref[at : at + 1, :] = jnp.sum(expo * dprobs, axis=0, keepdims=True)


def text_stats(queries, out_grad, text_kv, segment):
    tiles, heads = queries.shape[0] // TILE, text_kv.shape[1] // (2 * HD)
    vmem = pl.BlockSpec(memory_space=pltpu.VMEM)
    shape = jax.ShapeDtypeStruct((tiles * heads, QPK * TILE), F32)
    pairs = heads * QPK * (2 * tiles - 1) * TILE * TILE
    return pl.pallas_call(
        text_stats_kernel,
        out_shape=[shape] * 3,
        in_specs=[vmem] * 4,
        out_specs=[vmem] * 3,
        compiler_params=params(24),
        cost_estimate=cost(4 * pairs * HD, 4 * queries.size, pairs),
        name="text_stats",
    )(queries, out_grad, text_kv, segment)


def slot_tiles(query_ref, grad_ref, segment_ref, slots_ref):
    tiles = query_ref.shape[0] // TILE
    width = slots_ref.shape[1] - TILE
    masks = [
        repeated(slot_mask(slots_ref[:, width:], segment_ref, tile)) for tile in range(tiles)
    ]
    for head in range(width // (2 * HD)):
        first = head * 2 * HD
        keys = slots_ref[:, first : first + HD]
        values = slots_ref[:, first + HD : first + 2 * HD]
        for tile in range(tiles):
            query, grad = stacked(query_ref, tile, head), stacked(grad_ref, tile, head)
            scores = dot_nt(keys, query) + masks[tile]
            yield head, tile, head * tiles + tile, query, grad, scores, dot_nt(values, grad)


def joined(scores, dprobs, top_ref, sum_ref, inner_ref, at):
    before = top_ref[at : at + 1, :]
    top = jnp.maximum(before, jnp.max(scores, axis=0, keepdims=True))
    expo = jnp.exp2((scores - top) * (SCALE * LOG2E))
    shift = jnp.exp2((before - top) * (SCALE * LOG2E))
    total = sum_ref[at : at + 1, :] * shift + jnp.sum(expo, axis=0, keepdims=True)
    inner = inner_ref[at : at + 1, :] * shift + jnp.sum(expo * dprobs, axis=0, keepdims=True)
    return expo, top, total, inner


def slot_stats_kernel(
    query_ref, grad_ref, segment_ref, slots_ref, top_ref, sum_ref, inner_ref, *outs
):
    for _, _, at, _, _, scores, dprobs in slot_tiles(query_ref, grad_ref, segment_ref, slots_ref):
        found = joined(scores, dprobs, top_ref, sum_ref, inner_ref, at)
        for out, row in zip(outs, found[1:], strict=True):
            out[at : at + 1, :] = row


def slot_grad_kernel(
    query_ref, grad_ref, segment_ref, slots_ref, top_ref, sum_ref, inner_ref, out_ref, *outs
):
    tiles, slots = query_ref.shape[0] // TILE, slots_ref.shape[0]
    for head, tile, at, query, grad, scores, dprobs in slot_tiles(
        query_ref, grad_ref, segment_ref, slots_ref
    ):
        if outs:
            expo, top, total, inner = joined(scores, dprobs, top_ref, sum_ref, inner_ref, at)
            inverse = 1.0 / total
            inner = inner * inverse
            for out, row in zip(outs, (top, inverse, inner), strict=True):
                out[at : at + 1, :] = row
        else:
            expo = jnp.exp2((scores - top_ref[at : at + 1, :]) * (SCALE * LOG2E))
            inverse, inner = sum_ref[at : at + 1, :], inner_ref[at : at + 1, :]
        probs = expo * inverse
        dscores = (probs * (dprobs - inner)).astype(BF16)
        value_part = dot_nn(probs.astype(BF16), grad)
        key_part = dot_nn(dscores, query)
        value_grad = value_part if tile == 0 else value_grad + value_part
        key_grad = key_part if tile == 0 else key_grad + key_part
        if tile == tiles - 1:
            first = head * 2 * HD
            out_ref[:, first : first + HD] = (key_grad * SCALE).astype(BF16)
            out_ref[:, first + HD : first + 2 * HD] = value_grad.astype(BF16)


def slot_call(kernel, queries, out_grad, segment, slots, stats, grads, joins, name):
    vmem = pl.BlockSpec(memory_space=pltpu.VMEM)
    pairs = slots.shape[0] * queries.shape[0] * queries.shape[1] // HD
    shapes = []
    if grads:
        shapes.append(jax.ShapeDtypeStruct((slots.shape[0], slots.shape[1] - TILE), BF16))
    if joins:
        shapes += [jax.ShapeDtypeStruct(stats[0].shape, F32)] * 3
    return pl.pallas_call(
        kernel,
        out_shape=shapes,
        in_specs=[vmem] * 7,
        out_specs=[vmem] * len(shapes),
        compiler_params=params(24),
        cost_estimate=cost((8 if grads else 4) * pairs * HD, 4 * queries.size, pairs),
        name=name,
    )(queries, out_grad, segment, slots, *stats)


def text_grad_kernel(
    query_ref,
    grad_ref,
    kv_ref,
    segment_ref,
    top_ref,
    scale_ref,
    inner_ref,
    *refs,
    arrivals,
    head,
    held,
):
    visual, refs = refs[:arrivals], refs[arrivals + held :]
    outs, (attended_all, query_grad_all, kv_grad_all, sems) = refs[:3], refs[3:]
    tiles, width = query_ref.shape[0] // TILE, kv_ref.shape[1]
    first = head * 2 * HD
    tags = jnp.concatenate([one[:, width:] for one in visual], axis=0)
    slot_keys = jnp.concatenate([one[:, first : first + HD] for one in visual], axis=0)
    slot_values = jnp.concatenate([one[:, first + HD : first + 2 * HD] for one in visual], axis=0)
    key_held = value_held = None
    copies = []

    def send(which, held, rows, start):
        copy = pltpu.make_async_copy(
            held.at[rows],
            outs[which].at[rows, start : start + held.shape[1]],
            sems.at[len(copies)],
        )
        copy.start()
        copies.append(copy)

    for tile in range(tiles):
        at = head * tiles + tile
        low, high = text_span(tile)
        mask = repeated(
            jnp.concatenate(
                [text_mask(segment_ref, tile), slot_mask(tags, segment_ref, tile)], axis=0
            )
        )
        keys = jnp.concatenate([kv_ref[low:high, first : first + HD], slot_keys], axis=0)
        values = jnp.concatenate(
            [kv_ref[low:high, first + HD : first + 2 * HD], slot_values], axis=0
        )
        query, grad = stacked(query_ref, tile, head), stacked(grad_ref, tile, head)
        scores = dot_nt(keys, query) + mask
        expo = jnp.exp2((scores - top_ref[at : at + 1, :]) * (SCALE * LOG2E))
        probs = expo * scale_ref[at : at + 1, :]
        dprobs = dot_nt(values, grad)
        dscores = (probs * (dprobs - inner_ref[at : at + 1, :])).astype(BF16)
        weights = probs.astype(BF16)
        attended = dot_tn(values, weights)
        query_grad = dot_tn(keys, dscores) * SCALE
        rows = slice(tile * TILE, (tile + 1) * TILE)
        for j in range(QPK):
            lanes = slice(j * TILE, (j + 1) * TILE)
            columns = slice(j * HD, (j + 1) * HD)
            attended_all[rows, columns] = attended[:, lanes].T.astype(BF16)
            query_grad_all[rows, columns] = query_grad[:, lanes].T.astype(BF16)
        send(0, attended_all, rows, head * QPK * HD)
        send(1, query_grad_all, rows, head * QPK * HD)
        key_part = dot_nn(dscores[: high - low], query)
        value_part = dot_nn(weights[: high - low], grad)
        if tile > 0:
            before = slice((tile - 1) * TILE, tile * TILE)
            kv_grad_all[before, :HD] = ((key_held + key_part[:TILE]) * SCALE).astype(BF16)
            kv_grad_all[before, HD:] = (value_held + value_part[:TILE]).astype(BF16)
            send(2, kv_grad_all, before, first)
        key_held, value_held = key_part[high - low - TILE :], value_part[high - low - TILE :]
    last = slice((tiles - 1) * TILE, tiles * TILE)
    kv_grad_all[last, :HD] = (key_held * SCALE).astype(BF16)
    kv_grad_all[last, HD:] = value_held.astype(BF16)
    send(2, kv_grad_all, last, first)
    for copy in copies:
        copy.wait()


def text_grad(queries, out_grad, text_kv, segment, stats, visual, head, before):
    vmem, hbm = pl.BlockSpec(memory_space=pltpu.VMEM), pl.BlockSpec(memory_space=pltpu.HBM)
    length = queries.shape[0]
    slots = sum(one.shape[0] for one in visual)
    pairs = (slots + 2 * TILE) * length * QPK
    first = 7 + len(visual)
    return pl.pallas_call(
        functools.partial(
            text_grad_kernel, arrivals=len(visual), head=head, held=len(before)
        ),
        out_shape=[
            jax.ShapeDtypeStruct(queries.shape, BF16),
            jax.ShapeDtypeStruct(queries.shape, BF16),
            jax.ShapeDtypeStruct(text_kv.shape, BF16),
        ],
        in_specs=[vmem] * first + [hbm] * len(before),
        out_specs=[hbm] * 3,
        scratch_shapes=[
            pltpu.VMEM((length, QPK * HD), BF16),
            pltpu.VMEM((length, QPK * HD), BF16),
            pltpu.VMEM((length, 2 * HD), BF16),
            pltpu.SemaphoreType.DMA((3 * length // TILE,)),
        ],
        input_output_aliases={first + i: i for i in range(len(before))},
        compiler_params=params(24),
        cost_estimate=cost(12 * pairs * HD, 8 * queries.size, pairs),
        name="text_grad",
    )(queries, out_grad, text_kv, segment, *stats, *visual, *before)


def by_core(weights, body):
    if len(weights) == 1:
        body(weights[0])
    else:
        odd = lax.axis_index("group") & 1
        for parity, weight in enumerate(weights):
            pl.when(odd == parity)(functools.partial(body, weight))


def near_kernel(own_ref, own_weight, part_ref, *refs):
    *weights, out_ref = refs

    def body(weight):
        out_ref[...] = dot_nt(own_ref[...], own_weight[...]) + dot_nt(part_ref[...], weight[...])

    by_core(weights, body)


def far_kernel(before_ref, part_ref, *refs):
    *weights, out_ref = refs

    def body(weight):
        out_ref[...] = before_ref[...] + dot_nt(part_ref[...], weight[...])

    by_core(weights, body)


def feature_grad(kernel, operands, name):
    rows, width = operands[0].shape[0], operands[-1].shape[1]
    features = operands[-1].shape[0]
    vmem = pl.BlockSpec(memory_space=pltpu.VMEM)
    return pl.pallas_call(
        kernel,
        out_shape=jax.ShapeDtypeStruct((rows, features), F32),
        in_specs=[vmem] * len(operands),
        out_specs=vmem,
        compiler_params=params(16),
        cost_estimate=cost(4 * rows * width * features, 4 * width * features),
        name=name,
    )(*operands)


def last_kernel(before_ref, part_ref, *refs):
    *weights, out_ref, rounded, sems = refs
    steps = sems.shape[0]
    count = out_ref.shape[1] // steps

    def copy(step):
        columns = slice(step * count, (step + 1) * count)
        return pltpu.make_async_copy(
            rounded.at[:, columns], out_ref.at[:, columns], sems.at[step]
        )

    def body(weight):
        for step in range(steps):
            columns = slice(step * count, (step + 1) * count)
            term = dot_nt(part_ref[...], weight[columns, :])
            rounded[:, columns] = (before_ref[:, columns] + term).astype(BF16)
            copy(step).start()

    by_core(weights, body)
    for step in range(steps):
        copy(step).wait()


def last_grad(before, part, weights):
    rows, width = part.shape
    features = weights[0].shape[0]
    vmem, hbm = pl.BlockSpec(memory_space=pltpu.VMEM), pl.BlockSpec(memory_space=pltpu.HBM)
    return pl.pallas_call(
        last_kernel,
        out_shape=jax.ShapeDtypeStruct((rows, features), BF16),
        in_specs=[vmem] * (2 + len(weights)),
        out_specs=hbm,
        scratch_shapes=[pltpu.VMEM((rows, features), BF16), pltpu.SemaphoreType.DMA((4,))],
        compiler_params=params(16),
        cost_estimate=cost(2 * rows * width * features, 2 * width * features),
        name="last_grad",
    )(before, part, *weights)


def in_turn(*arrays):
    held = ()
    for array in arrays:
        held = lax.optimization_barrier((*held, array))
    return held


def on_device(
    queries, text_kv, out_grad, text_segment, visual_rows, kv_weight, visual_dest, visual_sample
):
    groups, shares = lax.axis_size("group"), lax.axis_size("tensor")
    rows = visual_rows.shape[0]
    capacity = 2 * rows // groups
    width = kv_weight.shape[1] // shares
    dest_row = visual_dest.reshape(1, rows)
    sample_row = visual_sample.reshape(1, rows)

    columns, after = {}, ()

    def blocks_of(flips, kinds):
        blocks, weights = project(visual_rows, kv_weight, after, width, flips, kinds)
        columns.update(zip(flips, weights, strict=True))
        return blocks

    def across_tensor(block, even_flip, odd_flip):
        pairs = [
            (g * shares + t, g * shares + (t ^ (odd_flip if g % 2 else even_flip)))
            for g in range(groups)
            for t in range(shares)
        ]
        return lax.ppermute(block, ("group", "tensor"), pairs)

    odd = lax.axis_index("group") % 2 == 1
    if shares == 4:
        (far,) = blocks_of([3], [BF16])
        far_landed = across_tensor(far, 1, 1)
        near, cross = blocks_of([1, 2], [BF16, F32])
        after = (cross,)
        (own,) = blocks_of([0], [F32])
        pair = (cross + far_landed.astype(F32)).astype(BF16)
        landed = [
            across_tensor(jnp.where(odd, pair, near), 1, 2),
            across_tensor(jnp.where(odd, near, pair), 2, 1),
        ]
    else:
        flips = list(range(shares - 1, 0, -1))
        landed = [
            across_tensor(block, flip, flip)
            for block, flip in zip(blocks_of(flips, [BF16] * len(flips)), flips, strict=True)
        ]
        (own,) = blocks_of([0], [F32])
    stats = text_stats(queries, out_grad, text_kv, text_segment)
    stats, *landed = in_turn(stats, *landed)

    pairwise = groups == 8
    inputs = (queries, out_grad, text_segment)
    if pairwise:
        ways = [
            [(g, g ^ (odd_flip if g % 2 else even_flip)) for g in range(groups)]
            for even_flip, odd_flip in FLIPS
        ]
        neighbour = [(g, g ^ 1) for g in range(groups)]
        pairs = place(
            dest_row, sample_row, own, landed, capacity, groups * capacity, FLIPS
        )
        pairs = in_turn(
            *[lax.ppermute(pair, "group", way) for pair, way in zip(pairs[:-1], ways[:-1])]
        ) + tuple(pairs[-1:])
        ours = jnp.concatenate([pair[:capacity] for pair in pairs], axis=0)
        theirs = jnp.concatenate([pair[capacity:] for pair in pairs], axis=0)
        theirs = lax.ppermute(theirs, "group", neighbour)
        stats = slot_call(
            slot_stats_kernel, *inputs, ours, stats, False, True, "slot_stats"
        )
        passed, *final = slot_call(
            slot_grad_kernel, *inputs, theirs, stats, True, True, "slot_grad"
        )
        passed = lax.ppermute(passed, "group", neighbour)
        (kept,) = slot_call(
            slot_grad_kernel, *inputs, ours, final, True, False, "slot_grad_kept"
        )
        visual = [ours, theirs]
        passed, final = lax.optimization_barrier((passed, final))
    else:
        (sent,) = place(
            dest_row, sample_row, own, landed, capacity, groups * capacity, None
        )
        visual = [
            lax.all_to_all(
                sent.reshape(groups, capacity, -1), "group", split_axis=0, concat_axis=0, tiled=True
            ).reshape(groups * capacity, -1)
        ]
        kept, *final = slot_call(
            slot_grad_kernel, *inputs, visual[0], stats, True, True, "slot_grad"
        )

    inputs = (queries, out_grad, text_kv, text_segment, final, visual)
    text_outs = text_grad(*inputs, 0, ())

    if pairwise:
        pairs = [
            jnp.concatenate(
                [kept[at * capacity : (at + 1) * capacity], passed[at * capacity : (at + 1) * capacity]],
                axis=0,
            )
            for at in range(len(FLIPS))
        ]
        back = [lax.ppermute(pairs[at], "group", ways[at]) for at in BACK]
        kept, *back = in_turn(text_outs[2], *back)
        text_outs = (*text_outs[:2], kept)
        landed_flips = tuple(FLIPS[at] for at in BACK) + FLIPS[-1:]
        kv_grad = collect(dest_row, back + pairs[-1:], capacity, landed_flips)
    else:
        returned = lax.all_to_all(
            kept.reshape(groups, capacity, -1), "group", split_axis=0, concat_axis=0, tiled=True
        ).reshape(groups * capacity, -1)
        kv_grad = collect(dest_row, [returned], capacity, None)

    for head in range(1, text_kv.shape[1] // (2 * HD)):
        text_outs = text_grad(*inputs, head, text_outs)
    attended, query_grad, text_kv_grad = text_outs

    if shares == 4:
        first = across_tensor(kv_grad, 2, 1)
        second = across_tensor(kv_grad, 1, 2)
        text_kv_grad, second, first = in_turn(text_kv_grad, second, first)
        crossed, near = jnp.where(odd, second, first), jnp.where(odd, first, second)
        gathered = [near, crossed, across_tensor(crossed, 1, 1)]
    else:
        gathered = [across_tensor(kv_grad, flip, flip) for flip in range(1, shares)]
    total = feature_grad(
        near_kernel, (kv_grad, columns[0], gathered[0], columns[1]), "near_grad"
    )
    for flip in range(2, shares - 1):
        total = feature_grad(far_kernel, (total, gathered[flip - 1], columns[flip]), "far_grad")
    total = last_grad(total, gathered[-1], [columns[shares - 1]])
    return (attended, query_grad, text_kv_grad, total)


def solution(mesh):
    placed = (
        P("group", "tensor"),
        P("group", "tensor"),
        P("group", "tensor"),
        P("group", None),
        P("group", "tensor"),
        P("tensor", None),
        P("group", None),
        P("group"),
    )
    return jax.shard_map(
        on_device,
        mesh=mesh,
        in_specs=placed,
        out_specs=(
            P("group", "tensor"),
            P("group", "tensor"),
            P("group", "tensor"),
            P("group", "tensor"),
        ),
        check_vma=False,
    )
```

time: 57.2 us -> 53.6 us (0.937)
  waiting for transfers between devices: 14.9 us -> 9.47 us
  Pallas kernels: 21.1 us -> 22.7 us
    ppermute x11, waiting for transfers between devices: 11 us -> 5.29 us  [the longest x6 3.95 us: across_tensor(): return lax.ppermute(block, ('group', 'tensor'), pairs)]
    pallas_call x8 -> x10, Pallas kernels: 12.8 us -> 14.5 us  [the longest x3 7.54 us: project(): pl.pallas_call(functools.partial(project_kernel, flips=flips, steps=steps...]
  transfers between devices with their start and end apart: 14 -> 14, of which waited for: 12 -> 8; matrix products, arithmetic and copies ran while one was open for 0% -> 0% of each run, Pallas kernels for 23% -> 32%
where the time goes in v3:
time: 53.6 us; the launch traced here: 53.4 us
  Pallas kernels  22.7 us (42%)
  starting transfers between devices  20.1 us (38%)
  waiting for transfers between devices  9.47 us (18%)
  between operations  0.87 us (2%)
    ppermute x6, starting transfers between devices, across_tensor(): return lax.ppermute(block, ('group', 'tensor'), pairs)  12.7 us
    pallas_call x3, Pallas kernels, project(): pl.pallas_call(functools.partial(project_kernel, flips=flips, steps=steps...  7.54 us
    pallas_call x2, Pallas kernels, text_grad(): pl.pallas_call(functools.partial(text_grad_kernel, arrivals=len(visual),...  5.62 us
    ppermute x3, waiting for transfers between devices, on_device(): lax.ppermute(pair, 'group', way)  4.18 us
    pallas_call x3, Pallas kernels, slot_call(): pl.pallas_call(kernel, out_shape=shapes, in_specs=[vmem] * 7, out_specs=[...  4.14 us
    ppermute x6, waiting for transfers between devices, across_tensor(): return lax.ppermute(block, ('group', 'tensor'), pairs)  3.95 us
    ppermute x3, starting transfers between devices, on_device(): lax.ppermute(pair, 'group', way)  3.55 us
    ppermute x3, starting transfers between devices, on_device(): back = [lax.ppermute(pairs[at], 'group', ways[at]) for at in BACK]  3.55 us
  transfers between devices with their start and end apart: 14, of which 8 were waited for; matrix products, arithmetic and copies ran while one was open for 0% of the time, Pallas kernels for 32%

profile of v3, /device:TPU:0, one launch (start us, length us, event | category | flops | bytes accessed | tf_op | source)
XLA Modules:
  0.0 53.4 jit_solution(9729479551813844371)
XLA Ops:
  0.6 2.0 %project.5 = (bf16[128,512]{1,0:T(8,128)(2,1)S(1)}, bf16[2048,512]{1,0:T(8,128)(2,1)S(1)}) custom-call(bf16[128,2048]{1,0:T(8,128)(2,1)} %rows_ref.5, bf16[2048,2048]{1,0:T(8,128)(2,1)} %weight_ref.5), custom_call_target="tpu_custom_call" | custom-call | flops 268435456 | bytes 2097152 | tf_op jit(solution)/shard_map/project/pallas_call | solution.py:81
  2.6 3.1 %collective-permute-start = (bf16[128,512]{1,0:T(8,128)(2,1)S(1)}, bf16[128,512]{1,0:T(8,128)(2,1)S(1)}, u32[]{:S(2)}, u32[]{:S(2)}) collective-permute-start(bf16[128,512]{1,0:T(8,128)(2,1)S(1)} %get-tuple-element.69), channel_id=1, source_target_pairs={{0,1},{1,0},{2,3},{3,2},{4,5},{5,4},{6,7},{7,6},{8,9},{9,8},{10,11... | collective-permute-start | bytes 393224 | tf_op jit(solution)/shard_map/ppermute | solution.py:552
  5.7 3.6 %project.3 = (bf16[128,512]{1,0:T(8,128)(2,1)S(1)}, f32[128,512]{1,0:T(8,128)S(1)}, bf16[2048,512]{1,0:T(8,128)(2,1)S(1)}, bf16[2048,512]{1,0:T(8,128)(2,1)S(1)}) custom-call(bf16[128,2048]{1,0:T(8,128)(2,1)} %rows_ref.5, bf16[2048,2048]{1,0:T(8,128)(2,1)} %weight_ref.5), custom_call_target="tpu_custom_call" | custom-call | flops 536870912 | bytes 4194304 | tf_op jit(solution)/shard_map/project/pallas_call | solution.py:81
  9.4 1.7 %collective-permute-start.1 = (bf16[128,512]{1,0:T(8,128)(2,1)S(1)}, bf16[128,512]{1,0:T(8,128)(2,1)S(1)}, u32[]{:S(2)}, u32[]{:S(2)}) collective-permute-start(bf16[128,512]{1,0:T(8,128)(2,1)S(1)} %get-tuple-element.125), channel_id=1, source_target_pairs={{0,1},{1,0},{2,3},{3,2},{4,6},{5,7},{6,4},{7,5},{8,9},{9,8},{10,11... | collective-permute-start | bytes 393224 | tf_op jit(solution)/shard_map/ppermute | solution.py:552
  11.1 2.6 %collective-permute-start.2 = (bf16[128,512]{1,0:T(8,128)(2,1)S(1)}, bf16[128,512]{1,0:T(8,128)(2,1)S(1)}, u32[]{:S(2)}, u32[]{:S(2)}) collective-permute-start(bf16[128,512]{1,0:T(8,128)(2,1)S(1)} %get-tuple-element.124), channel_id=1, source_target_pairs={{0,2},{1,3},{2,0},{3,1},{4,5},{5,4},{6,7},{7,6},{8,10},{9,11},{10,... | collective-permute-start | bytes 393224 | tf_op jit(solution)/shard_map/ppermute | solution.py:552
  13.7 1.2 %text_stats.1 = (f32[6,512]{1,0:T(8,128)S(1)}, f32[6,512]{1,0:T(8,128)S(1)}, f32[6,512]{1,0:T(8,128)S(1)}) custom-call(bf16[384,1024]{1,0:T(8,128)(2,1)S(1)} %copy-done, bf16[384,1024]{1,0:T(8,128)(2,1)S(1)} %copy-done.1, bf16[384,512]{1,0:T(8,128)(2,1)S(1)} %copy-done.2, s32[1,384]{1,0:T(1,128)S(1)} %copy-done.3), custom_call_target="tpu_custom_call" | custom-call | flops 335544320 | bytes 1572864 | tf_op jit(solution)/shard_map/text_stats/pallas_call | solution.py:241
  14.9 2.0 %project.4 = (f32[128,512]{1,0:T(8,128)S(1)}, bf16[2048,512]{1,0:T(8,128)(2,1)S(1)}) custom-call(bf16[128,2048]{1,0:T(8,128)(2,1)} %rows_ref.5, bf16[2048,2048]{1,0:T(8,128)(2,1)} %weight_ref.5, f32[128,512]{1,0:T(8,128)S(1)} %get-tuple-element.64.refs_0_), custom_call_target="tpu_custom_call" | custom-call | flops 268435456 | bytes 2097152 | tf_op jit(solution)/shard_map/project/pallas_call | solution.py:81
  16.8 0.5 collective-permute-done.1.refs_0_
  17.6 2.5 %collective-permute-start.3 = (bf16[64,640]{1,0:T(8,128)(2,1)S(1)}, bf16[64,640]{1,0:T(8,128)(2,1)S(1)}, u32[]{:S(2)}, u32[]{:S(2)}) collective-permute-start(bf16[64,640]{1,0:T(8,128)(2,1)S(1)} %get-tuple-element.77), channel_id=1, source_target_pairs={{0,24},{4,28},{8,16},{12,20},{16,8},{20,12},{24,0},{28,4},{1,25},{... | collective-permute-start | bytes 245768 | tf_op jit(solution)/shard_map/ppermute | solution.py:588
  20.1 0.5 collective-permute-start.4
  20.6 0.5 collective-permute-start.5
  21.2 2.7 %collective-permute-done.3 = bf16[64,640]{1,0:T(8,128)(2,1)S(1)} collective-permute-done((bf16[64,640]{1,0:T(8,128)(2,1)S(1)}, bf16[64,640]{1,0:T(8,128)(2,1)S(1)}, u32[]{:S(2)}, u32[]{:S(2)}) %collective-permute-start.3) | collective-permute-done | bytes 81952 | tf_op jit(solution)/shard_map/ppermute | solution.py:588
  23.9 1.5 %collective-permute-done.4 = bf16[64,640]{1,0:T(8,128)(2,1)S(1)} collective-permute-done((bf16[64,640]{1,0:T(8,128)(2,1)S(1)}, bf16[64,640]{1,0:T(8,128)(2,1)S(1)}, u32[]{:S(2)}, u32[]{:S(2)}) %collective-permute-start.4) | collective-permute-done | bytes 81952 | tf_op jit(solution)/shard_map/ppermute | solution.py:588
  25.5 0.9 %slot_stats.1 = (f32[6,512]{1,0:T(8,128)S(1)}, f32[6,512]{1,0:T(8,128)S(1)}, f32[6,512]{1,0:T(8,128)S(1)}) custom-call(bf16[384,1024]{1,0:T(8,128)(2,1)S(1)} %copy-done, bf16[384,1024]{1,0:T(8,128)(2,1)S(1)} %copy-done.1, s32[1,384]{1,0:T(1,128)S(1)} %copy-done.3, bf16[128,640]{1,0:T(8,128)(2,1)S(1)} %pad_maximum_fusion.1.slots_ref.refs_0_, ...), custom_call_target="tpu_custom_call" | custom-call | flops 201326592 | bytes 1572864 | tf_op jit(solution)/shard_map/slot_stats/pallas_call | solution.py:323
  26.4 0.5 collective-permute-done.6.slots_ref.refs_1_
  26.9 1.8 %slot_grad.1 = (bf16[128,512]{1,0:T(8,128)(2,1)S(1)}, f32[6,512]{1,0:T(8,128)S(1)}, f32[6,512]{1,0:T(8,128)S(1)}, f32[6,512]{1,0:T(8,128)S(1)}) custom-call(bf16[384,1024]{1,0:T(8,128)(2,1)S(1)} %copy-done, bf16[384,1024]{1,0:T(8,128)(2,1)S(1)} %copy-done.1, s32[1,384]{1,0:T(1,128)S(1)} %copy-done.3, ...), custom_call_target="tpu_custom_call" | custom-call | flops 402653184 | bytes 1572864 | tf_op jit(solution)/shard_map/slot_grad/pallas_call | solution.py:323
  28.9 1.4 %slot_grad_kept.1 = bf16[128,512]{1,0:T(8,128)(2,1)S(1)} custom-call(bf16[384,1024]{1,0:T(8,128)(2,1)S(1)} %copy-done, bf16[384,1024]{1,0:T(8,128)(2,1)S(1)} %copy-done.1, s32[1,384]{1,0:T(1,128)S(1)} %copy-done.3, bf16[128,640]{1,0:T(8,128)(2,1)S(1)} %pad_maximum_fusion.1.slots_ref.refs_0_, f32[6,512]{1,0:T(8,128)S(1)} %get-tuple-element.96.top_ref, ...), custom_call_target="tpu_custom_call" | custom-call | flops 402653184 | bytes 1572864 | tf_op jit(solution)/shard_map/slot_grad_kept/pallas_call | solution.py:323
  30.4 2.2 %collective-permute-start.8 = (bf16[64,512]{1,0:T(8,128)(2,1)S(1)}, bf16[64,512]{1,0:T(8,128)(2,1)S(1)}, u32[]{:S(2)}, u32[]{:S(2)}) collective-permute-start(bf16[64,512]{1,0:T(8,128)(2,1)S(1)} %pad_maximum_fusion.2), channel_id=1, source_target_pairs={{0,24},{4,28},{8,16},{12,20},{16,8},{20,12},{24,0},{28,4},{1,25},{... | collective-permute-start | bytes 196616 | tf_op jit(solution)/shard_map/ppermute | solution.py:629
  32.6 0.8 %collective-permute-start.9 = (bf16[64,512]{1,0:T(8,128)(2,1)S(1)}, bf16[64,512]{1,0:T(8,128)(2,1)S(1)}, u32[]{:S(2)}, u32[]{:S(2)}) collective-permute-start(bf16[64,512]{1,0:T(8,128)(2,1)S(1)} %pad_maximum_fusion.3), channel_id=1, source_target_pairs={{0,8},{4,20},{8,0},{12,28},{16,24},{20,4},{24,16},{28,12},{1,9},{5... | collective-permute-start | bytes 196616 | tf_op jit(solution)/shard_map/ppermute | solution.py:629
  33.4 0.6 %collective-permute-start.10 = (bf16[64,512]{1,0:T(8,128)(2,1)S(1)}, bf16[64,512]{1,0:T(8,128)(2,1)S(1)}, u32[]{:S(2)}, u32[]{:S(2)}) collective-permute-start(bf16[64,512]{1,0:T(8,128)(2,1)S(1)} %pad_maximum_fusion.4), channel_id=1, source_target_pairs={{0,16},{4,12},{8,24},{12,4},{16,0},{20,28},{24,8},{28,20},{1,17},{... | collective-permute-start | bytes 196616 | tf_op jit(solution)/shard_map/ppermute | solution.py:629
  34.0 2.8 %text_grad.2 = (bf16[384,1024]{1,0:T(8,128)(2,1)}, bf16[384,1024]{1,0:T(8,128)(2,1)}, bf16[384,512]{1,0:T(8,128)(2,1)}) custom-call(bf16[384,1024]{1,0:T(8,128)(2,1)S(1)} %copy-done, bf16[384,1024]{1,0:T(8,128)(2,1)S(1)} %copy-done.1, bf16[384,512]{1,0:T(8,128)(2,1)S(1)} %copy-done.2, s32[1,384]{1,0:T(1,128)S(1)} %copy-done.3, ...), custom_call_target="tpu_custom_call" | custom-call | flops 1207959552 | bytes 3145728 | tf_op jit(solution)/shard_map/text_grad/pallas_call | solution.py:417
  36.8 0.5 collective-permute-done.9.refs_1_
  37.3 0.4 collective-permute-done.10.refs_2_
  37.9 1.7 %collective-permute-start.11 = (bf16[128,512]{1,0:T(8,128)(2,1)S(1)}, bf16[128,512]{1,0:T(8,128)(2,1)S(1)}, u32[]{:S(2)}, u32[]{:S(2)}) collective-permute-start(bf16[128,512]{1,0:T(8,128)(2,1)S(1)} %collect.1.own_ref), channel_id=1, source_target_pairs={{0,1},{1,0},{2,3},{3,2},{4,6},{5,7},{6,4},{7,5},{8,9},{9,8},{10,11... | collective-permute-start | bytes 393224 | tf_op jit(solution)/shard_map/ppermute | solution.py:552
  39.6 1.7 %collective-permute-start.12 = (bf16[128,512]{1,0:T(8,128)(2,1)S(1)}, bf16[128,512]{1,0:T(8,128)(2,1)S(1)}, u32[]{:S(2)}, u32[]{:S(2)}) collective-permute-start(bf16[128,512]{1,0:T(8,128)(2,1)S(1)} %collect.1.own_ref), channel_id=1, source_target_pairs={{0,2},{1,3},{2,0},{3,1},{4,5},{5,4},{6,7},{7,6},{8,10},{9,11},{10,... | collective-permute-start | bytes 393224 | tf_op jit(solution)/shard_map/ppermute | solution.py:552
  41.3 2.8 %text_grad.3 = (bf16[384,1024]{1,0:T(8,128)(2,1)}, bf16[384,1024]{1,0:T(8,128)(2,1)}, bf16[384,512]{1,0:T(8,128)(2,1)}) custom-call(bf16[384,1024]{1,0:T(8,128)(2,1)S(1)} %copy-done, bf16[384,1024]{1,0:T(8,128)(2,1)S(1)} %copy-done.1, bf16[384,512]{1,0:T(8,128)(2,1)S(1)} %copy-done.2, ...), custom_call_target="tpu_custom_call", output_to_operand_aliasing={{0}: (9, {}), {1}: (10, {}), {2}: (11, {})} | custom-call | flops 1207959552 | bytes 3145728 | tf_op jit(solution)/shard_map/text_grad/pallas_call | solution.py:417
  44.1 1.9 %collective-permute-done.11 = bf16[128,512]{1,0:T(8,128)(2,1)S(1)} collective-permute-done((bf16[128,512]{1,0:T(8,128)(2,1)S(1)}, bf16[128,512]{1,0:T(8,128)(2,1)S(1)}, u32[]{:S(2)}, u32[]{:S(2)}) %collective-permute-start.11) | collective-permute-done | bytes 131104 | tf_op jit(solution)/shard_map/ppermute | solution.py:552
  46.0 2.0 %collective-permute-start.13 = (bf16[128,512]{1,0:T(8,128)(2,1)S(1)}, bf16[128,512]{1,0:T(8,128)(2,1)S(1)}, u32[]{:S(2)}, u32[]{:S(2)}) collective-permute-start(bf16[128,512]{1,0:T(8,128)(2,1)S(1)} %get-tuple-element.126.part_ref), channel_id=1, source_target_pairs={{0,1},{1,0},{2,3},{3,2},{4,5},{5,4},{6,7},{7,6},{8,9},{9,8},{10,11... | collective-permute-start | bytes 393224 | tf_op jit(solution)/shard_map/ppermute | solution.py:552
  48.0 1.4 %near_grad.1.before_ref = f32[128,2048]{1,0:T(8,128)S(1)} custom-call(bf16[128,512]{1,0:T(8,128)(2,1)S(1)} %collect.1.own_ref, bf16[2048,512]{1,0:T(8,128)(2,1)S(1)} %get-tuple-element.118.own_weight, bf16[128,512]{1,0:T(8,128)(2,1)S(1)} %get-tuple-element.127.part_ref, bf16[2048,512]{1,0:T(8,128)(2,1)S(1)} %get-tuple-element.121.refs_0_), custom_call_target="tpu_custom_call" | custom-call | flops 536870912 | bytes 4194304 | tf_op jit(solution)/shard_map/near_grad/pallas_call | solution.py:472
  49.5 0.8 %far_grad.1.before_ref = f32[128,2048]{1,0:T(8,128)S(1)} custom-call(f32[128,2048]{1,0:T(8,128)S(1)} %near_grad.1.before_ref, bf16[128,512]{1,0:T(8,128)(2,1)S(1)} %get-tuple-element.126.part_ref, bf16[2048,512]{1,0:T(8,128)(2,1)S(1)} %get-tuple-element.122.refs_0_), custom_call_target="tpu_custom_call" | custom-call | flops 536870912 | bytes 4194304 | tf_op jit(solution)/shard_map/far_grad/pallas_call | solution.py:472
  50.3 1.6 %collective-permute-done.13.part_ref = bf16[128,512]{1,0:T(8,128)(2,1)S(1)} collective-permute-done((bf16[128,512]{1,0:T(8,128)(2,1)S(1)}, bf16[128,512]{1,0:T(8,128)(2,1)S(1)}, u32[]{:S(2)}, u32[]{:S(2)}) %collective-permute-start.13) | collective-permute-done | bytes 131104 | tf_op jit(solution)/shard_map/ppermute | solution.py:552
  51.9 1.5 %last_grad.1 = bf16[128,2048]{1,0:T(8,128)(2,1)} custom-call(f32[128,2048]{1,0:T(8,128)S(1)} %far_grad.1.before_ref, bf16[128,512]{1,0:T(8,128)(2,1)S(1)} %collective-permute-done.13.part_ref, bf16[2048,512]{1,0:T(8,128)(2,1)S(1)} %get-tuple-element.123.refs_0_), custom_call_target="tpu_custom_call" | custom-call | flops 268435456 | bytes 2097152 | tf_op jit(solution)/shard_map/last_grad/pallas_call | solution.py:510
  (35 shorter events, 1.0 us)
Async XLA Ops:
  2.6 6.7 %collective-permute-start = (bf16[128,512]{1,0:T(8,128)(2,1)S(1)}, bf16[128,512]{1,0:T(8,128)(2,1)S(1)}, u32[]{:S(2)}, u32[]{:S(2)}) collective-permute-start(bf16[128,512]{1,0:T(8,128)(2,1)S(1)} %get-tuple-element.69), channel_id=1, source_target_pairs={{0,1},{1,0},{2,3},{3,2},{4,5},{5,4},{6,7},{7,6},{8,9},{9,8},{10,11... | collective-permute-start | bytes 393224 | tf_op jit(solution)/shard_map/ppermute | solution.py:552
  5.7 8.0 %copy-start = (bf16[384,1024]{1,0:T(8,128)(2,1)S(1)}, bf16[384,1024]{1,0:T(8,128)(2,1)}, u32[]{:S(2)}) copy-start(bf16[384,1024]{1,0:T(8,128)(2,1)} %query_ref.11) | copy-start | bytes 2359300
  5.7 8.0 %copy-start.1 = (bf16[384,1024]{1,0:T(8,128)(2,1)S(1)}, bf16[384,1024]{1,0:T(8,128)(2,1)}, u32[]{:S(2)}) copy-start(bf16[384,1024]{1,0:T(8,128)(2,1)} %grad_ref.11) | copy-start | bytes 2359300
  5.7 8.0 %copy-start.2 = (bf16[384,512]{1,0:T(8,128)(2,1)S(1)}, bf16[384,512]{1,0:T(8,128)(2,1)}, u32[]{:S(2)}) copy-start(bf16[384,512]{1,0:T(8,128)(2,1)} %kv_ref.5) | copy-start | bytes 1179652
  5.7 8.0 %copy-start.3 = (s32[1,384]{1,0:T(1,128)S(1)}, s32[1,384]{1,0:T(1,128)}, u32[]{:S(2)}) copy-start(s32[1,384]{1,0:T(1,128)} %segment_ref.11) | copy-start | bytes 4612
  9.4 7.9 %collective-permute-start.1 = (bf16[128,512]{1,0:T(8,128)(2,1)S(1)}, bf16[128,512]{1,0:T(8,128)(2,1)S(1)}, u32[]{:S(2)}, u32[]{:S(2)}) collective-permute-start(bf16[128,512]{1,0:T(8,128)(2,1)S(1)} %get-tuple-element.125), channel_id=1, source_target_pairs={{0,1},{1,0},{2,3},{3,2},{4,6},{5,7},{6,4},{7,5},{8,9},{9,8},{10,11... | collective-permute-start | bytes 393224 | tf_op jit(solution)/shard_map/ppermute | solution.py:552
  11.1 6.3 %collective-permute-start.2 = (bf16[128,512]{1,0:T(8,128)(2,1)S(1)}, bf16[128,512]{1,0:T(8,128)(2,1)S(1)}, u32[]{:S(2)}, u32[]{:S(2)}) collective-permute-start(bf16[128,512]{1,0:T(8,128)(2,1)S(1)} %get-tuple-element.124), channel_id=1, source_target_pairs={{0,2},{1,3},{2,0},{3,1},{4,5},{5,4},{6,7},{7,6},{8,10},{9,11},{10,... | collective-permute-start | bytes 393224 | tf_op jit(solution)/shard_map/ppermute | solution.py:552
  14.8 2.5 %copy-start.4 = (s32[128,1]{0,1:T(1,128)S(1)}, s32[128,1]{0,1:T(1,128)}, u32[]{:S(2)}) copy-start(s32[128,1]{0,1:T(1,128)} %param.14) | copy-start | bytes 1540
  14.8 2.5 %copy-start.5 = (s32[128]{0:T(128)S(1)}, s32[128]{0:T(128)}, u32[]{:S(2)}) copy-start(s32[128]{0:T(128)} %param.15) | copy-start | bytes 1540
  17.6 6.3 %collective-permute-start.3 = (bf16[64,640]{1,0:T(8,128)(2,1)S(1)}, bf16[64,640]{1,0:T(8,128)(2,1)S(1)}, u32[]{:S(2)}, u32[]{:S(2)}) collective-permute-start(bf16[64,640]{1,0:T(8,128)(2,1)S(1)} %get-tuple-element.77), channel_id=1, source_target_pairs={{0,24},{4,28},{8,16},{12,20},{16,8},{20,12},{24,0},{28,4},{1,25},{... | collective-permute-start | bytes 245768 | tf_op jit(solution)/shard_map/ppermute | solution.py:588
  20.1 5.2 %collective-permute-start.4 = (bf16[64,640]{1,0:T(8,128)(2,1)S(1)}, bf16[64,640]{1,0:T(8,128)(2,1)S(1)}, u32[]{:S(2)}, u32[]{:S(2)}) collective-permute-start(bf16[64,640]{1,0:T(8,128)(2,1)S(1)} %get-tuple-element.78), channel_id=1, source_target_pairs={{0,16},{4,12},{8,24},{12,4},{16,0},{20,28},{24,8},{28,20},{1,17},{... | collective-permute-start | bytes 245768 | tf_op jit(solution)/shard_map/ppermute | solution.py:588
  20.6 4.7 %collective-permute-start.5 = (bf16[64,640]{1,0:T(8,128)(2,1)S(1)}, bf16[64,640]{1,0:T(8,128)(2,1)S(1)}, u32[]{:S(2)}, u32[]{:S(2)}) collective-permute-start(bf16[64,640]{1,0:T(8,128)(2,1)S(1)} %get-tuple-element.81), channel_id=1, source_target_pairs={{0,8},{4,20},{8,0},{12,28},{16,24},{20,4},{24,16},{28,12},{1,9},{5... | collective-permute-start | bytes 245768 | tf_op jit(solution)/shard_map/ppermute | solution.py:588
  25.4 1.5 %collective-permute-start.6 = (bf16[128,640]{1,0:T(8,128)(2,1)S(1)}, bf16[128,640]{1,0:T(8,128)(2,1)S(1)}, u32[]{:S(2)}, u32[]{:S(2)}) collective-permute-start(bf16[128,640]{1,0:T(8,128)(2,1)S(1)} %pad_maximum_fusion), channel_id=1, source_target_pairs={{0,4},{4,0},{8,12},{12,8},{16,20},{20,16},{24,28},{28,24},{1,5},{5... | collective-permute-start | bytes 491528 | tf_op jit(solution)/shard_map/ppermute | solution.py:592
  28.7 1.6 %collective-permute-start.7 = (bf16[128,512]{1,0:T(8,128)(2,1)S(1)}, bf16[128,512]{1,0:T(8,128)(2,1)S(1)}, u32[]{:S(2)}, u32[]{:S(2)}) collective-permute-start(bf16[128,512]{1,0:T(8,128)(2,1)S(1)} %get-tuple-element.92), channel_id=1, source_target_pairs={{0,4},{4,0},{8,12},{12,8},{16,20},{20,16},{24,28},{28,24},{1,5},{5... | collective-permute-start | bytes 393224 | tf_op jit(solution)/shard_map/ppermute | solution.py:599
  30.4 6.4 %collective-permute-start.8 = (bf16[64,512]{1,0:T(8,128)(2,1)S(1)}, bf16[64,512]{1,0:T(8,128)(2,1)S(1)}, u32[]{:S(2)}, u32[]{:S(2)}) collective-permute-start(bf16[64,512]{1,0:T(8,128)(2,1)S(1)} %pad_maximum_fusion.2), channel_id=1, source_target_pairs={{0,24},{4,28},{8,16},{12,20},{16,8},{20,12},{24,0},{28,4},{1,25},{... | collective-permute-start | bytes 196616 | tf_op jit(solution)/shard_map/ppermute | solution.py:629
  32.6 4.6 %collective-permute-start.9 = (bf16[64,512]{1,0:T(8,128)(2,1)S(1)}, bf16[64,512]{1,0:T(8,128)(2,1)S(1)}, u32[]{:S(2)}, u32[]{:S(2)}) collective-permute-start(bf16[64,512]{1,0:T(8,128)(2,1)S(1)} %pad_maximum_fusion.3), channel_id=1, source_target_pairs={{0,8},{4,20},{8,0},{12,28},{16,24},{20,4},{24,16},{28,12},{1,9},{5... | collective-permute-start | bytes 196616 | tf_op jit(solution)/shard_map/ppermute | solution.py:629
  33.4 4.3 %collective-permute-start.10 = (bf16[64,512]{1,0:T(8,128)(2,1)S(1)}, bf16[64,512]{1,0:T(8,128)(2,1)S(1)}, u32[]{:S(2)}, u32[]{:S(2)}) collective-permute-start(bf16[64,512]{1,0:T(8,128)(2,1)S(1)} %pad_maximum_fusion.4), channel_id=1, source_target_pairs={{0,16},{4,12},{8,24},{12,4},{16,0},{20,28},{24,8},{28,20},{1,17},{... | collective-permute-start | bytes 196616 | tf_op jit(solution)/shard_map/ppermute | solution.py:629
  37.9 8.1 %collective-permute-start.11 = (bf16[128,512]{1,0:T(8,128)(2,1)S(1)}, bf16[128,512]{1,0:T(8,128)(2,1)S(1)}, u32[]{:S(2)}, u32[]{:S(2)}) collective-permute-start(bf16[128,512]{1,0:T(8,128)(2,1)S(1)} %collect.1.own_ref), channel_id=1, source_target_pairs={{0,1},{1,0},{2,3},{3,2},{4,6},{5,7},{6,4},{7,5},{8,9},{9,8},{10,11... | collective-permute-start | bytes 393224 | tf_op jit(solution)/shard_map/ppermute | solution.py:552
  39.6 6.4 %collective-permute-start.12 = (bf16[128,512]{1,0:T(8,128)(2,1)S(1)}, bf16[128,512]{1,0:T(8,128)(2,1)S(1)}, u32[]{:S(2)}, u32[]{:S(2)}) collective-permute-start(bf16[128,512]{1,0:T(8,128)(2,1)S(1)} %collect.1.own_ref), channel_id=1, source_target_pairs={{0,2},{1,3},{2,0},{3,1},{4,5},{5,4},{6,7},{7,6},{8,10},{9,11},{10,... | collective-permute-start | bytes 393224 | tf_op jit(solution)/shard_map/ppermute | solution.py:552
  46.0 5.9 %collective-permute-start.13 = (bf16[128,512]{1,0:T(8,128)(2,1)S(1)}, bf16[128,512]{1,0:T(8,128)(2,1)S(1)}, u32[]{:S(2)}, u32[]{:S(2)}) collective-permute-start(bf16[128,512]{1,0:T(8,128)(2,1)S(1)} %get-tuple-element.126.part_ref), channel_id=1, source_target_pairs={{0,1},{1,0},{2,3},{3,2},{4,5},{5,4},{6,7},{7,6},{8,9},{9,8},{10,11... | collective-permute-start | bytes 393224 | tf_op jit(solution)/shard_map/ppermute | solution.py:552

commit v4 on v3

--- a/solution.py
+++ b/solution.py
@@ -438,31 +438,32 @@
     )(queries, out_grad, text_kv, segment, *stats, *visual, *before)
 
 
-def by_core(weights, body):
-    if len(weights) == 1:
-        body(weights[0])
-    else:
-        odd = lax.axis_index("group") & 1
-        for parity, weight in enumerate(weights):
-            pl.when(odd == parity)(functools.partial(body, weight))
-
-
-def near_kernel(own_ref, own_weight, part_ref, *refs):
-    *weights, out_ref = refs
-
-    def body(weight):
-        out_ref[...] = dot_nt(own_ref[...], own_weight[...]) + dot_nt(part_ref[...], weight[...])
-
-    by_core(weights, body)
-
-
-def far_kernel(before_ref, part_ref, *refs):
-    *weights, out_ref = refs
-
-    def body(weight):
-        out_ref[...] = before_ref[...] + dot_nt(part_ref[...], weight[...])
-
-    by_core(weights, body)
+def crossed_kernel(first_ref, second_ref, out_ref):
+    odd = lax.axis_index("group") & 1 == 1
+    out_ref[...] = jnp.where(odd, second_ref[...], first_ref[...])
+
+
+def crossed_of(first, second):
+    vmem = pl.BlockSpec(memory_space=pltpu.VMEM)
+    return pl.pallas_call(
+        crossed_kernel,
+        out_shape=jax.ShapeDtypeStruct(first.shape, BF16),
+        in_specs=[vmem] * 2,
+        out_specs=vmem,
+        compiler_params=params(8),
+        cost_estimate=cost(first.size, 6 * first.size),
+        name="crossed",
+    )(first, second)
+
+
+def near_kernel(own_ref, own_weight, first_ref, second_ref, weight_ref, out_ref):
+    odd = lax.axis_index("group") & 1 == 1
+    near = jnp.where(odd, first_ref[...], second_ref[...])
+    out_ref[...] = dot_nt(own_ref[...], own_weight[...]) + dot_nt(near, weight_ref[...])
+
+
+def next_kernel(before_ref, part_ref, weight_ref, out_ref):
+    out_ref[...] = before_ref[...] + dot_nt(part_ref[...], weight_ref[...])
 
 
 def feature_grad(kernel, operands, name):
@@ -480,43 +481,57 @@
     )(*operands)
 
 
-def last_kernel(before_ref, part_ref, *refs):
-    *weights, out_ref, rounded, sems = refs
+def turn_kernel(weight_ref, out_ref):
+    for start in range(0, weight_ref.shape[0], 2 * TILE):
+        out_ref[:, start : start + 2 * TILE] = weight_ref[start : start + 2 * TILE, :].T
+
+
+def turn(weight):
+    features, width = weight.shape
+    vmem = pl.BlockSpec(memory_space=pltpu.VMEM)
+    return pl.pallas_call(
+        turn_kernel,
+        out_shape=jax.ShapeDtypeStruct((width, features), BF16),
+        in_specs=[vmem],
+        out_specs=vmem,
+        compiler_params=params(16),
+        cost_estimate=cost(0, 4 * width * features),
+        name="turn",
+    )(weight)
+
+
+def last_kernel(before_ref, part_ref, weight_ref, out_ref, rounded, sems):
     steps = sems.shape[0]
     count = out_ref.shape[1] // steps
-
-    def copy(step):
+    copies = []
+    for step in range(steps):
         columns = slice(step * count, (step + 1) * count)
-        return pltpu.make_async_copy(
-            rounded.at[:, columns], out_ref.at[:, columns], sems.at[step]
-        )
-
-    def body(weight):
-        for step in range(steps):
-            columns = slice(step * count, (step + 1) * count)
-            term = dot_nt(part_ref[...], weight[columns, :])
-            rounded[:, columns] = (before_ref[:, columns] + term).astype(BF16)
-            copy(step).start()
-
-    by_core(weights, body)
-    for step in range(steps):
-        copy(step).wait()
-
-
-def last_grad(before, part, weights):
+        term = dot_nn(part_ref[...], weight_ref[:, columns])
+        rounded[:, columns] = (before_ref[:, columns] + term).astype(BF16)
+        copies.append(
+            pltpu.make_async_copy(
+                rounded.at[:, columns], out_ref.at[:, columns], sems.at[step]
+            )
+        )
+        copies[-1].start()
+    for copy in copies:
+        copy.wait()
+
+
+def last_grad(before, part, weight):
     rows, width = part.shape
-    features = weights[0].shape[0]
+    features = weight.shape[1]
     vmem, hbm = pl.BlockSpec(memory_space=pltpu.VMEM), pl.BlockSpec(memory_space=pltpu.HBM)
     return pl.pallas_call(
         last_kernel,
         out_shape=jax.ShapeDtypeStruct((rows, features), BF16),
-        in_specs=[vmem] * (2 + len(weights)),
+        in_specs=[vmem] * 3,
         out_specs=hbm,
         scratch_shapes=[pltpu.VMEM((rows, features), BF16), pltpu.SemaphoreType.DMA((4,))],
         compiler_params=params(16),
         cost_estimate=cost(2 * rows * width * features, 2 * width * features),
         name="last_grad",
-    )(before, part, *weights)
+    )(before, part, weight)
 
 
 def in_turn(*arrays):
@@ -644,17 +659,21 @@
     if shares == 4:
         first = across_tensor(kv_grad, 2, 1)
         second = across_tensor(kv_grad, 1, 2)
-        text_kv_grad, second, first = in_turn(text_kv_grad, second, first)
-        crossed, near = jnp.where(odd, second, first), jnp.where(odd, first, second)
-        gathered = [near, crossed, across_tensor(crossed, 1, 1)]
+        text_kv_grad, turned, second, first = in_turn(
+            text_kv_grad, turn(columns[shares - 1]), second, first
+        )
+        crossed = crossed_of(first, second)
+        last = across_tensor(crossed, 1, 1)
+        operands = (kv_grad, columns[0], first, second, columns[1])
+        total = feature_grad(near_kernel, operands, "near_grad")
+        total = feature_grad(next_kernel, (total, crossed, columns[2]), "next_grad")
     else:
-        gathered = [across_tensor(kv_grad, flip, flip) for flip in range(1, shares)]
-    total = feature_grad(
-        near_kernel, (kv_grad, columns[0], gathered[0], columns[1]), "near_grad"
-    )
-    for flip in range(2, shares - 1):
-        total = feature_grad(far_kernel, (total, gathered[flip - 1], columns[flip]), "far_grad")
-    total = last_grad(total, gathered[-1], [columns[shares - 1]])
+        *gathered, last = [across_tensor(kv_grad, flip, flip) for flip in range(1, shares)]
+        turned = turn(columns[shares - 1])
+        total = jnp.zeros((rows, kv_weight.shape[0]), F32)
+        for flip, part in enumerate([kv_grad, *gathered]):
+            total = feature_grad(next_kernel, (total, part, columns[flip]), "next_grad")
+    total = last_grad(total, last, turned)
     return (attended, query_grad, text_kv_grad, total)
 
 

time: 53.6 us -> 53.3 us (level)
  waiting for transfers between devices: 9.47 us -> 8.78 us
    ppermute x6, waiting for transfers between devices: 3.95 us -> 3.27 us  [across_tensor(): return lax.ppermute(block, ('group', 'tensor'), pairs)]
    pallas_call x0 -> x2, Pallas kernels: none -> 0.65 us  [the longest x1 0.63 us: turn(): pl.pallas_call(turn_kernel, out_shape=jax.ShapeDtypeStruct((width, featur...]
  transfers between devices with their start and end apart: 14 -> 14, of which waited for: 8 -> 8; matrix products, arithmetic and copies ran while one was open for 0% -> 0% of each run, Pallas kernels for 32% -> 33%
where the time goes in v4:
time: 53.3 us; the launch traced here: 53.1 us
  Pallas kernels  23.1 us (43%)
  starting transfers between devices  20.2 us (38%)
  waiting for transfers between devices  8.78 us (16%)
  between operations  0.87 us (2%)
    ppermute x6, starting transfers between devices, across_tensor(): return lax.ppermute(block, ('group', 'tensor'), pairs)  12.8 us
    pallas_call x3, Pallas kernels, project(): pl.pallas_call(functools.partial(project_kernel, flips=flips, steps=steps...  7.54 us
    pallas_call x2, Pallas kernels, text_grad(): pl.pallas_call(functools.partial(text_grad_kernel, arrivals=len(visual),...  5.63 us
    ppermute x3, waiting for transfers between devices, on_device(): lax.ppermute(pair, 'group', way)  4.18 us
    pallas_call x3, Pallas kernels, slot_call(): pl.pallas_call(kernel, out_shape=shapes, in_specs=[vmem] * 7, out_specs=[...  4.12 us
    ppermute x3, starting transfers between devices, on_device(): back = [lax.ppermute(pairs[at], 'group', ways[at]) for at in BACK]  3.57 us
    ppermute x3, starting transfers between devices, on_device(): lax.ppermute(pair, 'group', way)  3.55 us
    ppermute x6, waiting for transfers between devices, across_tensor(): return lax.ppermute(block, ('group', 'tensor'), pairs)  3.27 us
  transfers between devices with their start and end apart: 14, of which 8 were waited for; matrix products, arithmetic and copies ran while one was open for 0% of the time, Pallas kernels for 33%

profile of v4, /device:TPU:0, one launch (start us, length us, event | category | flops | bytes accessed | tf_op | source)
XLA Modules:
  0.0 53.1 jit_solution(18303973796526384915)
XLA Ops:
  0.6 2.0 %project.5 = (bf16[128,512]{1,0:T(8,128)(2,1)S(1)}, bf16[2048,512]{1,0:T(8,128)(2,1)S(1)}) custom-call(bf16[128,2048]{1,0:T(8,128)(2,1)} %rows_ref.5, bf16[2048,2048]{1,0:T(8,128)(2,1)} %weight_ref.5), custom_call_target="tpu_custom_call" | custom-call | flops 268435456 | bytes 2097152 | tf_op jit(solution)/shard_map/project/pallas_call | solution.py:81
  2.6 3.1 %collective-permute-start = (bf16[128,512]{1,0:T(8,128)(2,1)S(1)}, bf16[128,512]{1,0:T(8,128)(2,1)S(1)}, u32[]{:S(2)}, u32[]{:S(2)}) collective-permute-start(bf16[128,512]{1,0:T(8,128)(2,1)S(1)} %get-tuple-element.73), channel_id=1, source_target_pairs={{0,1},{1,0},{2,3},{3,2},{4,5},{5,4},{6,7},{7,6},{8,9},{9,8},{10,11... | collective-permute-start | bytes 393224 | tf_op jit(solution)/shard_map/ppermute | solution.py:567
  5.7 3.6 %project.3 = (bf16[128,512]{1,0:T(8,128)(2,1)S(1)}, f32[128,512]{1,0:T(8,128)S(1)}, bf16[2048,512]{1,0:T(8,128)(2,1)S(1)}, bf16[2048,512]{1,0:T(8,128)(2,1)S(1)}) custom-call(bf16[128,2048]{1,0:T(8,128)(2,1)} %rows_ref.5, bf16[2048,2048]{1,0:T(8,128)(2,1)} %weight_ref.5), custom_call_target="tpu_custom_call" | custom-call | flops 536870912 | bytes 4194304 | tf_op jit(solution)/shard_map/project/pallas_call | solution.py:81
  9.4 1.7 %collective-permute-start.1 = (bf16[128,512]{1,0:T(8,128)(2,1)S(1)}, bf16[128,512]{1,0:T(8,128)(2,1)S(1)}, u32[]{:S(2)}, u32[]{:S(2)}) collective-permute-start(bf16[128,512]{1,0:T(8,128)(2,1)S(1)} %get-tuple-element.133), channel_id=1, source_target_pairs={{0,1},{1,0},{2,3},{3,2},{4,6},{5,7},{6,4},{7,5},{8,9},{9,8},{10,11... | collective-permute-start | bytes 393224 | tf_op jit(solution)/shard_map/ppermute | solution.py:567
  11.1 2.6 %collective-permute-start.2 = (bf16[128,512]{1,0:T(8,128)(2,1)S(1)}, bf16[128,512]{1,0:T(8,128)(2,1)S(1)}, u32[]{:S(2)}, u32[]{:S(2)}) collective-permute-start(bf16[128,512]{1,0:T(8,128)(2,1)S(1)} %get-tuple-element.132), channel_id=1, source_target_pairs={{0,2},{1,3},{2,0},{3,1},{4,5},{5,4},{6,7},{7,6},{8,10},{9,11},{10,... | collective-permute-start | bytes 393224 | tf_op jit(solution)/shard_map/ppermute | solution.py:567
  13.7 1.2 %text_stats.1 = (f32[6,512]{1,0:T(8,128)S(1)}, f32[6,512]{1,0:T(8,128)S(1)}, f32[6,512]{1,0:T(8,128)S(1)}) custom-call(bf16[384,1024]{1,0:T(8,128)(2,1)S(1)} %copy-done, bf16[384,1024]{1,0:T(8,128)(2,1)S(1)} %copy-done.1, bf16[384,512]{1,0:T(8,128)(2,1)S(1)} %copy-done.2, s32[1,384]{1,0:T(1,128)S(1)} %copy-done.3), custom_call_target="tpu_custom_call" | custom-call | flops 335544320 | bytes 1572864 | tf_op jit(solution)/shard_map/text_stats/pallas_call | solution.py:241
  14.9 2.0 %project.4 = (f32[128,512]{1,0:T(8,128)S(1)}, bf16[2048,512]{1,0:T(8,128)(2,1)S(1)}) custom-call(bf16[128,2048]{1,0:T(8,128)(2,1)} %rows_ref.5, bf16[2048,2048]{1,0:T(8,128)(2,1)} %weight_ref.5, f32[128,512]{1,0:T(8,128)S(1)} %get-tuple-element.68.refs_0_), custom_call_target="tpu_custom_call" | custom-call | flops 268435456 | bytes 2097152 | tf_op jit(solution)/shard_map/project/pallas_call | solution.py:81
  16.8 0.5 collective-permute-done.1.refs_0_
  17.6 2.5 %collective-permute-start.3 = (bf16[64,640]{1,0:T(8,128)(2,1)S(1)}, bf16[64,640]{1,0:T(8,128)(2,1)S(1)}, u32[]{:S(2)}, u32[]{:S(2)}) collective-permute-start(bf16[64,640]{1,0:T(8,128)(2,1)S(1)} %get-tuple-element.81), channel_id=1, source_target_pairs={{0,24},{4,28},{8,16},{12,20},{16,8},{20,12},{24,0},{28,4},{1,25},{... | collective-permute-start | bytes 245768 | tf_op jit(solution)/shard_map/ppermute | solution.py:603
  20.1 0.5 collective-permute-start.4
  20.6 0.5 collective-permute-start.5
  21.2 2.7 %collective-permute-done.3 = bf16[64,640]{1,0:T(8,128)(2,1)S(1)} collective-permute-done((bf16[64,640]{1,0:T(8,128)(2,1)S(1)}, bf16[64,640]{1,0:T(8,128)(2,1)S(1)}, u32[]{:S(2)}, u32[]{:S(2)}) %collective-permute-start.3) | collective-permute-done | bytes 81952 | tf_op jit(solution)/shard_map/ppermute | solution.py:603
  23.9 1.5 %collective-permute-done.4 = bf16[64,640]{1,0:T(8,128)(2,1)S(1)} collective-permute-done((bf16[64,640]{1,0:T(8,128)(2,1)S(1)}, bf16[64,640]{1,0:T(8,128)(2,1)S(1)}, u32[]{:S(2)}, u32[]{:S(2)}) %collective-permute-start.4) | collective-permute-done | bytes 81952 | tf_op jit(solution)/shard_map/ppermute | solution.py:603
  25.5 0.9 %slot_stats.1 = (f32[6,512]{1,0:T(8,128)S(1)}, f32[6,512]{1,0:T(8,128)S(1)}, f32[6,512]{1,0:T(8,128)S(1)}) custom-call(bf16[384,1024]{1,0:T(8,128)(2,1)S(1)} %copy-done, bf16[384,1024]{1,0:T(8,128)(2,1)S(1)} %copy-done.1, s32[1,384]{1,0:T(1,128)S(1)} %copy-done.3, bf16[128,640]{1,0:T(8,128)(2,1)S(1)} %pad_maximum_fusion.1.slots_ref.refs_0_, ...), custom_call_target="tpu_custom_call" | custom-call | flops 201326592 | bytes 1572864 | tf_op jit(solution)/shard_map/slot_stats/pallas_call | solution.py:323
  26.4 0.5 collective-permute-done.6.slots_ref.refs_1_
  26.9 1.8 %slot_grad.1 = (bf16[128,512]{1,0:T(8,128)(2,1)S(1)}, f32[6,512]{1,0:T(8,128)S(1)}, f32[6,512]{1,0:T(8,128)S(1)}, f32[6,512]{1,0:T(8,128)S(1)}) custom-call(bf16[384,1024]{1,0:T(8,128)(2,1)S(1)} %copy-done, bf16[384,1024]{1,0:T(8,128)(2,1)S(1)} %copy-done.1, s32[1,384]{1,0:T(1,128)S(1)} %copy-done.3, ...), custom_call_target="tpu_custom_call" | custom-call | flops 402653184 | bytes 1572864 | tf_op jit(solution)/shard_map/slot_grad/pallas_call | solution.py:323
  28.9 1.4 %slot_grad_kept.1 = bf16[128,512]{1,0:T(8,128)(2,1)S(1)} custom-call(bf16[384,1024]{1,0:T(8,128)(2,1)S(1)} %copy-done, bf16[384,1024]{1,0:T(8,128)(2,1)S(1)} %copy-done.1, s32[1,384]{1,0:T(1,128)S(1)} %copy-done.3, bf16[128,640]{1,0:T(8,128)(2,1)S(1)} %pad_maximum_fusion.1.slots_ref.refs_0_, f32[6,512]{1,0:T(8,128)S(1)} %get-tuple-element.100.top_ref, ...), custom_call_target="tpu_custom_call" | custom-call | flops 402653184 | bytes 1572864 | tf_op jit(solution)/shard_map/slot_grad_kept/pallas_call | solution.py:323
  30.4 2.2 %collective-permute-start.8 = (bf16[64,512]{1,0:T(8,128)(2,1)S(1)}, bf16[64,512]{1,0:T(8,128)(2,1)S(1)}, u32[]{:S(2)}, u32[]{:S(2)}) collective-permute-start(bf16[64,512]{1,0:T(8,128)(2,1)S(1)} %pad_maximum_fusion.2), channel_id=1, source_target_pairs={{0,24},{4,28},{8,16},{12,20},{16,8},{20,12},{24,0},{28,4},{1,25},{... | collective-permute-start | bytes 196616 | tf_op jit(solution)/shard_map/ppermute | solution.py:644
  32.6 0.8 %collective-permute-start.9 = (bf16[64,512]{1,0:T(8,128)(2,1)S(1)}, bf16[64,512]{1,0:T(8,128)(2,1)S(1)}, u32[]{:S(2)}, u32[]{:S(2)}) collective-permute-start(bf16[64,512]{1,0:T(8,128)(2,1)S(1)} %pad_maximum_fusion.3), channel_id=1, source_target_pairs={{0,8},{4,20},{8,0},{12,28},{16,24},{20,4},{24,16},{28,12},{1,9},{5... | collective-permute-start | bytes 196616 | tf_op jit(solution)/shard_map/ppermute | solution.py:644
  33.4 0.6 %collective-permute-start.10 = (bf16[64,512]{1,0:T(8,128)(2,1)S(1)}, bf16[64,512]{1,0:T(8,128)(2,1)S(1)}, u32[]{:S(2)}, u32[]{:S(2)}) collective-permute-start(bf16[64,512]{1,0:T(8,128)(2,1)S(1)} %pad_maximum_fusion.4), channel_id=1, source_target_pairs={{0,16},{4,12},{8,24},{12,4},{16,0},{20,28},{24,8},{28,20},{1,17},{... | collective-permute-start | bytes 196616 | tf_op jit(solution)/shard_map/ppermute | solution.py:644
  34.0 2.8 %text_grad.2 = (bf16[384,1024]{1,0:T(8,128)(2,1)}, bf16[384,1024]{1,0:T(8,128)(2,1)}, bf16[384,512]{1,0:T(8,128)(2,1)}) custom-call(bf16[384,1024]{1,0:T(8,128)(2,1)S(1)} %copy-done, bf16[384,1024]{1,0:T(8,128)(2,1)S(1)} %copy-done.1, bf16[384,512]{1,0:T(8,128)(2,1)S(1)} %copy-done.2, s32[1,384]{1,0:T(1,128)S(1)} %copy-done.3, ...), custom_call_target="tpu_custom_call" | custom-call | flops 1207959552 | bytes 3145728 | tf_op jit(solution)/shard_map/text_grad/pallas_call | solution.py:417
  36.8 0.5 collective-permute-done.9.refs_1_
  37.9 1.7 %collective-permute-start.11 = (bf16[128,512]{1,0:T(8,128)(2,1)S(1)}, bf16[128,512]{1,0:T(8,128)(2,1)S(1)}, u32[]{:S(2)}, u32[]{:S(2)}) collective-permute-start(bf16[128,512]{1,0:T(8,128)(2,1)S(1)} %collect.1.own_ref), channel_id=1, source_target_pairs={{0,1},{1,0},{2,3},{3,2},{4,6},{5,7},{6,4},{7,5},{8,9},{9,8},{10,11... | collective-permute-start | bytes 393224 | tf_op jit(solution)/shard_map/ppermute | solution.py:567
  39.6 1.7 %collective-permute-start.12 = (bf16[128,512]{1,0:T(8,128)(2,1)S(1)}, bf16[128,512]{1,0:T(8,128)(2,1)S(1)}, u32[]{:S(2)}, u32[]{:S(2)}) collective-permute-start(bf16[128,512]{1,0:T(8,128)(2,1)S(1)} %collect.1.own_ref), channel_id=1, source_target_pairs={{0,2},{1,3},{2,0},{3,1},{4,5},{5,4},{6,7},{7,6},{8,10},{9,11},{10,... | collective-permute-start | bytes 393224 | tf_op jit(solution)/shard_map/ppermute | solution.py:567
  41.3 0.6 %turn.1.weight_ref = bf16[512,2048]{1,0:T(8,128)(2,1)S(1)} custom-call(bf16[2048,512]{1,0:T(8,128)(2,1)S(1)} %get-tuple-element.116.weight_ref), custom_call_target="tpu_custom_call" | custom-call | bytes 4194304 | tf_op jit(solution)/shard_map/turn/pallas_call | solution.py:492
  42.0 2.8 %text_grad.3 = (bf16[384,1024]{1,0:T(8,128)(2,1)}, bf16[384,1024]{1,0:T(8,128)(2,1)}, bf16[384,512]{1,0:T(8,128)(2,1)}) custom-call(bf16[384,1024]{1,0:T(8,128)(2,1)S(1)} %copy-done, bf16[384,1024]{1,0:T(8,128)(2,1)S(1)} %copy-done.1, bf16[384,512]{1,0:T(8,128)(2,1)S(1)} %copy-done.2, ...), custom_call_target="tpu_custom_call", output_to_operand_aliasing={{0}: (9, {}), {1}: (10, {}), {2}: (11, {})} | custom-call | flops 1207959552 | bytes 3145728 | tf_op jit(solution)/shard_map/text_grad/pallas_call | solution.py:417
  44.8 1.2 %collective-permute-done.11.second_ref = bf16[128,512]{1,0:T(8,128)(2,1)S(1)} collective-permute-done((bf16[128,512]{1,0:T(8,128)(2,1)S(1)}, bf16[128,512]{1,0:T(8,128)(2,1)S(1)}, u32[]{:S(2)}, u32[]{:S(2)}) %collective-permute-start.11) | collective-permute-done | bytes 131104 | tf_op jit(solution)/shard_map/ppermute | solution.py:567
  46.0 2.0 %collective-permute-start.13 = (bf16[128,512]{1,0:T(8,128)(2,1)S(1)}, bf16[128,512]{1,0:T(8,128)(2,1)S(1)}, u32[]{:S(2)}, u32[]{:S(2)}) collective-permute-start(bf16[128,512]{1,0:T(8,128)(2,1)S(1)} %crossed.1.part_ref), channel_id=1, source_target_pairs={{0,1},{1,0},{2,3},{3,2},{4,5},{5,4},{6,7},{7,6},{8,9},{9,8},{10,11... | collective-permute-start | bytes 393224 | tf_op jit(solution)/shard_map/ppermute | solution.py:567
  48.1 1.5 %near_grad.1.before_ref = f32[128,2048]{1,0:T(8,128)S(1)} custom-call(bf16[128,512]{1,0:T(8,128)(2,1)S(1)} %collect.1.own_ref, bf16[2048,512]{1,0:T(8,128)(2,1)S(1)} %get-tuple-element.126.own_weight, bf16[128,512]{1,0:T(8,128)(2,1)S(1)} %collective-permute-done.12.first_ref, bf16[128,512]{1,0:T(8,128)(2,1)S(1)} %collective-permute-done.11.second_ref, ...), custom_call_target="tpu_custom_call" | custom-call | flops 536870912 | bytes 4194304 | tf_op jit(solution)/shard_map/near_grad/pallas_call | solution.py:473
  49.5 0.8 %next_grad.1.before_ref = f32[128,2048]{1,0:T(8,128)S(1)} custom-call(f32[128,2048]{1,0:T(8,128)S(1)} %near_grad.1.before_ref, bf16[128,512]{1,0:T(8,128)(2,1)S(1)} %crossed.1.part_ref, bf16[2048,512]{1,0:T(8,128)(2,1)S(1)} %get-tuple-element.130.weight_ref), custom_call_target="tpu_custom_call" | custom-call | flops 536870912 | bytes 4194304 | tf_op jit(solution)/shard_map/next_grad/pallas_call | solution.py:473
  50.4 1.6 %collective-permute-done.13.part_ref = bf16[128,512]{1,0:T(8,128)(2,1)S(1)} collective-permute-done((bf16[128,512]{1,0:T(8,128)(2,1)S(1)}, bf16[128,512]{1,0:T(8,128)(2,1)S(1)}, u32[]{:S(2)}, u32[]{:S(2)}) %collective-permute-start.13) | collective-permute-done | bytes 131104 | tf_op jit(solution)/shard_map/ppermute | solution.py:567
  51.9 1.2 %last_grad.1 = bf16[128,2048]{1,0:T(8,128)(2,1)} custom-call(f32[128,2048]{1,0:T(8,128)S(1)} %next_grad.1.before_ref, bf16[128,512]{1,0:T(8,128)(2,1)S(1)} %collective-permute-done.13.part_ref, bf16[512,2048]{1,0:T(8,128)(2,1)S(1)} %turn.1.weight_ref), custom_call_target="tpu_custom_call" | custom-call | flops 268435456 | bytes 2097152 | tf_op jit(solution)/shard_map/last_grad/pallas_call | solution.py:525
  (36 shorter events, 1.4 us)
Async XLA Ops:
  2.6 6.7 %collective-permute-start = (bf16[128,512]{1,0:T(8,128)(2,1)S(1)}, bf16[128,512]{1,0:T(8,128)(2,1)S(1)}, u32[]{:S(2)}, u32[]{:S(2)}) collective-permute-start(bf16[128,512]{1,0:T(8,128)(2,1)S(1)} %get-tuple-element.73), channel_id=1, source_target_pairs={{0,1},{1,0},{2,3},{3,2},{4,5},{5,4},{6,7},{7,6},{8,9},{9,8},{10,11... | collective-permute-start | bytes 393224 | tf_op jit(solution)/shard_map/ppermute | solution.py:567
  5.7 8.0 %copy-start = (bf16[384,1024]{1,0:T(8,128)(2,1)S(1)}, bf16[384,1024]{1,0:T(8,128)(2,1)}, u32[]{:S(2)}) copy-start(bf16[384,1024]{1,0:T(8,128)(2,1)} %query_ref.11) | copy-start | bytes 2359300
  5.7 8.0 %copy-start.1 = (bf16[384,1024]{1,0:T(8,128)(2,1)S(1)}, bf16[384,1024]{1,0:T(8,128)(2,1)}, u32[]{:S(2)}) copy-start(bf16[384,1024]{1,0:T(8,128)(2,1)} %grad_ref.11) | copy-start | bytes 2359300
  5.7 8.0 %copy-start.2 = (bf16[384,512]{1,0:T(8,128)(2,1)S(1)}, bf16[384,512]{1,0:T(8,128)(2,1)}, u32[]{:S(2)}) copy-start(bf16[384,512]{1,0:T(8,128)(2,1)} %kv_ref.5) | copy-start | bytes 1179652
  5.7 8.0 %copy-start.3 = (s32[1,384]{1,0:T(1,128)S(1)}, s32[1,384]{1,0:T(1,128)}, u32[]{:S(2)}) copy-start(s32[1,384]{1,0:T(1,128)} %segment_ref.11) | copy-start | bytes 4612
  9.4 7.9 %collective-permute-start.1 = (bf16[128,512]{1,0:T(8,128)(2,1)S(1)}, bf16[128,512]{1,0:T(8,128)(2,1)S(1)}, u32[]{:S(2)}, u32[]{:S(2)}) collective-permute-start(bf16[128,512]{1,0:T(8,128)(2,1)S(1)} %get-tuple-element.133), channel_id=1, source_target_pairs={{0,1},{1,0},{2,3},{3,2},{4,6},{5,7},{6,4},{7,5},{8,9},{9,8},{10,11... | collective-permute-start | bytes 393224 | tf_op jit(solution)/shard_map/ppermute | solution.py:567
  11.1 6.3 %collective-permute-start.2 = (bf16[128,512]{1,0:T(8,128)(2,1)S(1)}, bf16[128,512]{1,0:T(8,128)(2,1)S(1)}, u32[]{:S(2)}, u32[]{:S(2)}) collective-permute-start(bf16[128,512]{1,0:T(8,128)(2,1)S(1)} %get-tuple-element.132), channel_id=1, source_target_pairs={{0,2},{1,3},{2,0},{3,1},{4,5},{5,4},{6,7},{7,6},{8,10},{9,11},{10,... | collective-permute-start | bytes 393224 | tf_op jit(solution)/shard_map/ppermute | solution.py:567
  14.8 2.5 %copy-start.4 = (s32[128,1]{0,1:T(1,128)S(1)}, s32[128,1]{0,1:T(1,128)}, u32[]{:S(2)}) copy-start(s32[128,1]{0,1:T(1,128)} %param.14) | copy-start | bytes 1540
  14.9 2.5 %copy-start.5 = (s32[128]{0:T(128)S(1)}, s32[128]{0:T(128)}, u32[]{:S(2)}) copy-start(s32[128]{0:T(128)} %param.15) | copy-start | bytes 1540
  17.6 6.3 %collective-permute-start.3 = (bf16[64,640]{1,0:T(8,128)(2,1)S(1)}, bf16[64,640]{1,0:T(8,128)(2,1)S(1)}, u32[]{:S(2)}, u32[]{:S(2)}) collective-permute-start(bf16[64,640]{1,0:T(8,128)(2,1)S(1)} %get-tuple-element.81), channel_id=1, source_target_pairs={{0,24},{4,28},{8,16},{12,20},{16,8},{20,12},{24,0},{28,4},{1,25},{... | collective-permute-start | bytes 245768 | tf_op jit(solution)/shard_map/ppermute | solution.py:603
  20.1 5.2 %collective-permute-start.4 = (bf16[64,640]{1,0:T(8,128)(2,1)S(1)}, bf16[64,640]{1,0:T(8,128)(2,1)S(1)}, u32[]{:S(2)}, u32[]{:S(2)}) collective-permute-start(bf16[64,640]{1,0:T(8,128)(2,1)S(1)} %get-tuple-element.82), channel_id=1, source_target_pairs={{0,16},{4,12},{8,24},{12,4},{16,0},{20,28},{24,8},{28,20},{1,17},{... | collective-permute-start | bytes 245768 | tf_op jit(solution)/shard_map/ppermute | solution.py:603
  20.6 4.7 %collective-permute-start.5 = (bf16[64,640]{1,0:T(8,128)(2,1)S(1)}, bf16[64,640]{1,0:T(8,128)(2,1)S(1)}, u32[]{:S(2)}, u32[]{:S(2)}) collective-permute-start(bf16[64,640]{1,0:T(8,128)(2,1)S(1)} %get-tuple-element.85), channel_id=1, source_target_pairs={{0,8},{4,20},{8,0},{12,28},{16,24},{20,4},{24,16},{28,12},{1,9},{5... | collective-permute-start | bytes 245768 | tf_op jit(solution)/shard_map/ppermute | solution.py:603
  25.4 1.5 %collective-permute-start.6 = (bf16[128,640]{1,0:T(8,128)(2,1)S(1)}, bf16[128,640]{1,0:T(8,128)(2,1)S(1)}, u32[]{:S(2)}, u32[]{:S(2)}) collective-permute-start(bf16[128,640]{1,0:T(8,128)(2,1)S(1)} %pad_maximum_fusion), channel_id=1, source_target_pairs={{0,4},{4,0},{8,12},{12,8},{16,20},{20,16},{24,28},{28,24},{1,5},{5... | collective-permute-start | bytes 491528 | tf_op jit(solution)/shard_map/ppermute | solution.py:607
  28.7 1.6 %collective-permute-start.7 = (bf16[128,512]{1,0:T(8,128)(2,1)S(1)}, bf16[128,512]{1,0:T(8,128)(2,1)S(1)}, u32[]{:S(2)}, u32[]{:S(2)}) collective-permute-start(bf16[128,512]{1,0:T(8,128)(2,1)S(1)} %get-tuple-element.96), channel_id=1, source_target_pairs={{0,4},{4,0},{8,12},{12,8},{16,20},{20,16},{24,28},{28,24},{1,5},{5... | collective-permute-start | bytes 393224 | tf_op jit(solution)/shard_map/ppermute | solution.py:614
  30.4 6.4 %collective-permute-start.8 = (bf16[64,512]{1,0:T(8,128)(2,1)S(1)}, bf16[64,512]{1,0:T(8,128)(2,1)S(1)}, u32[]{:S(2)}, u32[]{:S(2)}) collective-permute-start(bf16[64,512]{1,0:T(8,128)(2,1)S(1)} %pad_maximum_fusion.2), channel_id=1, source_target_pairs={{0,24},{4,28},{8,16},{12,20},{16,8},{20,12},{24,0},{28,4},{1,25},{... | collective-permute-start | bytes 196616 | tf_op jit(solution)/shard_map/ppermute | solution.py:644
  32.6 4.7 %collective-permute-start.9 = (bf16[64,512]{1,0:T(8,128)(2,1)S(1)}, bf16[64,512]{1,0:T(8,128)(2,1)S(1)}, u32[]{:S(2)}, u32[]{:S(2)}) collective-permute-start(bf16[64,512]{1,0:T(8,128)(2,1)S(1)} %pad_maximum_fusion.3), channel_id=1, source_target_pairs={{0,8},{4,20},{8,0},{12,28},{16,24},{20,4},{24,16},{28,12},{1,9},{5... | collective-permute-start | bytes 196616 | tf_op jit(solution)/shard_map/ppermute | solution.py:644
  33.4 4.3 %collective-permute-start.10 = (bf16[64,512]{1,0:T(8,128)(2,1)S(1)}, bf16[64,512]{1,0:T(8,128)(2,1)S(1)}, u32[]{:S(2)}, u32[]{:S(2)}) collective-permute-start(bf16[64,512]{1,0:T(8,128)(2,1)S(1)} %pad_maximum_fusion.4), channel_id=1, source_target_pairs={{0,16},{4,12},{8,24},{12,4},{16,0},{20,28},{24,8},{28,20},{1,17},{... | collective-permute-start | bytes 196616 | tf_op jit(solution)/shard_map/ppermute | solution.py:644
  37.9 8.1 %collective-permute-start.11 = (bf16[128,512]{1,0:T(8,128)(2,1)S(1)}, bf16[128,512]{1,0:T(8,128)(2,1)S(1)}, u32[]{:S(2)}, u32[]{:S(2)}) collective-permute-start(bf16[128,512]{1,0:T(8,128)(2,1)S(1)} %collect.1.own_ref), channel_id=1, source_target_pairs={{0,1},{1,0},{2,3},{3,2},{4,6},{5,7},{6,4},{7,5},{8,9},{9,8},{10,11... | collective-permute-start | bytes 393224 | tf_op jit(solution)/shard_map/ppermute | solution.py:567
  39.6 6.4 %collective-permute-start.12 = (bf16[128,512]{1,0:T(8,128)(2,1)S(1)}, bf16[128,512]{1,0:T(8,128)(2,1)S(1)}, u32[]{:S(2)}, u32[]{:S(2)}) collective-permute-start(bf16[128,512]{1,0:T(8,128)(2,1)S(1)} %collect.1.own_ref), channel_id=1, source_target_pairs={{0,2},{1,3},{2,0},{3,1},{4,5},{5,4},{6,7},{7,6},{8,10},{9,11},{10,... | collective-permute-start | bytes 393224 | tf_op jit(solution)/shard_map/ppermute | solution.py:567
  46.0 5.9 %collective-permute-start.13 = (bf16[128,512]{1,0:T(8,128)(2,1)S(1)}, bf16[128,512]{1,0:T(8,128)(2,1)S(1)}, u32[]{:S(2)}, u32[]{:S(2)}) collective-permute-start(bf16[128,512]{1,0:T(8,128)(2,1)S(1)} %crossed.1.part_ref), channel_id=1, source_target_pairs={{0,1},{1,0},{2,3},{3,2},{4,5},{5,4},{6,7},{7,6},{8,9},{9,8},{10,11... | collective-permute-start | bytes 393224 | tf_op jit(solution)/shard_map/ppermute | solution.py:567
